TPU v7x, 32 devices: a whole 2x2x4 slice. The times are simulated.
32 devices in a mesh: seq: 4 (over z), dp: 8 (over y, x, core).
Axes of the slice: x: 2, y: 2, z: 4, core: 2. Of those that a mesh axis runs over, the one named last changes fastest.
Arguments:
- hidden_in: bfloat16 [8, 512, 2048], P('dp', 'seq'), may hold values from -6 to 6
- routes: int32 [8, 512, 8], P('dp', 'seq'), may hold values from 0 to 31, all different within a row; in each aligned block of 128 rows (0 to 127, 128 to 255, ..., all dimensions but the last counted through in order) at most 36 rows name the same one
- norm1_gain: bfloat16 [2048], P(('seq', 'dp')), may hold values from 0.5 to 1.5
- query_gain: bfloat16 [128], P(('seq', 'dp')), may hold values from 0.5 to 1.5
- key_gain: bfloat16 [128], P(('seq', 'dp')), may hold values from 0.5 to 1.5
- qkv_weight: bfloat16 [2048, 5120], P(('seq', 'dp')), may hold values from -0.125 to 0.125
- out_weight: bfloat16 [4096, 2048], P(('seq', 'dp')), may hold values from -1.5 to 1.5
- norm2_gain: bfloat16 [2048], P(('seq', 'dp')), may hold values from 0.5 to 1.5
- router: bfloat16 [2048, 32], P(('seq', 'dp')), may hold values from -0.06982422 to 0.06982422
- gate_up_weight: bfloat16 [32, 2048, 1536], P(('seq', 'dp')), may hold values from -0.125 to 0.125
- down_weight: bfloat16 [32, 768, 2048], P(('seq', 'dp')), may hold values from -0.875 to 0.875
- cotangent: bfloat16 [8, 512, 2048], P('dp', 'seq'), may hold values from -6 to 6
Outputs:
- output: bfloat16 [8, 512, 2048], P('dp', 'seq')
- grad_input: float32 [8, 512, 2048], P('dp', 'seq')
- grad_norm1: float32 [2048], P(('seq', 'dp'))
- grad_query_gain: float32 [128], P(('seq', 'dp'))
- grad_key_gain: float32 [128], P(('seq', 'dp'))
- grad_qkv: float32 [2048, 5120], P(('seq', 'dp'))
- grad_out: float32 [4096, 2048], P(('seq', 'dp'))
- grad_norm2: float32 [2048], P(('seq', 'dp'))
- grad_router: float32 [2048, 32], P(('seq', 'dp'))
- grad_gate_up: float32 [32, 2048, 1536], P(('seq', 'dp'))
- grad_down: float32 [32, 768, 2048], P(('seq', 'dp'))
Inputs may be any that keep to these rules, and one draw needn't show every extreme that they name: Each token names 8 different experts; in the rows of one device no expert is named by more than 36 routes, and in some device's rows one is named by exactly 36; every expert is named somewhere.
All inputs are finite; a program needn't handle non-finite values.
Results may differ from a plain program's by a relative error of at most 0.025.
Values may be sent and summed in bfloat16 or wider, within the bound.
A program may use at most 320 MiB of HBM per device.

v0:
```python
import jax
import jax.numpy as jnp
from jax import lax
from jax.sharding import PartitionSpec as P

MODEL_WIDTH = 2048
QUERY_HEADS = 32
KEY_VALUE_HEADS = 4
HEAD_SIZE = 128
FF = 768
TOP = 8


EPSILON = 1e-06
ROPE_BASE = 1000000.0
FILLER = -1e30
QUERY_BLOCK = 512


def rms_norm(values, gain):
    return values * lax.rsqrt(jnp.mean(values * values, axis=-1, keepdims=True) + EPSILON) * gain


def rope_tables(positions, width):
    half_width = width // 2
    freqs = ROPE_BASE ** (-(jnp.arange(half_width, dtype=jnp.float32) * (2.0 / width)))
    angles = positions[:, None] * freqs[None, :]
    return (jnp.cos(angles), jnp.sin(angles))


def rotate(values, cosine, sine_table):
    half_width = values.shape[-1] // 2
    first = values[..., :half_width]
    second = values[..., half_width:]
    cosine = cosine[:, None, :]
    sine_table = sine_table[:, None, :]
    return jnp.concatenate(
        [first * cosine - second * sine_table, second * cosine + first * sine_table], axis=-1
    )


def prepare_heads(projected_rows, gain_query, gain_key, cosine, sine_table):
    row_count = projected_rows.shape[0]
    query_columns = projected_rows.shape[1] - 2 * HEAD_SIZE
    queries = projected_rows[:, :query_columns].reshape(
        row_count, query_columns // HEAD_SIZE, HEAD_SIZE
    )
    key_head = projected_rows[:, query_columns : query_columns + HEAD_SIZE].reshape(
        row_count, 1, HEAD_SIZE
    )
    value_head = projected_rows[:, query_columns + HEAD_SIZE :]
    queries = rotate(rms_norm(queries, gain_query), cosine, sine_table)
    key_head = rotate(rms_norm(key_head, gain_key), cosine, sine_table).reshape(
        row_count, HEAD_SIZE
    )
    return (queries, key_head, value_head)


def inner_rows(left, right):
    return lax.dot_general(
        left, right, (((0,), (0,)), ((), ())), preferred_element_type=jnp.float32
    )


def outer_cols(left, right):
    return lax.dot_general(
        left, right, (((1,), (1,)), ((), ())), preferred_element_type=jnp.float32
    )


def block_slice(array, index, block_rows):
    return lax.dynamic_slice_in_dim(array, index * block_rows, block_rows, 0)


def block_scores(query_block, key_block, i, j, block_rows):
    scores = jnp.einsum(
        "qhd,kd->hqk", query_block, key_block, preferred_element_type=jnp.float32
    ) * HEAD_SIZE ** (-0.5)
    row_ids = i * block_rows + jnp.arange(block_rows)
    col_ids = j * block_rows + jnp.arange(block_rows)
    return jnp.where((row_ids[:, None] >= col_ids[None, :])[None], scores, FILLER)


def attend_forward(queries, keys_in, values_in):
    sequence_length, head_count = (queries.shape[0], queries.shape[1])
    block_rows = min(QUERY_BLOCK, sequence_length)
    block_count = sequence_length // block_rows

    def one_block(i):
        query_block = block_slice(queries, i, block_rows)

        def max_step(j, carry):
            row_top, row_total = carry
            scores = block_scores(
                query_block, block_slice(keys_in, j, block_rows), i, j, block_rows
            )
            new_top = jnp.maximum(row_top, jnp.max(scores, axis=-1))
            row_total = row_total * jnp.exp(row_top - new_top) + jnp.sum(
                jnp.exp(scores - new_top[..., None]), axis=-1
            )
            return (new_top, row_total)

        start = (
            jnp.full((head_count, block_rows), FILLER, jnp.float32),
            jnp.zeros((head_count, block_rows), jnp.float32),
        )
        row_top, row_total = lax.fori_loop(0, i + 1, max_step, start)
        log_totals = row_top + jnp.log(row_total)

        def out_step(j, accum_out):
            scores = block_scores(
                query_block, block_slice(keys_in, j, block_rows), i, j, block_rows
            )
            probabilities = jnp.exp(scores - log_totals[..., None]).astype(jnp.bfloat16)
            return accum_out + jnp.einsum(
                "hqk,kd->qhd",
                probabilities,
                block_slice(values_in, j, block_rows),
                preferred_element_type=jnp.float32,
            )

        accum_out = lax.fori_loop(
            0, i + 1, out_step, jnp.zeros((block_rows, head_count, HEAD_SIZE), jnp.float32)
        )
        return (accum_out, log_totals)

    outputs, log_totals = lax.map(one_block, jnp.arange(block_count))
    return (outputs.reshape(sequence_length, head_count, HEAD_SIZE), log_totals)


def attend_backward(queries, keys_in, values_in, out_full, log_totals, grad_heads):
    sequence_length, head_count = (queries.shape[0], queries.shape[1])
    block_rows = min(QUERY_BLOCK, sequence_length)
    block_count = sequence_length // block_rows
    row_dots = jnp.sum(grad_heads.astype(jnp.float32) * out_full, axis=-1)

    def one_block(carry, i):
        query_block = block_slice(queries, i, block_rows)
        grad_block = block_slice(grad_heads, i, block_rows)
        dot_block = block_slice(row_dots, i, block_rows).T
        block_totals = log_totals[i]

        def step(j, inner):
            grad_query, grad_keys, grad_values = inner
            key_block = block_slice(keys_in, j, block_rows)
            value_block = block_slice(values_in, j, block_rows)
            scores = block_scores(query_block, key_block, i, j, block_rows)
            probabilities = jnp.exp(scores - block_totals[..., None])
            grad_probs = jnp.einsum(
                "qhd,kd->hqk", grad_block, value_block, preferred_element_type=jnp.float32
            )
            grad_scores = (probabilities * (grad_probs - dot_block[..., None])).astype(jnp.bfloat16)
            grad_query = grad_query + jnp.einsum(
                "hqk,kd->qhd", grad_scores, key_block, preferred_element_type=jnp.float32
            ) * HEAD_SIZE ** (-0.5)
            key_part = jnp.einsum(
                "hqk,qhd->kd", grad_scores, query_block, preferred_element_type=jnp.float32
            ) * HEAD_SIZE ** (-0.5)
            value_part = jnp.einsum(
                "hqk,qhd->kd",
                probabilities.astype(jnp.bfloat16),
                grad_block,
                preferred_element_type=jnp.float32,
            )
            grad_keys = lax.dynamic_update_slice_in_dim(
                grad_keys, block_slice(grad_keys, j, block_rows) + key_part, j * block_rows, 0
            )
            grad_values = lax.dynamic_update_slice_in_dim(
                grad_values, block_slice(grad_values, j, block_rows) + value_part, j * block_rows, 0
            )
            return (grad_query, grad_keys, grad_values)

        start = (jnp.zeros((block_rows, head_count, HEAD_SIZE), jnp.float32), carry[0], carry[1])
        grad_query, grad_keys, grad_values = lax.fori_loop(0, i + 1, step, start)
        return ((grad_keys, grad_values), grad_query)

    empty = jnp.zeros((sequence_length, HEAD_SIZE), jnp.float32)
    (grad_keys, grad_values), grad_query = lax.scan(
        one_block, (empty, empty), jnp.arange(block_count)
    )
    return (grad_query.reshape(sequence_length, head_count, HEAD_SIZE), grad_keys, grad_values)


def body(
    hidden_in,
    routes,
    norm1_gain,
    query_gain,
    key_gain,
    qkv_weight,
    out_weight,
    norm2_gain,
    router,
    gate_up_weight,
    down_weight,
    cotangent,
):
    tokens = hidden_in.shape[1]
    sequence_number = lax.axis_size("seq")
    devices = lax.axis_size(("seq", "dp"))
    per_device = QUERY_HEADS // sequence_number
    query_columns = per_device * HEAD_SIZE
    head_replicas = sequence_number // KEY_VALUE_HEADS
    capacity = (tokens * TOP * 9 + 8 * devices - 1) // (8 * devices)
    gain_one, gain_query, gain_key, gain_two, full_router = (
        lax.all_gather(norm1_gain, ("seq", "dp"), axis=0, tiled=True),
        lax.all_gather(query_gain, ("seq", "dp"), axis=0, tiled=True),
        lax.all_gather(key_gain, ("seq", "dp"), axis=0, tiled=True),
        lax.all_gather(norm2_gain, ("seq", "dp"), axis=0, tiled=True),
        lax.all_gather(router, ("seq", "dp"), axis=0, tiled=True),
    )
    gain_one = gain_one.astype(jnp.float32)
    gain_two = gain_two.astype(jnp.float32)
    gain_query = gain_query.astype(jnp.float32)
    gain_key = gain_key.astype(jnp.float32)
    query_key_value_rows, out_rows = (
        lax.all_gather(qkv_weight, "dp", axis=0, tiled=True),
        lax.all_gather(out_weight, "dp", axis=0, tiled=True),
    )
    block_of_rows = query_key_value_rows.shape[0]
    query_part = query_key_value_rows[:, : QUERY_HEADS * HEAD_SIZE].reshape(
        block_of_rows, sequence_number, query_columns
    )
    paired_portion = jnp.repeat(
        query_key_value_rows[:, QUERY_HEADS * HEAD_SIZE :].reshape(
            block_of_rows, 2, KEY_VALUE_HEADS, HEAD_SIZE
        ),
        head_replicas,
        axis=2,
    )
    paired_portion = jnp.transpose(paired_portion, (0, 2, 1, 3)).reshape(
        block_of_rows, sequence_number, 2 * HEAD_SIZE
    )
    column_send = jnp.concatenate([query_part, paired_portion], axis=-1)
    own_cols = lax.all_to_all(column_send, "seq", split_axis=1, concat_axis=0, tiled=True).reshape(
        block_of_rows * sequence_number, query_columns + 2 * HEAD_SIZE
    )
    residual = hidden_in[0].astype(jnp.float32)
    normed_low = rms_norm(residual, gain_one).astype(jnp.bfloat16)
    normed_full = lax.all_gather(normed_low, "seq", axis=0, tiled=True)
    sequence_length = normed_full.shape[0]
    cosine, sine_table = rope_tables(jnp.arange(sequence_length).astype(jnp.float32), HEAD_SIZE)
    projected_rows = jnp.dot(normed_full, own_cols, preferred_element_type=jnp.float32)
    queries, key_head, value_head = prepare_heads(
        projected_rows, gain_query, gain_key, cosine, sine_table
    )
    query_heads = queries.astype(jnp.bfloat16)
    key_heads = key_head.astype(jnp.bfloat16)
    value_heads = value_head.astype(jnp.bfloat16)
    out_full, log_totals = attend_forward(query_heads, key_heads, value_heads)
    heads_low = out_full.astype(jnp.bfloat16).reshape(sequence_length, query_columns)
    branch_part = jnp.dot(heads_low, out_rows, preferred_element_type=jnp.float32)
    hidden1 = residual + lax.psum_scatter(
        branch_part.astype(jnp.bfloat16), "seq", scatter_dimension=0, tiled=True
    ).astype(jnp.float32)
    mixed_low = rms_norm(hidden1, gain_two).astype(jnp.bfloat16)
    logits = jnp.dot(mixed_low, full_router, preferred_element_type=jnp.float32)
    local_routes = routes[0]
    chosen = jnp.take_along_axis(logits, local_routes, axis=1)
    gate_weights = jax.nn.softmax(chosen, axis=-1)
    flat_routes = local_routes.reshape(-1)
    onehot = (flat_routes[:, None] == jnp.arange(devices, dtype=jnp.int32)[None, :]).astype(
        jnp.int32
    )
    slot_index = jnp.sum(jnp.cumsum(onehot, axis=0) * onehot, axis=-1) - 1
    target = flat_routes * capacity + slot_index
    owner_row = jnp.arange(tokens * TOP, dtype=jnp.int32) // TOP
    route_ids = jnp.arange(tokens * TOP, dtype=jnp.int32)
    source = jnp.zeros((devices * capacity,), jnp.int32).at[target].set(owner_row)
    route_of = jnp.zeros((devices * capacity,), jnp.int32).at[target].set(route_ids)
    filled = jnp.zeros((devices * capacity,), jnp.bool_).at[target].set(True)
    outgoing = jnp.where(filled[:, None], mixed_low[source], jnp.zeros((), jnp.bfloat16)).reshape(
        devices, capacity, MODEL_WIDTH
    )
    arrived = lax.all_to_all(
        outgoing, ("seq", "dp"), split_axis=0, concat_axis=0, tiled=True
    ).reshape(-1, MODEL_WIDTH)
    weight_in = gate_up_weight[0]
    weight_back = down_weight[0]
    gate_up = jnp.dot(arrived, weight_in, preferred_element_type=jnp.float32)
    hidden = (jax.nn.silu(gate_up[:, :FF]) * gate_up[:, FF:]).astype(jnp.bfloat16)
    expert_out = jnp.dot(hidden, weight_back, preferred_element_type=jnp.float32).astype(
        jnp.bfloat16
    )
    returned = lax.all_to_all(
        expert_out.reshape(devices, capacity, MODEL_WIDTH),
        ("seq", "dp"),
        split_axis=0,
        concat_axis=0,
        tiled=True,
    ).reshape(-1, MODEL_WIDTH)
    picked = returned[target].reshape(tokens, TOP, MODEL_WIDTH)
    combined = jnp.einsum("tk,tkd->td", gate_weights, picked.astype(jnp.float32))
    output = (hidden1 + combined).astype(jnp.bfloat16)
    grad_result = cotangent[0].astype(jnp.float32)
    flat_gates = gate_weights.reshape(-1)
    grad_returned = jnp.where(
        filled[:, None], flat_gates[route_of][:, None] * grad_result[source], 0.0
    ).astype(jnp.bfloat16)
    grad_gates = jnp.einsum("tkd,td->tk", picked.astype(jnp.float32), grad_result)
    grad_chosen = gate_weights * (
        grad_gates - jnp.sum(gate_weights * grad_gates, axis=-1, keepdims=True)
    )
    route_table = (
        local_routes[:, :, None] == jnp.arange(devices, dtype=jnp.int32)[None, None, :]
    ).astype(jnp.float32)
    grad_logits = jnp.sum(route_table * grad_chosen[:, :, None], axis=1).astype(jnp.bfloat16)
    back_rows = lax.all_to_all(
        grad_returned.reshape(devices, capacity, MODEL_WIDTH),
        ("seq", "dp"),
        split_axis=0,
        concat_axis=0,
        tiled=True,
    ).reshape(-1, MODEL_WIDTH)
    grad_weight_back = inner_rows(hidden, back_rows)
    grad_hidden = outer_cols(back_rows, weight_back)
    _, pull_act = jax.vjp(
        lambda gate_in, up_in: jax.nn.silu(gate_in) * up_in, gate_up[:, :FF], gate_up[:, FF:]
    )
    grad_gate_in, grad_up_in = pull_act(grad_hidden)
    grad_gate_up = jnp.concatenate([grad_gate_in, grad_up_in], axis=1).astype(jnp.bfloat16)
    grad_weight_in = inner_rows(arrived, grad_gate_up)
    grad_arrived = (
        outer_cols(grad_gate_up, weight_in)
        .astype(jnp.bfloat16)
        .reshape(devices, capacity, MODEL_WIDTH)
    )
    grad_sent = lax.all_to_all(
        grad_arrived, ("seq", "dp"), split_axis=0, concat_axis=0, tiled=True
    ).reshape(-1, MODEL_WIDTH)
    grad_mixed = jnp.sum(
        grad_sent[target].reshape(tokens, TOP, MODEL_WIDTH).astype(jnp.float32), axis=1
    ) + outer_cols(grad_logits, full_router)
    grad_router_w = inner_rows(mixed_low, grad_logits)
    _, pull_two = jax.vjp(rms_norm, hidden1, gain_two)
    grad_hidden_norm, grad_gain_two = pull_two(grad_mixed)
    grad_hidden1 = grad_result + grad_hidden_norm
    grad_branch = grad_hidden1.astype(jnp.bfloat16)
    branch_full = lax.all_gather(grad_branch, "seq", axis=0, tiled=True)
    grad_out_rows = inner_rows(heads_low, branch_full)
    grad_heads = (
        outer_cols(branch_full, out_rows)
        .astype(jnp.bfloat16)
        .reshape(sequence_length, per_device, HEAD_SIZE)
    )
    grad_query, grad_keys, grad_values = attend_backward(
        query_heads, key_heads, value_heads, out_full, log_totals, grad_heads
    )
    _, pull_prep = jax.vjp(
        lambda proj_in, query_in, key_in: prepare_heads(
            proj_in, query_in, key_in, cosine, sine_table
        ),
        projected_rows,
        gain_query,
        gain_key,
    )
    grad_projected, grad_gain_query, grad_gain_key = pull_prep((grad_query, grad_keys, grad_values))
    grad_proj_low = grad_projected.astype(jnp.bfloat16)
    gradient_columns = inner_rows(normed_full, grad_proj_low)
    grad_normed = lax.psum_scatter(
        outer_cols(grad_proj_low, own_cols).astype(jnp.bfloat16),
        "seq",
        scatter_dimension=0,
        tiled=True,
    ).astype(jnp.float32)
    _, pull_one = jax.vjp(rms_norm, residual, gain_one)
    grad_residual_norm, grad_gain_one = pull_one(grad_normed)
    grad_input = grad_hidden1 + grad_residual_norm
    group = lax.axis_index("seq")
    paired_heads = group // head_replicas
    query_key_value_width = jnp.zeros(
        (MODEL_WIDTH, (QUERY_HEADS + 2 * KEY_VALUE_HEADS) * HEAD_SIZE), jnp.float32
    )
    query_key_value_width = lax.dynamic_update_slice(
        query_key_value_width, gradient_columns[:, :query_columns], (0, group * query_columns)
    )
    query_key_value_width = lax.dynamic_update_slice(
        query_key_value_width,
        gradient_columns[:, query_columns : query_columns + HEAD_SIZE],
        (0, QUERY_HEADS * HEAD_SIZE + paired_heads * HEAD_SIZE),
    )
    query_key_value_width = lax.dynamic_update_slice(
        query_key_value_width,
        gradient_columns[:, query_columns + HEAD_SIZE :],
        (0, (QUERY_HEADS + KEY_VALUE_HEADS) * HEAD_SIZE + paired_heads * HEAD_SIZE),
    )
    out_total = lax.dynamic_update_slice(
        jnp.zeros((QUERY_HEADS * HEAD_SIZE, MODEL_WIDTH), jnp.float32),
        grad_out_rows,
        (group * query_columns, 0),
    )
    (
        shard_gain_one,
        shard_gain_query,
        shard_gain_key,
        shard_qkv,
        shard_out,
        shard_gain_two,
        shard_router,
    ) = (
        lax.psum_scatter(grad_gain_one, ("seq", "dp"), scatter_dimension=0, tiled=True),
        lax.psum_scatter(grad_gain_query, ("seq", "dp"), scatter_dimension=0, tiled=True),
        lax.psum_scatter(grad_gain_key, ("seq", "dp"), scatter_dimension=0, tiled=True),
        lax.psum_scatter(query_key_value_width, ("seq", "dp"), scatter_dimension=0, tiled=True),
        lax.psum_scatter(out_total, ("seq", "dp"), scatter_dimension=0, tiled=True),
        lax.psum_scatter(grad_gain_two, ("seq", "dp"), scatter_dimension=0, tiled=True),
        lax.psum_scatter(grad_router_w, ("seq", "dp"), scatter_dimension=0, tiled=True),
    )
    return (
        output[None],
        grad_input[None],
        shard_gain_one,
        shard_gain_query,
        shard_gain_key,
        shard_qkv,
        shard_out,
        shard_gain_two,
        shard_router,
        grad_weight_in[None],
        grad_weight_back[None],
    )


def solution(mesh):
    in_specs = (
        P("dp", "seq", None),
        P("dp", "seq", None),
        P(("seq", "dp")),
        P(("seq", "dp")),
        P(("seq", "dp")),
        P(("seq", "dp"), None),
        P(("seq", "dp"), None),
        P(("seq", "dp")),
        P(("seq", "dp"), None),
        P(("seq", "dp"), None, None),
        P(("seq", "dp"), None, None),
        P("dp", "seq", None),
    )
    out_specs = (
        P("dp", "seq", None),
        P("dp", "seq", None),
        P(("seq", "dp")),
        P(("seq", "dp")),
        P(("seq", "dp")),
        P(("seq", "dp"), None),
        P(("seq", "dp"), None),
        P(("seq", "dp")),
        P(("seq", "dp"), None),
        P(("seq", "dp"), None, None),
        P(("seq", "dp"), None, None),
    )
    return jax.shard_map(body, mesh=mesh, in_specs=in_specs, out_specs=out_specs, check_vma=False)
```

profile of v0, /device:TPU:0, one launch (start us, length us, event | category | flops | bytes accessed | tf_op | source)
XLA Modules:
  0.0 2007.2 jit_solution(3772900924309482301)
XLA Ops:
  8.8 45.8 %all-gather.8.cloned.1.call-done = bf16[512,5120]{1,0:T(8,128)(2,1)} async-done(((bf16[64,5120]{1,0:T(8,128)(2,1)}), bf16[512,5120]{1,0:T(8,128)(2,1)}) %all-gather.8.cloned.1.call-update) | async-done | bytes 5242896 | tf_op jit(solution)/shard_map/all_gather | solution.py:217
  61.8 4.7 slice.81
  66.5 6.4 copy.244
  72.9 5.2 pad_maximum_fusion
  78.1 5.2 all-to-all-start
  84.4 134.6 %all-reduce.16 = (bf16[2048]{0:T(1024)(128)(2,1)S(1)}, bf16[128]{0:T(256)(128)(2,1)S(1)}, bf16[128]{0:T(256)(128)(2,1)S(1)}, bf16[2048]{0:T(1024)(128)(2,1)S(1)}) all-reduce(bf16[2048]{0:T(1024)(128)(2,1)S(1)} %dynamic-update-slice, bf16[128]{0:T(256)(128)(2,1)S(1)} %dynamic-update-slice.2, ...), channel_id=1, replica_groups=mesh['seq'=4,'dp'=8] {'seq','dp'}, use_global_device_ids=true, to_apply=%add.7 | all-reduce | flops 4352 | bytes 17408
  226.1 7.9 copy.194
  234.0 35.9 %all-gather.6.cloned.1.call-done = bf16[512,2048]{1,0:T(8,128)(2,1)} async-done(((bf16[128,2048]{1,0:T(8,128)(2,1)}), bf16[512,2048]{1,0:T(8,128)(2,1)}) %all-gather.6.cloned.1.call-update) | async-done | bytes 2097168 | tf_op jit(solution)/shard_map/all_gather | solution.py:240
  269.9 6.0 fusion.93
  293.5 4.8 bitcast_convert_fusion
  298.3 8.7 all-gather.10.cloned.1.call-done
  307.0 6.2 convolution_convert_fusion.2
  313.8 9.0 reduce-window.6
  323.3 4.3 scatter_custom_fusion.1
  327.7 4.6 scatter_custom_fusion
  332.4 24.6 %reduce-scatter.8.cloned.1.call-done = bf16[128,2048]{1,0:T(8,128)(2,1)} async-done(((bf16[512,2048]{1,0:T(8,128)(2,1)}), bf16[128,2048]{1,0:T(8,128)(2,1)}) %reduce-scatter.8.cloned.1.call-update) | async-done | bytes 524304 | tf_op jit(solution)/shard_map/reduce_scatter | solution.py:253
  360.6 11.8 gather_fusion
  372.4 7.2 gather.27
  379.6 5.2 broadcast_select_fusion
  384.8 4.2 all-to-all-start.1
  391.1 11.7 gather_fusion.3
  402.8 9.8 gather.32
  412.6 99.0 %all-gather = bf16[32,64,32]{1,2,0:T(8,128)(2,1)S(1)} all-gather(bf16[1,64,32]{1,2,0:T(8,128)(2,1)S(1)} %bitcast.252), channel_id=1, replica_groups=mesh['seq'=4,'dp'=8] {'seq','dp'}, dimensions={0}, use_global_device_ids=true | all-gather | bytes 135168 | tf_op jit(solution)/shard_map/all_gather | solution.py:210
  513.8 4.3 scatter_custom_fusion.2
  519.5 7.4 gather_fusion.5
  527.7 4.6 gather_fusion.2
  532.4 7.2 select_convert_fusion
  539.6 22.3 %all-to-all-start.3 = ((bf16[32,36,2048]{2,1,0:T(8,128)(2,1)}), bf16[32,36,2048]{2,1,0:T(8,128)(2,1)}, u32[]{:S(2)}, u32[]{:S(2)}) async-start(bf16[32,36,2048]{2,1,0:T(8,128)(2,1)} %select_convert_fusion), calls=%async_computation.4 | async-start | bytes 10485760 | tf_op jit(solution)/shard_map/all_to_all | solution.py:308
  561.9 7.3 reshape.530
  569.2 12.8 fusion.4
  582.0 97.0 %all-to-all-done.3 = bf16[32,36,2048]{2,1,0:T(8,128)(2,1)} async-done(((bf16[32,36,2048]{2,1,0:T(8,128)(2,1)}), bf16[32,36,2048]{2,1,0:T(8,128)(2,1)}, u32[]{:S(2)}, u32[]{:S(2)}) %all-to-all-start.3) | async-done | bytes 4718624 | tf_op jit(solution)/shard_map/all_to_all | solution.py:308
  679.0 7.2 reshape.534
  686.2 9.5 fusion.13
  697.5 11.8 convolution_convert_fusion.1
  709.4 7.2 reshape.535
  716.6 3.6 all-to-all-start.4
  720.2 7.0 convolution_convert_fusion
  727.2 7.2 reshape.531
  734.4 102.6 %all-to-all-done.4 = bf16[32,36,2048]{2,1,0:T(8,128)(2,1)} async-done(((bf16[32,36,2048]{2,1,0:T(8,128)(2,1)}), bf16[32,36,2048]{2,1,0:T(8,128)(2,1)}, u32[]{:S(2)}, u32[]{:S(2)}) %all-to-all-start.4) | async-done | bytes 4718624 | tf_op jit(solution)/shard_map/all_to_all | solution.py:328
  840.6 7.4 reshape.536
  848.0 11.7 gather_fusion.4
  859.7 6.0 convert_reduce_fusion
  865.7 91.5 %all-to-all-done.2 = bf16[32,36,2048]{2,1,0:T(8,128)(2,1)} async-done(((bf16[32,36,2048]{2,1,0:T(8,128)(2,1)}), bf16[32,36,2048]{2,1,0:T(8,128)(2,1)}, u32[]{:S(2)}, u32[]{:S(2)}) %all-to-all-start.2) | async-done | bytes 4718624 | tf_op jit(solution)/shard_map/all_to_all | solution.py:285
  957.3 7.2 reshape.532
  964.5 11.8 gather_fusion.1
  976.3 5.0 fusion.7
  986.4 43.3 %all-gather.12.cloned.1.call-done = bf16[512,2048]{1,0:T(8,128)(2,1)} async-done(((bf16[128,2048]{1,0:T(8,128)(2,1)}), bf16[512,2048]{1,0:T(8,128)(2,1)}) %all-gather.12.cloned.1.call-update) | async-done | bytes 2097168 | tf_op jit(solution)/shard_map/all_gather | solution.py:339
  1029.8 6.2 convolution_convert_fusion.4
  1040.2 5.0 fusion.1
  1048.1 5.3 convolution_bitcast_fusion.3
  1062.8 4.2 convolution_convert_fusion.3
  1067.1 11.5 broadcast_in_dim.208
  1078.6 5.6 convolution_dynamic-update-slice_fusion
  1085.8 4.6 fusion.90
  1090.4 13.9 broadcast_in_dim.207
  1104.2 4.4 slice_dynamic-update-slice_fusion
  1112.3 8.7 convolution_bitcast_fusion.1
  1121.0 13.2 convolution_bitcast_fusion
  1136.4 11.3 reduce-scatter.16.cloned.1.call-done
  1149.2 40.7 %reduce-scatter.10.cloned.1.call-done = bf16[128,2048]{1,0:T(8,128)(2,1)} async-done(((bf16[512,2048]{1,0:T(8,128)(2,1)}), bf16[128,2048]{1,0:T(8,128)(2,1)}) %reduce-scatter.10.cloned.1.call-update) | async-done | bytes 524304 | tf_op jit(solution)/shard_map/reduce_scatter | solution.py:360
  1191.6 55.6 %all-reduce.15 = (f32[2048]{0:T(1024)S(1)}, f32[128]{0:T(128)S(1)}, f32[128]{0:T(128)S(1)}, f32[2048]{0:T(1024)S(1)}) all-reduce(f32[2048]{0:T(1024)S(1)} %get-tuple-element.407, f32[128]{0:T(128)S(1)} %get-tuple-element.401, f32[128]{0:T(128)S(1)} %get-tuple-element.403, ...), channel_id=4, replica_groups=mesh['seq'=4,'dp'=8] {'seq','dp'}, use_global_device_ids=true, to_apply=%region_25.26.clone | all-reduce | flops 4352 | bytes 34816
  1249.6 4.3 fusion.30
  1253.9 293.3 %reduce-scatter.14.cloned.1.call-done = f32[128,2048]{1,0:T(8,128)} async-done(((f32[4096,2048]{1,0:T(8,128)}), f32[128,2048]{1,0:T(8,128)}) %reduce-scatter.14.cloned.1.call-update) | async-done | bytes 1048592 | tf_op jit(solution)/shard_map/reduce_scatter | solution.py:405
  1547.2 452.4 %reduce-scatter.12.cloned.1.call-done = f32[64,5120]{1,0:T(8,128)} async-done(((f32[2048,5120]{1,0:T(8,128)}), f32[64,5120]{1,0:T(8,128)}) %reduce-scatter.12.cloned.1.call-update) | async-done | bytes 1310736 | tf_op jit(solution)/shard_map/reduce_scatter | solution.py:404
  (285 shorter events, 84.4 us)
Async XLA Ops:
  8.0 678.2 %copy-start = (bf16[1,768,2048]{2,1,0:T(8,128)(2,1)S(1)}, bf16[1,768,2048]{2,1,0:T(8,128)(2,1)}, u32[]{:S(2)}) copy-start(bf16[1,768,2048]{2,1,0:T(8,128)(2,1)} %param.22) | copy-start | bytes 9437188
  8.0 46.6 %all-gather.8.cloned.1.call-start = ((), (), s32[]{:S(2)}) async-start(), calls=%async_computation.11 | async-start | bytes 5898240 | tf_op jit(solution)/shard_map/all_gather | solution.py:217
  78.1 5.3 copy-start.62
  78.1 5.6 copy-start.63
  78.1 5.8 copy-start.64
  78.1 6.0 copy-start.65
  78.1 148.0 %all-to-all-start = ((bf16[512,4,1280]{0,2,1:T(8,128)(2,1)}), bf16[512,4,1280]{0,2,1:T(8,128)(2,1)}, u32[]{:S(2)}, u32[]{:S(2)}) async-start(bf16[512,4,1280]{0,2,1:T(8,128)(2,1)} %pad_maximum_fusion), calls=%async_computation | async-start | bytes 10485760 | tf_op jit(solution)/shard_map/all_to_all | solution.py:235
  83.4 186.5 %all-gather.6.cloned.1.call-start = ((), (), s32[]{:S(2)}) async-start(), calls=%async_computation.10 | async-start | bytes 2621440 | tf_op jit(solution)/shard_map/all_gather | solution.py:240
  223.5 83.5 %all-gather.10.cloned.1.call-start = ((), (), s32[]{:S(2)}) async-start(), calls=%async_computation.12 | async-start | bytes 4718592 | tf_op jit(solution)/shard_map/all_gather | solution.py:218
  224.0 132.9 %reduce-scatter.8.cloned.1.call-start = ((), (), s32[]{:S(2)}) async-start(), calls=%async_computation.13 | async-start | bytes 2621440 | tf_op jit(solution)/shard_map/reduce_scatter | solution.py:253
  224.1 60.0 %copy-start.55 = (f32[128]{0:T(128)}, f32[128]{0:T(128)S(1)}, u32[]{:S(2)}) copy-start(f32[128]{0:T(128)S(1)} %convert_element_type.160) | copy-start | bytes 1540
  224.1 57.6 %copy-start.49 = (f32[128]{0:T(128)}, f32[128]{0:T(128)S(1)}, u32[]{:S(2)}) copy-start(f32[128]{0:T(128)S(1)} %convert_element_type.157) | copy-start | bytes 1540
  224.2 58.7 %copy-start.51 = (f32[64]{0:T(128)}, f32[64]{0:T(128)S(1)}, u32[]{:S(2)}) copy-start(f32[64]{0:T(128)S(1)} %negate_power_fusion) | copy-start | bytes 772
  224.2 58.7 %copy-start.38 = (f32[512]{0:T(512)}, f32[512]{0:T(512)S(1)}, u32[]{:S(2)}) copy-start(f32[512]{0:T(512)S(1)} %iota_convert_fusion) | copy-start | bytes 6148
  224.3 67.0 %copy-start.17 = (pred[512,512]{0,1:T(8,128)(4,1)}, pred[512,512]{0,1:T(8,128)(4,1)S(1)}, u32[]{:S(2)}) copy-start(pred[512,512]{0,1:T(8,128)(4,1)S(1)} %iota_compare_fusion) | copy-start | bytes 786436
  280.5 6.6 copy-start.33
  280.5 5.8 copy-start.19
  280.5 5.8 copy-start.21
  281.7 4.6 copy-start.42
  281.7 4.6 copy-start.40
  281.7 4.6 copy-start.29
  289.5 3.5 copy-start.3
  307.0 6.2 copy-start.37
  313.5 58.8 %copy-start.31 = (f32[2048]{0:T(1024)}, f32[2048]{0:T(1024)S(1)}, u32[]{:S(2)}) copy-start(f32[2048]{0:T(1024)S(1)} %convert_element_type.165) | copy-start | bytes 24580
  358.4 14.0 copy-start.59
  358.4 14.0 copy-start.47
  384.8 154.8 %all-to-all-start.1 = ((bf16[32,36,2048]{2,1,0:T(8,128)(2,1)}), bf16[32,36,2048]{2,1,0:T(8,128)(2,1)}, u32[]{:S(2)}, u32[]{:S(2)}) async-start(bf16[32,36,2048]{2,1,0:T(8,128)(2,1)} %broadcast_select_fusion), calls=%async_computation.2 | async-start | bytes 10485760 | tf_op jit(solution)/shard_map/all_to_all | solution.py:275
  402.8 9.8 copy-start.46
  539.6 139.3 %all-to-all-start.3 = ((bf16[32,36,2048]{2,1,0:T(8,128)(2,1)}), bf16[32,36,2048]{2,1,0:T(8,128)(2,1)}, u32[]{:S(2)}, u32[]{:S(2)}) async-start(bf16[32,36,2048]{2,1,0:T(8,128)(2,1)} %select_convert_fusion), calls=%async_computation.4 | async-start | bytes 10485760 | tf_op jit(solution)/shard_map/all_to_all | solution.py:308
  716.6 120.4 %all-to-all-start.4 = ((bf16[32,36,2048]{2,1,0:T(8,128)(2,1)}), bf16[32,36,2048]{2,1,0:T(8,128)(2,1)}, u32[]{:S(2)}, u32[]{:S(2)}) async-start(bf16[32,36,2048]{2,1,0:T(8,128)(2,1)} %reshape.535), calls=%async_computation.5 | async-start | bytes 10485760 | tf_op jit(solution)/shard_map/all_to_all | solution.py:328
  836.9 120.3 %all-to-all-start.2 = ((bf16[32,36,2048]{2,1,0:T(8,128)(2,1)}), bf16[32,36,2048]{2,1,0:T(8,128)(2,1)}, u32[]{:S(2)}, u32[]{:S(2)}) async-start(bf16[32,36,2048]{2,1,0:T(8,128)(2,1)} %reshape.531), calls=%async_computation.3 | async-start | bytes 10485760 | tf_op jit(solution)/shard_map/all_to_all | solution.py:285
  840.5 189.2 %all-gather.12.cloned.1.call-start = ((), (), s32[]{:S(2)}) async-start(), calls=%async_computation.14 | async-start | bytes 2621440 | tf_op jit(solution)/shard_map/all_gather | solution.py:339
  964.5 11.8 copy-start.13
  976.3 5.4 copy-start.5
  976.3 5.4 copy-start.7
  976.3 5.4 copy-start.32
  976.3 5.4 copy-start.48
  981.6 3.4 copy-start.2
  983.6 52.3 %copy-start.8 = (f32[128,2048]{1,0:T(8,128)}, f32[128,2048]{1,0:T(8,128)S(1)}, u32[]{:S(2)}) copy-start(f32[128,2048]{1,0:T(8,128)S(1)} %get-tuple-element.440) | copy-start | bytes 3145732
  984.9 162.8 %reduce-scatter.16.cloned.1.call-start = ((), (), s32[]{:S(2)}) async-start(), calls=%async_computation.18 | async-start | bytes 1081344
  986.4 203.5 %reduce-scatter.10.cloned.1.call-start = ((), (), s32[]{:S(2)}) async-start(), calls=%async_computation.15 | async-start | bytes 2621440 | tf_op jit(solution)/shard_map/reduce_scatter | solution.py:360
  1035.9 4.3 copy-start.18
  1035.9 4.3 copy-start.45
  1040.2 5.0 copy-start.26
  1040.2 5.0 copy-start.28
  1048.1 5.4 copy-start.20
  1048.1 5.4 copy-start.22
  1053.5 9.2 copy-start.68
  1055.2 7.5 slice-start
  1057.1 3.1 copy-start.41
  1057.1 4.4 copy-start.43
  1057.1 5.6 slice-start.1
  1059.0 3.8 copy-start.23
  1067.0 480.2 %reduce-scatter.14.cloned.1.call-start = ((), (), s32[]{:S(2)}) async-start(), calls=%async_computation.17 | async-start | bytes 34603008 | tf_op jit(solution)/shard_map/reduce_scatter | solution.py:405
  1067.1 11.5 copy-start.61
  1067.1 11.5 copy-start.66
  1084.2 915.4 %reduce-scatter.12.cloned.1.call-start = ((), (), s32[]{:S(2)}) async-start(), calls=%async_computation.16 | async-start | bytes 43253760 | tf_op jit(solution)/shard_map/reduce_scatter | solution.py:404
  1112.3 8.7 copy-start.71
  1112.3 8.7 copy-start.73
  1121.0 13.2 copy-start.6
  1134.2 55.7 %copy-start.36 = (f32[2048]{0:T(1024)S(1)}, f32[2048]{0:T(1024)}, u32[]{:S(2)}) copy-start(f32[2048]{0:T(1024)} %copy-done.35) | copy-start | bytes 24580
  1134.2 55.7 %copy-start.54 = (f32[128]{0:T(128)S(1)}, f32[128]{0:T(128)}, u32[]{:S(2)}) copy-start(f32[128]{0:T(128)} %copy-done.53) | copy-start | bytes 1540
  1134.2 115.4 %copy-start.58 = (f32[128]{0:T(128)S(1)}, f32[128]{0:T(128)}, u32[]{:S(2)}) copy-start(f32[128]{0:T(128)} %copy-done.57) | copy-start | bytes 1540
  1134.2 865.5 %copy-start.1 = (bf16[1,768,2048]{2,1,0:T(8,128)(2,1)S(1)}, bf16[1,768,2048]{2,1,0:T(8,128)(2,1)}, u32[]{:S(2)}) copy-start(bf16[1,768,2048]{2,1,0:T(8,128)(2,1)} %param.22) | copy-start | bytes 9437188
  (26 other events, 47.9 us)
Sparse Core Ops, SparseCore 0:
  10.7 43.8 all-gather.7
  988.1 159.6 reduce-scatter.15
  1150.1 39.7 reduce-scatter.9
  1192.7 354.4 reduce-scatter.13
  1550.1 449.5 reduce-scatter.11
Sparse Core Ops, SparseCore 1:
  223.5 46.3 all-gather.5
  271.6 35.3 all-gather.9
  313.3 43.6 reduce-scatter.7
  985.0 44.7 all-gather.11
where the time goes:
time: 2020 us; the launch traced here: 2010 us
  waiting for transfers between devices  1250 us (62%)
  blocking collectives  289 us (14%)
  local copies, waits for them, and re-layouts  214 us (11%)
  matrix products  127 us (6%)
  other arithmetic  71.9 us (4%)
  starting transfers between devices  39.2 us (2%)
    reduce_scatter x1, waiting for transfers between devices, body(): lax.psum_scatter(query_key_value_width, ('seq', 'dp'), scatter_dimension=...  452 us
    reduce_scatter x1, waiting for transfers between devices, body(): lax.psum_scatter(out_total, ('seq', 'dp'), scatter_dimension=0, tiled=True)  293 us
    unnamed x2, blocking collectives  190 us
    all_to_all x1, waiting for transfers between devices, body(): lax.all_to_all(grad_arrived, ('seq', 'dp'), split_axis=0, concat_axis=0,...  103 us
    all_gather x1, blocking collectives, body(): lax.all_gather(router, ('seq', 'dp'), axis=0, tiled=True)  99 us
    all_to_all x1, waiting for transfers between devices, body(): lax.all_to_all(grad_returned.reshape(devices, capacity, MODEL_WIDTH), ('s...  97 us
    all_to_all x1, waiting for transfers between devices, body(): lax.all_to_all(expert_out.reshape(devices, capacity, MODEL_WIDTH), ('seq'...  91.5 us
    all_gather x1, waiting for transfers between devices, body(): lax.all_gather(qkv_weight, 'dp', axis=0, tiled=True)  45.8 us
  transfers between devices with their start and end apart: 14, of which 12 were waited for; matrix products, arithmetic and copies ran while one was open for 14% of the time, Pallas kernels for 0%

commit v1 on v0

--- a/solution.py
+++ b/solution.py
@@ -179,6 +179,14 @@
         one_block, (empty, empty), jnp.arange(block_count)
     )
     return (grad_query.reshape(sequence_length, head_count, HEAD_SIZE), grad_keys, grad_values)
+
+
+def masked_softmax(logits, mask):
+    shifted = jnp.where(mask > 0, logits, FILLER)
+    top = jnp.max(shifted, axis=-1, keepdims=True)
+    powers = jnp.where(mask > 0, jnp.exp(shifted - top), 0.0)
+    total = jnp.sum(powers, axis=-1, keepdims=True)
+    return powers / jnp.where(total > 0, total, 1.0)
 
 
 def body(
@@ -197,48 +205,100 @@
 ):
     tokens = hidden_in.shape[1]
     sequence_number = lax.axis_size("seq")
-    devices = lax.axis_size(("seq", "dp"))
+    planes = lax.axis_size("dp")
+    devices = sequence_number * planes
+    group = lax.axis_index("seq")
+    member = lax.axis_index("dp")
     per_device = QUERY_HEADS // sequence_number
     query_columns = per_device * HEAD_SIZE
+    own_width = query_columns + 2 * HEAD_SIZE
     head_replicas = sequence_number // KEY_VALUE_HEADS
     capacity = (tokens * TOP * 9 + 8 * devices - 1) // (8 * devices)
-    gain_one, gain_query, gain_key, gain_two, full_router = (
-        lax.all_gather(norm1_gain, ("seq", "dp"), axis=0, tiled=True),
-        lax.all_gather(query_gain, ("seq", "dp"), axis=0, tiled=True),
-        lax.all_gather(key_gain, ("seq", "dp"), axis=0, tiled=True),
-        lax.all_gather(norm2_gain, ("seq", "dp"), axis=0, tiled=True),
-        lax.all_gather(router, ("seq", "dp"), axis=0, tiled=True),
-    )
-    gain_one = gain_one.astype(jnp.float32)
-    gain_two = gain_two.astype(jnp.float32)
-    gain_query = gain_query.astype(jnp.float32)
-    gain_key = gain_key.astype(jnp.float32)
-    query_key_value_rows, out_rows = (
-        lax.all_gather(qkv_weight, "dp", axis=0, tiled=True),
-        lax.all_gather(out_weight, "dp", axis=0, tiled=True),
-    )
-    block_of_rows = query_key_value_rows.shape[0]
-    query_part = query_key_value_rows[:, : QUERY_HEADS * HEAD_SIZE].reshape(
-        block_of_rows, sequence_number, query_columns
+    slots = sequence_number * capacity
+    sequence_length = sequence_number * tokens
+    extra = -(-2 * devices // 128) * 128
+
+    shard = norm1_gain.shape[0]
+    small_shard = query_gain.shape[0]
+    small_width = 2 * shard + 2 * small_shard + shard * devices
+    small_rows = -(-small_width // 2048) * 16
+    packed = jnp.concatenate(
+        [norm1_gain, norm2_gain, query_gain, key_gain, router.reshape(-1)]
+    )
+    packed = jnp.pad(packed, (0, small_rows * 128 - small_width)).reshape(small_rows, 128)
+    packed = lax.all_gather(packed, ("seq", "dp"), axis=0, tiled=True)
+    packed = packed.reshape(devices, small_rows * 128)
+    cut = 0
+    pieces = []
+    for width in (shard, shard, small_shard, small_shard, shard * devices):
+        pieces.append(packed[:, cut : cut + width])
+        cut += width
+    gain_one = pieces[0].reshape(-1).astype(jnp.float32)
+    gain_two = pieces[1].reshape(-1).astype(jnp.float32)
+    gain_query = pieces[2].reshape(-1).astype(jnp.float32)
+    gain_key = pieces[3].reshape(-1).astype(jnp.float32)
+    full_router = pieces[4].reshape(MODEL_WIDTH, devices)
+
+    query_part = qkv_weight[:, : QUERY_HEADS * HEAD_SIZE].reshape(
+        shard, sequence_number, query_columns
     )
     paired_portion = jnp.repeat(
-        query_key_value_rows[:, QUERY_HEADS * HEAD_SIZE :].reshape(
-            block_of_rows, 2, KEY_VALUE_HEADS, HEAD_SIZE
-        ),
+        qkv_weight[:, QUERY_HEADS * HEAD_SIZE :].reshape(shard, 2, KEY_VALUE_HEADS, HEAD_SIZE),
         head_replicas,
         axis=2,
     )
     paired_portion = jnp.transpose(paired_portion, (0, 2, 1, 3)).reshape(
-        block_of_rows, sequence_number, 2 * HEAD_SIZE
-    )
-    column_send = jnp.concatenate([query_part, paired_portion], axis=-1)
-    own_cols = lax.all_to_all(column_send, "seq", split_axis=1, concat_axis=0, tiled=True).reshape(
-        block_of_rows * sequence_number, query_columns + 2 * HEAD_SIZE
-    )
+        shard, sequence_number, 2 * HEAD_SIZE
+    )
+    column_send = jnp.transpose(
+        jnp.concatenate([query_part, paired_portion], axis=-1), (1, 0, 2)
+    )
+    own_part = lax.all_to_all(column_send, "seq", split_axis=0, concat_axis=0, tiled=True)
+    own_cols = lax.all_gather(own_part, "dp", axis=1, tiled=True).reshape(MODEL_WIDTH, own_width)
+    out_rows = lax.all_gather(out_weight, "dp", axis=0, tiled=True)
+
+    full_routes = lax.all_gather(routes[0], "seq", axis=0, tiled=True)
+    expert_ids = jnp.arange(devices, dtype=jnp.int32)
+    route_mask = jnp.sum(
+        (full_routes[:, :, None] == expert_ids[None, None, :]).astype(jnp.float32), axis=1
+    )
+    before = (
+        jnp.arange(tokens)[:, None] > jnp.arange(tokens)[None, :]
+    ).astype(jnp.bfloat16)
+    places = jnp.einsum(
+        "tu,sue->ste",
+        before,
+        route_mask.astype(jnp.bfloat16).reshape(sequence_number, tokens, devices),
+        preferred_element_type=jnp.float32,
+    ).astype(jnp.int32)
+    places = places + (jnp.arange(sequence_number, dtype=jnp.int32) * capacity)[:, None, None]
+    places = jnp.where(route_mask > 0, places.reshape(sequence_length, devices), -1)
+    plane_places = lax.dynamic_slice_in_dim(places, group * planes, planes, 1)
+    picker = (
+        plane_places.T[:, None, :] == jnp.arange(slots, dtype=jnp.int32)[None, :, None]
+    ).astype(jnp.bfloat16).reshape(planes * slots, sequence_length)
+
+    def dispatch(rows):
+        sent = jnp.dot(picker, rows, preferred_element_type=jnp.float32).astype(jnp.bfloat16)
+        return lax.all_to_all(
+            sent.reshape(planes, slots, rows.shape[-1]), "dp", split_axis=0, concat_axis=0, tiled=True
+        ).reshape(planes * slots, rows.shape[-1])
+
+    def combine(rows):
+        width = rows.shape[-1]
+        back = lax.all_to_all(
+            rows.reshape(planes, slots, width), "dp", split_axis=0, concat_axis=0, tiled=True
+        ).reshape(planes * slots, width)
+        sums = inner_rows(picker, back).astype(jnp.bfloat16)
+        return lax.psum_scatter(sums, "seq", scatter_dimension=0, tiled=True).astype(jnp.float32)
+
+    mask_columns = jnp.pad(route_mask.astype(jnp.bfloat16), ((0, 0), (0, extra - devices)))
+    cotangent_full = lax.all_gather(cotangent[0], "seq", axis=0, tiled=True)
+    grad_arrived = dispatch(jnp.concatenate([cotangent_full, mask_columns], axis=1))
+
+    hidden_full = lax.all_gather(hidden_in[0], "seq", axis=0, tiled=True)
     residual = hidden_in[0].astype(jnp.float32)
-    normed_low = rms_norm(residual, gain_one).astype(jnp.bfloat16)
-    normed_full = lax.all_gather(normed_low, "seq", axis=0, tiled=True)
-    sequence_length = normed_full.shape[0]
+    normed_full = rms_norm(hidden_full.astype(jnp.float32), gain_one).astype(jnp.bfloat16)
     cosine, sine_table = rope_tables(jnp.arange(sequence_length).astype(jnp.float32), HEAD_SIZE)
     projected_rows = jnp.dot(normed_full, own_cols, preferred_element_type=jnp.float32)
     queries, key_head, value_head = prepare_heads(
@@ -254,64 +314,28 @@
         branch_part.astype(jnp.bfloat16), "seq", scatter_dimension=0, tiled=True
     ).astype(jnp.float32)
     mixed_low = rms_norm(hidden1, gain_two).astype(jnp.bfloat16)
-    logits = jnp.dot(mixed_low, full_router, preferred_element_type=jnp.float32)
-    local_routes = routes[0]
-    chosen = jnp.take_along_axis(logits, local_routes, axis=1)
-    gate_weights = jax.nn.softmax(chosen, axis=-1)
-    flat_routes = local_routes.reshape(-1)
-    onehot = (flat_routes[:, None] == jnp.arange(devices, dtype=jnp.int32)[None, :]).astype(
-        jnp.int32
-    )
-    slot_index = jnp.sum(jnp.cumsum(onehot, axis=0) * onehot, axis=-1) - 1
-    target = flat_routes * capacity + slot_index
-    owner_row = jnp.arange(tokens * TOP, dtype=jnp.int32) // TOP
-    route_ids = jnp.arange(tokens * TOP, dtype=jnp.int32)
-    source = jnp.zeros((devices * capacity,), jnp.int32).at[target].set(owner_row)
-    route_of = jnp.zeros((devices * capacity,), jnp.int32).at[target].set(route_ids)
-    filled = jnp.zeros((devices * capacity,), jnp.bool_).at[target].set(True)
-    outgoing = jnp.where(filled[:, None], mixed_low[source], jnp.zeros((), jnp.bfloat16)).reshape(
-        devices, capacity, MODEL_WIDTH
-    )
-    arrived = lax.all_to_all(
-        outgoing, ("seq", "dp"), split_axis=0, concat_axis=0, tiled=True
-    ).reshape(-1, MODEL_WIDTH)
+    mixed_full = lax.all_gather(mixed_low, "seq", axis=0, tiled=True)
+    arrived = dispatch(mixed_full)
+
     weight_in = gate_up_weight[0]
     weight_back = down_weight[0]
+    own_expert = group * planes + member
+    row_mask = grad_arrived[:, MODEL_WIDTH : MODEL_WIDTH + devices].astype(jnp.float32)
+    grad_rows = grad_arrived[:, :MODEL_WIDTH].astype(jnp.float32)
+    row_gates = masked_softmax(
+        jnp.dot(arrived, full_router, preferred_element_type=jnp.float32), row_mask
+    )
+    gate = jnp.sum(jnp.where(expert_ids[None, :] == own_expert, row_gates, 0.0), axis=1)[:, None]
     gate_up = jnp.dot(arrived, weight_in, preferred_element_type=jnp.float32)
     hidden = (jax.nn.silu(gate_up[:, :FF]) * gate_up[:, FF:]).astype(jnp.bfloat16)
-    expert_out = jnp.dot(hidden, weight_back, preferred_element_type=jnp.float32).astype(
-        jnp.bfloat16
-    )
-    returned = lax.all_to_all(
-        expert_out.reshape(devices, capacity, MODEL_WIDTH),
-        ("seq", "dp"),
-        split_axis=0,
-        concat_axis=0,
-        tiled=True,
-    ).reshape(-1, MODEL_WIDTH)
-    picked = returned[target].reshape(tokens, TOP, MODEL_WIDTH)
-    combined = jnp.einsum("tk,tkd->td", gate_weights, picked.astype(jnp.float32))
-    output = (hidden1 + combined).astype(jnp.bfloat16)
-    grad_result = cotangent[0].astype(jnp.float32)
-    flat_gates = gate_weights.reshape(-1)
-    grad_returned = jnp.where(
-        filled[:, None], flat_gates[route_of][:, None] * grad_result[source], 0.0
-    ).astype(jnp.bfloat16)
-    grad_gates = jnp.einsum("tkd,td->tk", picked.astype(jnp.float32), grad_result)
-    grad_chosen = gate_weights * (
-        grad_gates - jnp.sum(gate_weights * grad_gates, axis=-1, keepdims=True)
-    )
-    route_table = (
-        local_routes[:, :, None] == jnp.arange(devices, dtype=jnp.int32)[None, None, :]
-    ).astype(jnp.float32)
-    grad_logits = jnp.sum(route_table * grad_chosen[:, :, None], axis=1).astype(jnp.bfloat16)
-    back_rows = lax.all_to_all(
-        grad_returned.reshape(devices, capacity, MODEL_WIDTH),
-        ("seq", "dp"),
-        split_axis=0,
-        concat_axis=0,
-        tiled=True,
-    ).reshape(-1, MODEL_WIDTH)
+    expert_out = (
+        jnp.dot(hidden, weight_back, preferred_element_type=jnp.float32)
+        .astype(jnp.bfloat16)
+        .astype(jnp.float32)
+    )
+    grad_gate = jnp.sum(expert_out * grad_rows, axis=1, keepdims=True)
+    combined_rows = (gate * expert_out).astype(jnp.bfloat16)
+    back_rows = (gate * grad_rows).astype(jnp.bfloat16)
     grad_weight_back = inner_rows(hidden, back_rows)
     grad_hidden = outer_cols(back_rows, weight_back)
     _, pull_act = jax.vjp(
@@ -320,17 +344,30 @@
     grad_gate_in, grad_up_in = pull_act(grad_hidden)
     grad_gate_up = jnp.concatenate([grad_gate_in, grad_up_in], axis=1).astype(jnp.bfloat16)
     grad_weight_in = inner_rows(arrived, grad_gate_up)
-    grad_arrived = (
-        outer_cols(grad_gate_up, weight_in)
-        .astype(jnp.bfloat16)
-        .reshape(devices, capacity, MODEL_WIDTH)
-    )
-    grad_sent = lax.all_to_all(
-        grad_arrived, ("seq", "dp"), split_axis=0, concat_axis=0, tiled=True
-    ).reshape(-1, MODEL_WIDTH)
-    grad_mixed = jnp.sum(
-        grad_sent[target].reshape(tokens, TOP, MODEL_WIDTH).astype(jnp.float32), axis=1
-    ) + outer_cols(grad_logits, full_router)
+    grad_back = outer_cols(grad_gate_up, weight_in).astype(jnp.bfloat16)
+    high = grad_gate.astype(jnp.bfloat16)
+    rest = (grad_gate - high.astype(jnp.float32)).astype(jnp.bfloat16)
+    extra_ids = jnp.arange(extra, dtype=jnp.int32)[None, :]
+    gate_columns = jnp.where(
+        extra_ids == own_expert,
+        high,
+        jnp.where(extra_ids == own_expert + devices, rest, jnp.zeros((), jnp.bfloat16)),
+    )
+    grad_sent = combine(jnp.concatenate([grad_back, gate_columns], axis=1))
+    output = (hidden1 + combine(combined_rows)).astype(jnp.bfloat16)
+
+    grad_result = cotangent[0].astype(jnp.float32)
+    own_mask = lax.dynamic_slice_in_dim(route_mask, group * tokens, tokens, 0)
+    logits = jnp.dot(mixed_low, full_router, preferred_element_type=jnp.float32)
+    gates = masked_softmax(logits, own_mask)
+    grad_gates = (
+        grad_sent[:, MODEL_WIDTH : MODEL_WIDTH + devices]
+        + grad_sent[:, MODEL_WIDTH + devices : MODEL_WIDTH + 2 * devices]
+    )
+    grad_logits = (
+        gates * (grad_gates - jnp.sum(gates * grad_gates, axis=-1, keepdims=True))
+    ).astype(jnp.bfloat16)
+    grad_mixed = grad_sent[:, :MODEL_WIDTH] + outer_cols(grad_logits, full_router)
     grad_router_w = inner_rows(mixed_low, grad_logits)
     _, pull_two = jax.vjp(rms_norm, hidden1, gain_two)
     grad_hidden_norm, grad_gain_two = pull_two(grad_mixed)
@@ -338,6 +375,9 @@
     grad_branch = grad_hidden1.astype(jnp.bfloat16)
     branch_full = lax.all_gather(grad_branch, "seq", axis=0, tiled=True)
     grad_out_rows = inner_rows(heads_low, branch_full)
+    shard_out = lax.psum_scatter(
+        grad_out_rows.astype(jnp.bfloat16), "dp", scatter_dimension=0, tiled=True
+    ).astype(jnp.float32)
     grad_heads = (
         outer_cols(branch_full, out_rows)
         .astype(jnp.bfloat16)
@@ -356,66 +396,70 @@
     )
     grad_projected, grad_gain_query, grad_gain_key = pull_prep((grad_query, grad_keys, grad_values))
     grad_proj_low = grad_projected.astype(jnp.bfloat16)
-    gradient_columns = inner_rows(normed_full, grad_proj_low)
     grad_normed = lax.psum_scatter(
         outer_cols(grad_proj_low, own_cols).astype(jnp.bfloat16),
         "seq",
         scatter_dimension=0,
         tiled=True,
     ).astype(jnp.float32)
+    gradient_columns = inner_rows(normed_full, grad_proj_low).astype(jnp.bfloat16)
+    gradient_columns = jnp.transpose(
+        gradient_columns.reshape(sequence_number, planes, shard, own_width), (1, 0, 2, 3)
+    ).reshape(MODEL_WIDTH, own_width)
+    column_sums = lax.psum_scatter(gradient_columns, "dp", scatter_dimension=0, tiled=True)
+    column_sums = lax.all_to_all(
+        column_sums.reshape(sequence_number, shard, own_width),
+        "seq",
+        split_axis=0,
+        concat_axis=0,
+        tiled=True,
+    ).astype(jnp.float32)
+    shard_query = jnp.transpose(column_sums[:, :, :query_columns], (1, 0, 2)).reshape(
+        shard, QUERY_HEADS * HEAD_SIZE
+    )
+    shard_paired = jnp.sum(
+        column_sums[:, :, query_columns:].reshape(
+            KEY_VALUE_HEADS, head_replicas, shard, 2, HEAD_SIZE
+        ),
+        axis=1,
+    )
+    shard_paired = jnp.transpose(shard_paired, (1, 2, 0, 3)).reshape(
+        shard, 2 * KEY_VALUE_HEADS * HEAD_SIZE
+    )
+    shard_qkv = jnp.concatenate([shard_query, shard_paired], axis=1)
     _, pull_one = jax.vjp(rms_norm, residual, gain_one)
     grad_residual_norm, grad_gain_one = pull_one(grad_normed)
     grad_input = grad_hidden1 + grad_residual_norm
-    group = lax.axis_index("seq")
-    paired_heads = group // head_replicas
-    query_key_value_width = jnp.zeros(
-        (MODEL_WIDTH, (QUERY_HEADS + 2 * KEY_VALUE_HEADS) * HEAD_SIZE), jnp.float32
-    )
-    query_key_value_width = lax.dynamic_update_slice(
-        query_key_value_width, gradient_columns[:, :query_columns], (0, group * query_columns)
-    )
-    query_key_value_width = lax.dynamic_update_slice(
-        query_key_value_width,
-        gradient_columns[:, query_columns : query_columns + HEAD_SIZE],
-        (0, QUERY_HEADS * HEAD_SIZE + paired_heads * HEAD_SIZE),
-    )
-    query_key_value_width = lax.dynamic_update_slice(
-        query_key_value_width,
-        gradient_columns[:, query_columns + HEAD_SIZE :],
-        (0, (QUERY_HEADS + KEY_VALUE_HEADS) * HEAD_SIZE + paired_heads * HEAD_SIZE),
-    )
-    out_total = lax.dynamic_update_slice(
-        jnp.zeros((QUERY_HEADS * HEAD_SIZE, MODEL_WIDTH), jnp.float32),
-        grad_out_rows,
-        (group * query_columns, 0),
-    )
-    (
-        shard_gain_one,
-        shard_gain_query,
-        shard_gain_key,
-        shard_qkv,
-        shard_out,
-        shard_gain_two,
-        shard_router,
-    ) = (
-        lax.psum_scatter(grad_gain_one, ("seq", "dp"), scatter_dimension=0, tiled=True),
-        lax.psum_scatter(grad_gain_query, ("seq", "dp"), scatter_dimension=0, tiled=True),
-        lax.psum_scatter(grad_gain_key, ("seq", "dp"), scatter_dimension=0, tiled=True),
-        lax.psum_scatter(query_key_value_width, ("seq", "dp"), scatter_dimension=0, tiled=True),
-        lax.psum_scatter(out_total, ("seq", "dp"), scatter_dimension=0, tiled=True),
-        lax.psum_scatter(grad_gain_two, ("seq", "dp"), scatter_dimension=0, tiled=True),
-        lax.psum_scatter(grad_router_w, ("seq", "dp"), scatter_dimension=0, tiled=True),
-    )
+
+    small = jnp.concatenate(
+        [
+            grad_gain_one.reshape(devices, shard),
+            grad_gain_two.reshape(devices, shard),
+            grad_gain_query.reshape(devices, small_shard),
+            grad_gain_key.reshape(devices, small_shard),
+            grad_router_w.reshape(devices, shard * devices),
+        ],
+        axis=1,
+    )
+    small = jnp.pad(small, ((0, 0), (0, small_rows * 128 - small_width)))
+    small = lax.psum_scatter(
+        small.reshape(devices * small_rows, 128), ("seq", "dp"), scatter_dimension=0, tiled=True
+    ).reshape(-1)
+    cut = 0
+    pieces = []
+    for width in (shard, shard, small_shard, small_shard, shard * devices):
+        pieces.append(small[cut : cut + width])
+        cut += width
     return (
         output[None],
         grad_input[None],
-        shard_gain_one,
-        shard_gain_query,
-        shard_gain_key,
+        pieces[0],
+        pieces[2],
+        pieces[3],
         shard_qkv,
         shard_out,
-        shard_gain_two,
-        shard_router,
+        pieces[1],
+        pieces[4].reshape(shard, devices),
         grad_weight_in[None],
         grad_weight_back[None],
     )

time: 2020 us -> 968 us (0.48)
  waiting for transfers between devices: 1250 us -> 472 us
  local copies, waits for them, and re-layouts: 214 us -> 50.4 us
  blocking collectives: 289 us -> 218 us
  starting transfers between devices: 39.2 us -> 13.9 us
  other arithmetic: 71.9 us -> 50.5 us
    reduce_scatter x2 -> x5, waiting for transfers between devices: 746 us -> 271 us  [the longest x1 134 us: body(): lax.psum_scatter(small.reshape(devices * small_rows, 128), ('seq', 'dp'),...]
    all_to_all x5 -> x3, waiting for transfers between devices: 291 us -> 45.9 us  [the longest x2 45.9 us: dispatch(): lax.all_to_all(sent.reshape(planes, slots, rows.shape[-1]), 'dp', split_a...]
    unnamed x2 -> x0, blocking collectives: 190 us -> none
    all_to_all x0 -> x3, blocking collectives: none -> 161 us  [the longest x2 119 us: combine(): lax.all_to_all(rows.reshape(planes, slots, width), 'dp', split_axis=0, co...]
    gather x11 -> x0, local copies, waits for them, and re-layouts: 76.3 us -> none  [the longest x2 21.5 us: body(): grad_result[source]]
    all_gather x1 -> x2, blocking collectives: 99 us -> 57.1 us  [the longest x1 43 us: body(): packed = lax.all_gather(packed, ('seq', 'dp'), axis=0, tiled=True)]
    reduce_scatter x1, waiting for transfers between devices: 40.7 us -> 0.02 us  [body(): lax.psum_scatter(outer_cols(grad_proj_low, own_cols).astype(jnp.bfloat16)...]
    reshape x6 -> x17, local copies, waits for them, and re-layouts: 43.5 us -> 11.5 us  [the longest x1 2.58 us: body(): gradient_columns.reshape(sequence_number, planes, shard, own_width)]
  transfers between devices with their start and end apart: 14 -> 16, of which waited for: 12 -> 11; matrix products, arithmetic and copies ran while one was open for 14% -> 15% of each run, Pallas kernels for 0% -> 0%
where the time goes in v1:
time: 968 us; the launch traced here: 960 us
  waiting for transfers between devices  472 us (49%)
  blocking collectives  218 us (23%)
  matrix products  139 us (14%)
  other arithmetic  50.5 us (5%)
  local copies, waits for them, and re-layouts  50.4 us (5%)
  between operations  15.7 us (2%)
  starting transfers between devices  13.9 us (1%)
    reduce_scatter x1, waiting for transfers between devices, body(): lax.psum_scatter(small.reshape(devices * small_rows, 128), ('seq', 'dp'),...  134 us
    all_to_all x2, blocking collectives, combine(): lax.all_to_all(rows.reshape(planes, slots, width), 'dp', split_axis=0, co...  119 us
    reduce_scatter x2, waiting for transfers between devices, combine(): lax.psum_scatter(sums, 'seq', scatter_dimension=0, tiled=True)  89.5 us
    reduce_scatter x1, waiting for transfers between devices, body(): lax.psum_scatter(grad_out_rows.astype(jnp.bfloat16), 'dp', scatter_dimens...  46.8 us
    all_to_all x2, waiting for transfers between devices, dispatch(): lax.all_to_all(sent.reshape(planes, slots, rows.shape[-1]), 'dp', split_a...  45.9 us
    all_gather x1, waiting for transfers between devices, body(): branch_full = lax.all_gather(grad_branch, 'seq', axis=0, tiled=True)  45.5 us
    all_gather x1, waiting for transfers between devices, body(): mixed_full = lax.all_gather(mixed_low, 'seq', axis=0, tiled=True)  45.4 us
    dot_general x7, matrix products, inner_rows(): lax.dot_general(left, right, (((0,), (0,)), ((), ())), preferred_element_...  43.6 us
  transfers between devices with their start and end apart: 16, of which 11 were waited for; matrix products, arithmetic and copies ran while one was open for 15% of the time, Pallas kernels for 0%

profile of v1, /device:TPU:0, one launch (start us, length us, event | category | flops | bytes accessed | tf_op | source)
XLA Modules:
  0.0 959.5 jit_solution(3867272555280211742)
XLA Ops:
  9.0 1.9 slice.90
  11.2 2.2 reshape.556
  14.9 41.9 %all_to_all.30 = bf16[4,64,1280]{2,1,0:T(8,128)(2,1)S(1)} all-to-all(bf16[4,64,1280]{2,1,0:T(8,128)(2,1)S(1)} %copy.255), channel_id=1, replica_groups=mesh['seq'=4,'dp'=8] {'seq'}, dimensions={0} | all-to-all | bytes 1310720 | tf_op jit(solution)/shard_map/all_to_all | solution.py:256
  59.9 43.0 %all_gather.25 = bf16[1024,128]{1,0:T(8,128)(2,1)} all-gather(bf16[32,128]{1,0:T(8,128)(2,1)S(1)} %pad_bitcast_fusion), channel_id=1, replica_groups=mesh['seq'=4,'dp'=8] {'seq','dp'}, dimensions={0}, use_global_device_ids=true | all-gather | bytes 270336 | tf_op jit(solution)/shard_map/all_gather | solution.py:229
  102.9 1.8 reshape.555
  107.8 1.8 multiply_cosine_fusion
  109.6 2.1 fusion.12
  111.7 3.8 all-gather.10.cloned.1.call-done
  115.5 3.3 copy.257
  118.8 2.9 fusion.48
  121.8 1.9 slice_bitcast_fusion.1
  129.3 1.9 fusion.60
  131.3 2.3 fusion.30
  134.4 2.3 fusion.9
  136.7 1.8 exponential_reduce_fusion
  140.8 4.8 bitcast_convert_fusion.1
  145.6 8.5 all-gather.12.cloned.1.call-done
  154.0 6.2 convolution_convert_fusion.6
  163.6 14.2 %all-gather.1 = s32[1,512,8]{1,2,0:T(8,128)S(1)} all-gather(s32[1,128,8]{1,2,0:T(8,128)} %param.13), channel_id=3, replica_groups=mesh['seq'=4,'dp'=8] {'seq'}, dimensions={1}, use_global_device_ids=true | all-gather | bytes 20480 | tf_op jit(solution)/shard_map/all_gather | solution.py:260
  182.1 1.9 bitcast_compare_fusion
  184.1 17.5 %all-gather.20.cloned.1.call-done = bf16[1,512,2048]{2,1,0:T(8,128)(2,1)} async-done(((bf16[1,128,2048]{2,1,0:T(8,128)(2,1)}), bf16[1,512,2048]{2,1,0:T(8,128)(2,1)}) %all-gather.20.cloned.1.call-update) | async-done | bytes 2097168 | tf_op jit(solution)/shard_map/all_gather | solution.py:296
  201.6 7.1 convolution_convert_fusion
  208.6 4.6 all-to-all-start.1
  213.3 33.1 %reduce-scatter.8.cloned.1.call-done = bf16[128,2048]{1,0:T(8,128)(2,1)} async-done(((bf16[512,2048]{1,0:T(8,128)(2,1)}), bf16[128,2048]{1,0:T(8,128)(2,1)}) %reduce-scatter.8.cloned.1.call-update) | async-done | bytes 524304 | tf_op jit(solution)/shard_map/reduce_scatter | solution.py:313
  248.9 2.2 multiply_convert_fusion.2
  251.1 45.4 %all-gather.14.cloned.1.call-done = bf16[512,2048]{1,0:T(8,128)(2,1)} async-done(((bf16[128,2048]{1,0:T(8,128)(2,1)}), bf16[512,2048]{1,0:T(8,128)(2,1)}) %all-gather.14.cloned.1.call-update) | async-done | bytes 2097168 | tf_op jit(solution)/shard_map/all_gather | solution.py:317
  296.6 6.6 convolution_convert_fusion.3
  303.2 4.6 all-to-all-start.2
  309.5 2.1 reshape.566
  313.3 1.7 slice.127
  315.0 1.7 copy.303
  316.7 45.9 %all-to-all-done.2 = bf16[8,144,2048]{2,1,0:T(8,128)(2,1)} async-done(((bf16[8,144,2048]{2,1,0:T(8,128)(2,1)}), bf16[8,144,2048]{2,1,0:T(8,128)(2,1)}, u32[]{:S(2)}, u32[]{:S(2)}) %all-to-all-start.2) | async-done | bytes 4718624 | tf_op jit(solution)/shard_map/all_to_all | solution.py:283
  362.6 4.0 fusion.98
  366.7 11.4 %fusion.7 = f32[1152,1536]{1,0:T(8,128)S(1)} fusion(bf16[1152,2048]{1,0:T(8,128)(2,1)} %bitcast.23, bf16[1,2048,1536]{2,1,0:T(8,128)(2,1)} %param.21), kind=kOutput, calls=%fused_computation.20 | convolution fusion | flops 7247757312 | bytes 18087936 | tf_op jit(solution)/shard_map/dot_general | solution.py:329
  378.2 7.3 fusion.17
  385.5 9.2 fusion.2
  394.8 7.8 convolution_convert_fusion.4
  403.5 60.3 %all_to_all.31 = bf16[8,144,2176]{2,1,0:T(8,128)(2,1)S(1)} all-to-all(bf16[8,144,2176]{2,1,0:T(8,128)(2,1)S(1)} %bitcast.226), channel_id=1, replica_groups=mesh['seq'=4,'dp'=8] {'dp'}, dimensions={0} | all-to-all | bytes 10027008 | tf_op jit(solution)/shard_map/all_to_all | solution.py:289
  463.8 4.5 fusion.10
  470.0 41.4 %reduce-scatter.12.cloned.1.call-done = bf16[128,2176]{1,0:T(8,128)(2,1)} async-done(((bf16[512,2176]{1,0:T(8,128)(2,1)}), bf16[128,2176]{1,0:T(8,128)(2,1)}) %reduce-scatter.12.cloned.1.call-update) | async-done | bytes 557072 | tf_op jit(solution)/shard_map/reduce_scatter | solution.py:293
  512.8 2.3 multiply_reduce_fusion.2
  515.8 2.0 fusion.95
  517.9 45.5 %all-gather.16.cloned.1.call-done = bf16[512,2048]{1,0:T(8,128)(2,1)} async-done(((bf16[128,2048]{1,0:T(8,128)(2,1)}), bf16[512,2048]{1,0:T(8,128)(2,1)}) %all-gather.16.cloned.1.call-update) | async-done | bytes 2097168 | tf_op jit(solution)/shard_map/all_gather | solution.py:376
  563.3 6.2 convolution_convert_fusion.8
  569.5 1.7 copy.270
  571.2 2.3 fusion.29
  573.6 4.9 fusion.4
  581.4 5.3 convolution_bitcast_fusion.4
  588.5 1.8 multiply_reduce_fusion
  590.4 1.8 copy_bitcast_fusion
  596.1 4.1 convolution_convert_fusion.7
  600.3 5.4 convolution_convert_fusion.1
  605.7 2.6 copy.283
  608.3 58.3 %all_to_all.32 = bf16[8,144,2048]{2,1,0:T(8,128)(2,1)S(1)} all-to-all(bf16[8,144,2048]{2,1,0:T(8,128)(2,1)} %bitcast.234), channel_id=1, replica_groups=mesh['seq'=4,'dp'=8] {'dp'}, dimensions={0} | all-to-all | bytes 9437184 | tf_op jit(solution)/shard_map/all_to_all | solution.py:289
  666.7 4.2 bitcast_convert_fusion
  676.1 6.0 convolution_convert_fusion.5
  683.7 9.0 convolution_bitcast_fusion.2
  692.8 13.2 %convolution_bitcast_fusion = f32[1,2048,1536]{2,1,0:T(8,128)} fusion(bf16[1152,2048]{1,0:T(8,128)(2,1)} %bitcast.23, bf16[1152,768]{1,0:T(8,128)(2,1)S(1)} %copy-done.91, bf16[1152,768]{1,0:T(8,128)(2,1)S(1)} %copy-done.89), kind=kOutput, calls=%fused_computation.7 | convolution fusion | flops 7254835200 | bytes 20840448 | tf_op jit(solution)/shard_map/dot_general | solution.py:60
  706.0 4.2 all-to-all-start.5
  710.2 48.1 %reduce-scatter.10.cloned.1.call-done = bf16[128,2048]{1,0:T(8,128)(2,1)} async-done(((bf16[512,2048]{1,0:T(8,128)(2,1)}), bf16[128,2048]{1,0:T(8,128)(2,1)}) %reduce-scatter.10.cloned.1.call-update) | async-done | bytes 524304 | tf_op jit(solution)/shard_map/reduce_scatter | solution.py:293
  758.3 3.0 fusion.44
  761.3 134.2 %reduce-scatter.16.cloned.1.call-done = f32[32,128]{1,0:T(8,128)} async-done(((f32[1024,128]{1,0:T(8,128)}), f32[32,128]{1,0:T(8,128)}) %reduce-scatter.16.cloned.1.call-update) | async-done | bytes 16400 | tf_op jit(solution)/shard_map/reduce_scatter | solution.py:445
  899.7 46.8 %reduce-scatter.20.cloned.1.call-done = bf16[128,2048]{1,0:T(8,128)(2,1)} async-done(((bf16[1024,2048]{1,0:T(8,128)(2,1)}), bf16[128,2048]{1,0:T(8,128)(2,1)}) %reduce-scatter.20.cloned.1.call-update) | async-done | bytes 524304 | tf_op jit(solution)/shard_map/reduce_scatter | solution.py:378
  946.5 2.1 convert_element_type.310
  (319 shorter events, 60.2 us)
Async XLA Ops:
  7.2 371.0 %copy-start = (bf16[1,768,2048]{2,1,0:T(8,128)(2,1)S(1)}, bf16[1,768,2048]{2,1,0:T(8,128)(2,1)}, u32[]{:S(2)}) copy-start(bf16[1,768,2048]{2,1,0:T(8,128)(2,1)} %param.22) | copy-start | bytes 9437188
  7.2 102.4 %all-gather.18.cloned.1.call-start = ((), (), s32[]{:S(2)}) async-start(), calls=%async_computation.24 | async-start | bytes 2621440 | tf_op jit(solution)/shard_map/all_gather | solution.py:299
  7.9 107.5 %all-gather.10.cloned.1.call-start = ((), (), s32[]{:S(2)}) async-start(), calls=%async_computation.13 | async-start | bytes 5898240 | tf_op jit(solution)/shard_map/all_gather | solution.py:257
  14.8 44.8 %copy-start.58 = (bf16[64,32]{0,1:T(8,128)(2,1)S(1)}, bf16[64,32]{0,1:T(8,128)(2,1)}, u32[]{:S(2)}) copy-start(bf16[64,32]{0,1:T(8,128)(2,1)} %param.20) | copy-start | bytes 12292
  14.8 45.0 %copy-start.79 = (bf16[64]{0:T(256)(128)(2,1)S(1)}, bf16[64]{0:T(256)(128)(2,1)}, u32[]{:S(2)}) copy-start(bf16[64]{0:T(256)(128)(2,1)} %param.14) | copy-start | bytes 388
  14.8 45.0 %copy-start.80 = (bf16[64]{0:T(256)(128)(2,1)S(1)}, bf16[64]{0:T(256)(128)(2,1)}, u32[]{:S(2)}) copy-start(bf16[64]{0:T(256)(128)(2,1)} %param.19) | copy-start | bytes 388
  14.8 45.0 %copy-start.81 = (bf16[4]{0:T(256)(128)(2,1)S(1)}, bf16[4]{0:T(256)(128)(2,1)}, u32[]{:S(2)}) copy-start(bf16[4]{0:T(256)(128)(2,1)} %param.15) | copy-start | bytes 28
  14.8 45.0 %copy-start.82 = (bf16[4]{0:T(256)(128)(2,1)S(1)}, bf16[4]{0:T(256)(128)(2,1)}, u32[]{:S(2)}) copy-start(bf16[4]{0:T(256)(128)(2,1)} %param.16) | copy-start | bytes 28
  58.1 95.9 %all-gather.12.cloned.1.call-start = ((), (), s32[]{:S(2)}) async-start(), calls=%async_computation.14 | async-start | bytes 4718592 | tf_op jit(solution)/shard_map/all_gather | solution.py:258
  58.9 142.7 %all-gather.20.cloned.1.call-start = ((), (), s32[]{:S(2)}) async-start(), calls=%async_computation.25 | async-start | bytes 2621440 | tf_op jit(solution)/shard_map/all_gather | solution.py:296
  59.4 186.9 %reduce-scatter.8.cloned.1.call-start = ((), (), s32[]{:S(2)}) async-start(), calls=%async_computation.15 | async-start | bytes 2621440 | tf_op jit(solution)/shard_map/reduce_scatter | solution.py:313
  106.9 11.8 %copy-start.65 = (f32[64]{0:T(128)}, f32[64]{0:T(128)S(1)}, u32[]{:S(2)}) copy-start(f32[64]{0:T(128)S(1)} %negate_power_fusion) | copy-start | bytes 772
  107.0 11.8 %copy-start.46 = (f32[512]{0:T(512)}, f32[512]{0:T(512)S(1)}, u32[]{:S(2)}) copy-start(f32[512]{0:T(512)S(1)} %iota_convert_fusion) | copy-start | bytes 6148
  107.0 11.7 %copy-start.41 = (f32[2048]{0:T(1024)}, f32[2048]{0:T(1024)S(1)}, u32[]{:S(2)}) copy-start(f32[2048]{0:T(1024)S(1)} %reshape.587) | copy-start | bytes 24580
  107.8 19.3 %copy-start.56 = (f32[128]{0:T(128)}, f32[128]{0:T(128)S(1)}, u32[]{:S(2)}) copy-start(f32[128]{0:T(128)S(1)} %reshape.588) | copy-start | bytes 1540
  111.7 7.1 copy-start.73
  127.0 6.5 copy-start.21
  127.0 6.5 copy-start.23
  208.6 94.6 %all-to-all-start.1 = ((bf16[8,144,2176]{2,1,0:T(8,128)(2,1)}), bf16[8,144,2176]{2,1,0:T(8,128)(2,1)}, u32[]{:S(2)}, u32[]{:S(2)}) async-start(bf16[8,144,2176]{2,1,0:T(8,128)(2,1)} %bitcast.233), calls=%async_computation.2 | async-start | bytes 10027008 | tf_op jit(solution)/shard_map/all_to_all | solution.py:283
  213.3 83.3 %all-gather.14.cloned.1.call-start = ((), (), s32[]{:S(2)}) async-start(), calls=%async_computation.16 | async-start | bytes 2621440 | tf_op jit(solution)/shard_map/all_gather | solution.py:317
  303.2 59.4 %all-to-all-start.2 = ((bf16[8,144,2048]{2,1,0:T(8,128)(2,1)}), bf16[8,144,2048]{2,1,0:T(8,128)(2,1)}, u32[]{:S(2)}, u32[]{:S(2)}) async-start(bf16[8,144,2048]{2,1,0:T(8,128)(2,1)} %bitcast.235), calls=%async_computation.3 | async-start | bytes 9437184 | tf_op jit(solution)/shard_map/all_to_all | solution.py:283
  307.8 203.6 %reduce-scatter.12.cloned.1.call-start = ((), (), s32[]{:S(2)}) async-start(), calls=%async_computation.18 | async-start | bytes 2785280 | tf_op jit(solution)/shard_map/reduce_scatter | solution.py:293
  366.7 11.4 %copy-start.78 = (pred[32]{0:T(512)(128)(4,1)S(1)}, pred[32]{0:T(512)(128)(4,1)}, u32[]{:S(2)}) copy-start(pred[32]{0:T(512)(128)(4,1)} %iota_compare_fusion.9) | copy-start | bytes 100
  366.7 28.1 %slice-start.2 = ((s8[6291456]{0:T(1024)(128)(4,1)}), s8[4194304]{0:T(1024)(128)(4,1)S(1)}, s32[]{:S(2)}) async-start(s8[6291456]{0:T(1024)(128)(4,1)} %bitcast.248), calls=%async_computation.28 | async-start | bytes 8388608
  378.2 7.3 copy-start.59
  378.2 16.6 %slice-start.3 = ((s8[6291456]{0:T(1024)(128)(4,1)}), s8[2097152]{0:T(1024)(128)(4,1)S(1)}, s32[]{:S(2)}) async-start(s8[6291456]{0:T(1024)(128)(4,1)} %bitcast.248), calls=%async_computation.29 | async-start | bytes 4194304
  385.5 9.3 copy-start.85
  385.5 9.3 copy-start.88
  385.5 9.3 copy-start.90
  394.8 7.8 copy-start.76
  394.8 7.8 copy-start.77
  403.5 60.3 %copy-start.44 = (s32[8,512]{1,0:T(8,128)S(1)}, s32[8,512]{1,0:T(8,128)}, u32[]{:S(2)}) copy-start(s32[8,512]{1,0:T(8,128)} %copy-done.43) | copy-start | bytes 49156
  463.8 5.5 copy-start.10
  463.8 5.5 copy-start.15
  468.4 44.5 %copy-start.4 = (bf16[1,128,2048]{2,1,0:T(8,128)(2,1)S(1)}, bf16[1,128,2048]{2,1,0:T(8,128)(2,1)}, u32[]{:S(2)}) copy-start(bf16[1,128,2048]{2,1,0:T(8,128)(2,1)} %param.12) | copy-start | bytes 1572868
  468.4 44.5 %copy-start.9 = (bf16[128,2048]{1,0:T(8,128)(2,1)S(1)}, bf16[128,2048]{1,0:T(8,128)(2,1)}, u32[]{:S(2)}) copy-start(bf16[128,2048]{1,0:T(8,128)(2,1)} %reduce-scatter.8.cloned.1.call-done) | copy-start | bytes 1572868
  468.4 94.9 %all-gather.16.cloned.1.call-start = ((), (), s32[]{:S(2)}) async-start(), calls=%async_computation.19 | async-start | bytes 2621440 | tf_op jit(solution)/shard_map/all_gather | solution.py:376
  469.4 43.2 %copy-start.36 = (pred[128,32]{1,0:T(32,128)(4,1)}, pred[128,32]{1,0:T(32,128)(4,1)S(1)}, u32[]{:S(2)}) copy-start(pred[128,32]{1,0:T(32,128)(4,1)S(1)} %broadcast_compare_fusion) | copy-start | bytes 12292
  469.8 42.8 %copy-start.33 = (f32[128,32]{1,0:T(8,128)}, f32[128,32]{1,0:T(8,128)S(1)}, u32[]{:S(2)}) copy-start(f32[128,32]{1,0:T(8,128)S(1)} %get-tuple-element.523) | copy-start | bytes 49156
  469.8 42.8 %copy-start.54 = (f32[128]{0:T(128)}, f32[128]{0:T(128)S(1)}, u32[]{:S(2)}) copy-start(f32[128]{0:T(128)S(1)} %get-tuple-element.522) | copy-start | bytes 1540
  469.8 46.0 %copy-start.13 = (bf16[1,128,2048]{2,1,0:T(8,128)(2,1)S(1)}, bf16[1,128,2048]{2,1,0:T(8,128)(2,1)}, u32[]{:S(2)}) copy-start(bf16[1,128,2048]{2,1,0:T(8,128)(2,1)} %param.23) | copy-start | bytes 1572868
  470.0 42.6 %copy-start.69 = (f32[128]{0:T(128)}, f32[128]{0:T(128)S(1)}, u32[]{:S(2)}) copy-start(f32[128]{0:T(128)S(1)} %compare_select_fusion.1) | copy-start | bytes 1540
  515.1 54.4 %copy-start.16 = (f32[128,2048]{1,0:T(8,128)}, f32[128,2048]{1,0:T(8,128)S(1)}, u32[]{:S(2)}) copy-start(f32[128,2048]{1,0:T(8,128)S(1)} %get-tuple-element.524) | copy-start | bytes 3145732
  515.8 47.5 %copy-start.67 = (f32[128]{0:T(128)}, f32[128]{0:T(128)S(1)}, u32[]{:S(2)}) copy-start(f32[128]{0:T(128)S(1)} %multiply_multiply_fusion.3) | copy-start | bytes 1540
  517.8 155.4 %reduce-scatter.14.cloned.1.call-start = ((), (), s32[]{:S(2)}) async-start(), calls=%async_computation.20 | async-start | bytes 2621440 | tf_op jit(solution)/shard_map/reduce_scatter | solution.py:399
  581.4 5.3 copy-start.22
  581.4 5.3 copy-start.24
  586.8 9.2 copy-start.87
  588.5 7.5 slice-start
  590.4 5.6 slice-start.1
  600.2 105.8 %reduce-scatter.18.cloned.1.call-start = ((), (), s32[]{:S(2)}) async-start(), calls=%async_computation.22 | async-start | bytes 5898240 | tf_op jit(solution)/shard_map/reduce_scatter | solution.py:409
  608.3 150.0 %reduce-scatter.10.cloned.1.call-start = ((), (), s32[]{:S(2)}) async-start(), calls=%async_computation.17 | async-start | bytes 2621440 | tf_op jit(solution)/shard_map/reduce_scatter | solution.py:293
  608.3 58.3 %copy-start.45 = (s32[8,512]{1,0:T(8,128)S(1)}, s32[8,512]{1,0:T(8,128)}, u32[]{:S(2)}) copy-start(s32[8,512]{1,0:T(8,128)} %copy-done.43) | copy-start | bytes 49156
  670.9 224.6 %reduce-scatter.16.cloned.1.call-start = ((), (), s32[]{:S(2)}) async-start(), calls=%async_computation.21 | async-start | bytes 540672 | tf_op jit(solution)/shard_map/reduce_scatter | solution.py:445
  676.1 270.5 %reduce-scatter.20.cloned.1.call-start = ((), (), s32[]{:S(2)}) async-start(), calls=%async_computation.23 | async-start | bytes 4718592 | tf_op jit(solution)/shard_map/reduce_scatter | solution.py:378
  683.7 9.0 copy-start.89
  683.7 9.0 copy-start.91
  692.7 65.5 %copy-start.14 = (bf16[1,128,2048]{2,1,0:T(8,128)(2,1)S(1)}, bf16[1,128,2048]{2,1,0:T(8,128)(2,1)}, u32[]{:S(2)}) copy-start(bf16[1,128,2048]{2,1,0:T(8,128)(2,1)} %param.23) | copy-start | bytes 1572868
  692.7 65.5 %copy-start.17 = (f32[128,2048]{1,0:T(8,128)S(1)}, f32[128,2048]{1,0:T(8,128)}, u32[]{:S(2)}) copy-start(f32[128,2048]{1,0:T(8,128)} %copy-done.16) | copy-start | bytes 3145732
  692.7 65.5 %copy-start.25 = (bf16[128,2048]{1,0:T(8,128)(2,1)S(1)}, bf16[128,2048]{1,0:T(8,128)(2,1)}, u32[]{:S(2)}) copy-start(bf16[128,2048]{1,0:T(8,128)(2,1)} %reduce-scatter.14.cloned.1.call-done) | copy-start | bytes 1572868
  692.7 65.5 %copy-start.40 = (f32[2048]{0:T(1024)S(1)}, f32[2048]{0:T(1024)}, u32[]{:S(2)}) copy-start(f32[2048]{0:T(1024)} %reshape.590) | copy-start | bytes 24580
  692.7 65.5 %copy-start.64 = (f32[128]{0:T(128)S(1)}, f32[128]{0:T(128)}, u32[]{:S(2)}) copy-start(f32[128]{0:T(128)} %copy-done.63) | copy-start | bytes 1540
  692.8 65.5 %copy-start.68 = (f32[128]{0:T(128)S(1)}, f32[128]{0:T(128)}, u32[]{:S(2)}) copy-start(f32[128]{0:T(128)} %copy-done.67) | copy-start | bytes 1540
  706.0 242.7 %all-to-all-start.5 = ((bf16[4,64,1280]{2,1,0:T(8,128)(2,1)}), bf16[4,64,1280]{2,1,0:T(8,128)(2,1)}, u32[]{:S(2)}, u32[]{:S(2)}) async-start(bf16[4,64,1280]{2,1,0:T(8,128)(2,1)} %bitcast.240), calls=%async_computation.11 | async-start | bytes 1310720 | tf_op jit(solution)/shard_map/all_to_all | solution.py:410
  (48 other events, 126.5 us)
Sparse Core Ops, SparseCore 0:
  9.6 63.1 all-gather.17
  75.2 40.2 all-gather.9
  117.4 36.6 all-gather.11
  155.4 46.1 all-gather.19
  203.7 42.6 reduce-scatter.7
  251.3 45.2 all-gather.13
  468.5 42.8 reduce-scatter.11
  517.9 45.3 all-gather.15
  600.4 42.5 reduce-scatter.13
  646.2 55.8 reduce-scatter.17
  704.5 53.6 reduce-scatter.9
  760.9 134.5 reduce-scatter.15
  899.2 47.2 reduce-scatter.19

commit v2 on v1

--- a/solution.py
+++ b/solution.py
@@ -1,7 +1,11 @@
+import functools
 import jax
 import jax.numpy as jnp
 from jax import lax
+from jax.experimental import pallas as pl
+from jax.experimental.pallas import tpu as pltpu
 from jax.sharding import PartitionSpec as P
+
 
 MODEL_WIDTH = 2048
 QUERY_HEADS = 32
@@ -15,6 +19,438 @@
 ROPE_BASE = 1000000.0
 FILLER = -1e30
 QUERY_BLOCK = 512
+
+
+MESH = pl.DeviceIdType.MESH
+VMEM_BYTES = 62 * 1024 * 1024
+
+
+def dot_nn(left, right):
+    return jnp.dot(left, right, preferred_element_type=jnp.float32)
+
+
+def dot_nt(left, right):
+    return lax.dot_general(
+        left, right, (((1,), (1,)), ((), ())), preferred_element_type=jnp.float32
+    )
+
+
+def dot_tn(left, right):
+    return lax.dot_general(
+        left, right, (((0,), (0,)), ((), ())), preferred_element_type=jnp.float32
+    )
+
+
+def greet(peers):
+    barrier = pltpu.get_barrier_semaphore()
+    for peer in peers:
+        pl.semaphore_signal(barrier, inc=1, device_id=peer, device_id_type=MESH)
+    pl.semaphore_wait(barrier, len(peers))
+
+
+def remote(source, target, send_sem, recv_sem, device):
+    return pltpu.make_async_remote_copy(
+        src_ref=source,
+        dst_ref=target,
+        send_sem=send_sem,
+        recv_sem=recv_sem,
+        device_id=device,
+        device_id_type=MESH,
+    )
+
+
+def line_gather_step(step, count, place, column, blocks, send_sems, recv_sems):
+    right, left = place + 1, place - 1
+    if step > 0:
+
+        @pl.when(place - step >= 0)
+        def _():
+            block = blocks.at[place - step]
+            remote(block, block, send_sems.at[0, step], recv_sems.at[0, step], (right, column)).wait_recv()
+
+        @pl.when(place + step < count)
+        def _():
+            block = blocks.at[place + step]
+            remote(block, block, send_sems.at[1, step], recv_sems.at[1, step], (left, column)).wait_recv()
+
+    if step < count - 1:
+
+        @pl.when((place - step >= 0) & (place + 1 < count))
+        def _():
+            block = blocks.at[place - step]
+            remote(block, block, send_sems.at[0, step], recv_sems.at[0, step + 1], (right, column)).start()
+
+        @pl.when((place + step < count) & (place - 1 >= 0))
+        def _():
+            block = blocks.at[place + step]
+            remote(block, block, send_sems.at[1, step], recv_sems.at[1, step + 1], (left, column)).start()
+
+
+def line_gather_end(count, place, column, blocks, send_sems, recv_sems):
+    for step in range(count - 1):
+
+        @pl.when((place - step >= 0) & (place + 1 < count))
+        def _():
+            block = blocks.at[place - step]
+            remote(block, block, send_sems.at[0, step], recv_sems.at[0, step], (place + 1, column)).wait_send()
+
+        @pl.when((place + step < count) & (place - 1 >= 0))
+        def _():
+            block = blocks.at[place + step]
+            remote(block, block, send_sems.at[1, step], recv_sems.at[1, step], (place - 1, column)).wait_send()
+
+
+def line_sum_step(step, count, place, column, own, sums, send_sems, recv_sems):
+    turn = step - place
+    last = count - 1 - turn
+
+    @pl.when((turn >= 0) & (last > place))
+    def _():
+        block = sums.at[0, last]
+
+        @pl.when(place > 0)
+        def _():
+            remote(block, block, send_sems.at[0, last], recv_sems.at[0, last], (place, column)).wait_recv()
+            sums[0, last] = (
+                sums[0, last].astype(jnp.float32) + own[last].astype(jnp.float32)
+            ).astype(jnp.bfloat16)
+
+        @pl.when(place == 0)
+        def _():
+            sums[0, last] = own[last]
+
+        remote(block, block, send_sems.at[0, last], recv_sems.at[0, last], (place + 1, column)).start()
+
+    first = step - (count - 1 - place)
+
+    @pl.when((first >= 0) & (first < place))
+    def _():
+        block = sums.at[1, first]
+
+        @pl.when(place < count - 1)
+        def _():
+            remote(block, block, send_sems.at[1, first], recv_sems.at[1, first], (place, column)).wait_recv()
+            sums[1, first] = (
+                sums[1, first].astype(jnp.float32) + own[first].astype(jnp.float32)
+            ).astype(jnp.bfloat16)
+
+        @pl.when(place == count - 1)
+        def _():
+            sums[1, first] = own[first]
+
+        remote(block, block, send_sems.at[1, first], recv_sems.at[1, first], (place - 1, column)).start()
+
+
+def line_sum_end(count, place, column, own, sums, send_sems, recv_sems, total):
+    total[...] = own[place].astype(jnp.float32)
+
+    @pl.when(place > 0)
+    def _():
+        block = sums.at[0, place]
+        remote(block, block, send_sems.at[0, place], recv_sems.at[0, place], (place, column)).wait_recv()
+        total[...] += sums[0, place].astype(jnp.float32)
+
+    @pl.when(place < count - 1)
+    def _():
+        block = sums.at[1, place]
+        remote(block, block, send_sems.at[1, place], recv_sems.at[1, place], (place, column)).wait_recv()
+        total[...] += sums[1, place].astype(jnp.float32)
+
+    for step in range(count - 1):
+        last = count - 1 - step
+
+        @pl.when(last > place)
+        def _():
+            block = sums.at[0, last]
+            remote(block, block, send_sems.at[0, last], recv_sems.at[0, last], (place + 1, column)).wait_send()
+
+        @pl.when(step < place)
+        def _():
+            block = sums.at[1, step]
+            remote(block, block, send_sems.at[1, step], recv_sems.at[1, step], (place - 1, column)).wait_send()
+
+
+def backward_kernel(
+    count, planes, tokens, heads, shard,
+    branch_ref, out_rows_hbm, own_cols_hbm, normed_hbm, heads_hbm, query_hbm, pair_hbm,
+    proj_hbm, lse_ref, turn_cos_ref, turn_sin_ref, gain_ref,
+    normed_total, out_total, columns_out, gain_total,
+    out_rows, own_cols, normed, heads_low, queries, pair, proj, local_sems,
+    branch_full, ag_send, ag_recv,
+    grad_heads, grad_proj, grad_pair,
+    grad_out, out_pair, out_far, out_sems,
+    grad_cols, col_pair, col_far, col_sums, col_sems,
+    normed_part, normed_sums, rs_send, rs_recv, z_sems,
+):
+    place = lax.axis_index("seq")
+    member = lax.axis_index("dp")
+    core = lax.rem(member, 2)
+    chip = member // 2
+    chips = planes // 2
+    partner = member + 1 - 2 * core
+    length = count * tokens
+    query_columns = heads * HEAD_SIZE
+    out_block = query_columns // planes
+    scale = HEAD_SIZE ** (-0.5)
+
+    loads = [
+        pltpu.make_async_copy(source, target, local_sems.at[index])
+        for index, (source, target) in enumerate(
+            [
+                (out_rows_hbm, out_rows),
+                (query_hbm, queries),
+                (pair_hbm, pair),
+                (heads_hbm, heads_low),
+                (proj_hbm, proj),
+                (own_cols_hbm, own_cols),
+                (normed_hbm, normed),
+            ]
+        )
+    ]
+    for load in loads:
+        load.start()
+    branch_full[place] = branch_ref[...]
+
+    far_chips = [lax.rem(chip + k, chips) for k in range(1, chips)]
+    far_places = [lax.rem(place + k, count) for k in range(1, count)]
+    greet(
+        [(place, partner)]
+        + [(place, 2 * other + core) for other in far_chips]
+        + [(other, member) for other in far_places]
+    )
+
+    line = (count, place, member, branch_full, ag_send, ag_recv)
+    line_gather_step(0, *line)
+    for load in loads:
+        load.wait()
+
+    def head_gradients(block):
+        partial_heads = dot_nt(branch_full[block], out_rows[...]).astype(jnp.bfloat16)
+        for head in range(heads):
+            grad_heads[head, pl.ds(pl.multiple_of(block * tokens, tokens), tokens), :] = (
+                partial_heads[:, head * HEAD_SIZE : (head + 1) * HEAD_SIZE]
+            )
+
+    head_gradients(place)
+    for step in range(1, count):
+        line_gather_step(step, *line)
+
+        @pl.when(place - step >= 0)
+        def _():
+            head_gradients(place - step)
+
+        @pl.when(place + step < count)
+        def _():
+            head_gradients(place + step)
+
+    def out_copy(target, k):
+        rows = grad_out.at[2 * k + 1 - core]
+        return remote(rows, out_pair.at[k], out_sems.at[0, k], out_sems.at[1, k], (place, partner))
+
+    def out_gradient(block):
+        all_branch = branch_full[...].reshape(length, MODEL_WIDTH)
+        columns = heads_low[block]
+        grad_out[block] = dot_tn(columns, all_branch).astype(jnp.bfloat16)
+
+    for k in range(chips):
+        out_gradient(2 * k + 1 - core)
+        out_copy(None, k).start()
+    for k in range(chips):
+        out_gradient(2 * k + core)
+
+    def out_far_copy(k):
+        other = lax.rem(chip + k, chips)
+        return remote(
+            out_pair.at[other], out_far.at[k - 1], out_sems.at[2, k], out_sems.at[3, k],
+            (place, 2 * other + core),
+        )
+
+    for k in range(chips):
+        out_copy(None, k).wait_recv()
+        out_pair[k] = (
+            out_pair[k].astype(jnp.float32) + grad_out[2 * k + core].astype(jnp.float32)
+        ).astype(jnp.bfloat16)
+    for k in range(1, chips):
+        out_far_copy(k).start()
+
+    grad_pair[...] = jnp.zeros_like(grad_pair)
+    gain_total[...] = jnp.zeros_like(gain_total)
+    block_rows = min(256, length)
+
+    def unprepare(grad, raw, gain):
+        turned = grad * turn_cos_ref[...] + pltpu.roll(grad, HEAD_SIZE // 2, 1) * turn_sin_ref[...]
+        inverse = lax.rsqrt(jnp.mean(raw * raw, axis=-1, keepdims=True) + EPSILON)
+        unit = raw * inverse
+        gain_part = jnp.sum(turned * unit, axis=0, keepdims=True)
+        turned = turned * gain
+        middle = jnp.mean(turned * unit, axis=-1, keepdims=True)
+        return inverse * (turned - unit * middle), gain_part
+
+    def one_head(head, carry):
+        lse = lse_ref[head]
+        grads = []
+        for block in range(length // block_rows):
+            low, high = block * block_rows, (block + 1) * block_rows
+            query = queries[head, low:high, :]
+            grad = grad_heads[head, low:high, :]
+            key = pair[0, :high, :]
+            scores = dot_nt(key, query) * scale
+            row_ids = lax.broadcasted_iota(jnp.int32, (high, block_rows), 0)
+            col_ids = lax.broadcasted_iota(jnp.int32, (high, block_rows), 1) + low
+            scores = jnp.where(row_ids <= col_ids, scores, FILLER)
+            probs = jnp.exp(scores - lse[:, low:high])
+            grad_probs = dot_nt(pair[1, :high, :], grad)
+            delta = jnp.sum(probs * grad_probs, axis=0, keepdims=True)
+            grad_scores = (probs * (grad_probs - delta)).astype(jnp.bfloat16)
+            grad_pair[0, :high, :] += dot_nn(grad_scores, query) * scale
+            grad_pair[1, :high, :] += dot_nn(probs.astype(jnp.bfloat16), grad)
+            grads.append(dot_tn(grad_scores, key) * scale)
+        grad_query = jnp.concatenate(grads, axis=0)
+        grad_raw, gain_part = unprepare(grad_query, proj[head], gain_ref[0:1, :])
+        gain_total[0:1, :] += gain_part
+        grad_proj[head] = grad_raw.astype(jnp.bfloat16)
+        return carry
+
+    lax.fori_loop(0, heads, one_head, 0)
+    grad_raw, gain_part = unprepare(grad_pair[0], proj[heads], gain_ref[1:2, :])
+    gain_total[1:2, :] += gain_part
+    grad_proj[heads] = grad_raw.astype(jnp.bfloat16)
+    grad_proj[heads + 1] = grad_pair[1].astype(jnp.bfloat16)
+    grad_rows = jnp.concatenate([grad_proj[head] for head in range(heads + 2)], axis=1)
+
+    for block in range(count):
+        normed_part[block] = dot_nt(
+            grad_rows[block * tokens : (block + 1) * tokens, :], own_cols[...]
+        ).astype(jnp.bfloat16)
+    sums = (count, place, member, normed_part, normed_sums, rs_send, rs_recv)
+    line_sum_step(0, *sums)
+
+    for block in range(count):
+        width = planes * shard
+        part = dot_tn(normed[:, block * width : (block + 1) * width], grad_rows).astype(jnp.bfloat16)
+        grad_cols[block] = part.reshape(planes, shard, part.shape[-1])
+
+    def col_copy(k):
+        rows = grad_cols.at[:, 2 * k + 1 - core]
+        return remote(rows, col_pair.at[k], col_sems.at[0, k], col_sems.at[1, k], (place, partner))
+
+    def col_far_copy(k):
+        other = lax.rem(chip + k, chips)
+        return remote(
+            col_pair.at[other], col_far.at[k - 1], col_sems.at[2, k], col_sems.at[3, k],
+            (place, 2 * other + core),
+        )
+
+    for k in range(chips):
+        col_copy(k).start()
+    for k in range(chips):
+        col_copy(k).wait_recv()
+        col_pair[k] = (
+            col_pair[k].astype(jnp.float32) + grad_cols[:, 2 * k + core].astype(jnp.float32)
+        ).astype(jnp.bfloat16)
+    for k in range(1, chips):
+        col_far_copy(k).start()
+
+    if count > 2:
+        line_sum_step(1, *sums)
+
+    total = out_pair[chip].astype(jnp.float32)
+    for k in range(1, chips):
+        out_far_copy(k).wait_recv()
+        total += out_far[k - 1].astype(jnp.float32)
+    out_total[...] = total
+
+    for step in range(2, count - 1):
+        line_sum_step(step, *sums)
+
+    columns = col_pair[chip].astype(jnp.float32)
+    for k in range(1, chips):
+        col_far_copy(k).wait_recv()
+        columns += col_far[k - 1].astype(jnp.float32)
+    col_sums[...] = columns.astype(jnp.bfloat16)
+
+    def z_copy(k):
+        other = lax.rem(place + k, count)
+        return remote(
+            col_sums.at[other], columns_out.at[place], z_sems.at[0, k], z_sems.at[1, k], (other, member)
+        )
+
+    for k in range(1, count):
+        z_copy(k).start()
+    columns_out[place] = col_sums[place]
+
+    line_sum_end(*sums, normed_total)
+    for k in range(1, count):
+        z_copy(k).wait_recv()
+    for k in range(1, count):
+        z_copy(k).wait_send()
+    for k in range(chips):
+        out_copy(None, k).wait_send()
+        col_copy(k).wait_send()
+    for k in range(1, chips):
+        out_far_copy(k).wait_send()
+        col_far_copy(k).wait_send()
+    line_gather_end(*line)
+
+
+def attention_backward(
+    count, planes, heads, shard, branch, out_rows, own_cols, normed, heads_low, queries, pair, proj,
+    lse, turn_cos, turn_sin, gains,
+):
+    tokens = branch.shape[0]
+    length = count * tokens
+    width = (heads + 2) * HEAD_SIZE
+    chips = planes // 2
+    out_block = heads * HEAD_SIZE // planes
+    low = jnp.bfloat16
+    vmem = pl.BlockSpec(memory_space=pltpu.VMEM)
+    anywhere = pl.BlockSpec(memory_space=pl.ANY)
+    dma = pltpu.SemaphoreType.DMA
+    return pl.pallas_call(
+        functools.partial(backward_kernel, count, planes, tokens, heads, shard),
+        out_shape=(
+            jax.ShapeDtypeStruct((tokens, MODEL_WIDTH), jnp.float32),
+            jax.ShapeDtypeStruct((out_block, MODEL_WIDTH), jnp.float32),
+            jax.ShapeDtypeStruct((count, shard, width), low),
+            jax.ShapeDtypeStruct((8, HEAD_SIZE), jnp.float32),
+        ),
+        in_specs=[vmem] + [anywhere] * 7 + [vmem] * 4,
+        out_specs=(vmem,) * 4,
+        scratch_shapes=[
+            pltpu.VMEM(out_rows.shape, low),
+            pltpu.VMEM(own_cols.shape, low),
+            pltpu.VMEM(normed.shape, low),
+            pltpu.VMEM(heads_low.shape, low),
+            pltpu.VMEM(queries.shape, low),
+            pltpu.VMEM(pair.shape, low),
+            pltpu.VMEM(proj.shape, jnp.float32),
+            dma((7,)),
+            pltpu.VMEM((count, tokens, MODEL_WIDTH), low),
+            dma((2, count)),
+            dma((2, count)),
+            pltpu.VMEM((heads, length, HEAD_SIZE), low),
+            pltpu.VMEM((heads + 2, length, HEAD_SIZE), low),
+            pltpu.VMEM((2, length, HEAD_SIZE), jnp.float32),
+            pltpu.VMEM((planes, out_block, MODEL_WIDTH), low),
+            pltpu.VMEM((chips, out_block, MODEL_WIDTH), low),
+            pltpu.VMEM((chips - 1, out_block, MODEL_WIDTH), low),
+            dma((4, chips)),
+            pltpu.VMEM((count, planes, shard, width), low),
+            pltpu.VMEM((chips, count, shard, width), low),
+            pltpu.VMEM((chips - 1, count, shard, width), low),
+            pltpu.VMEM((count, shard, width), low),
+            dma((4, chips)),
+            pltpu.VMEM((count, tokens, MODEL_WIDTH), low),
+            pltpu.VMEM((2, count, tokens, MODEL_WIDTH), low),
+            dma((2, count)),
+            dma((2, count)),
+            dma((2, count)),
+        ],
+        compiler_params=pltpu.CompilerParams(
+            collective_id=3, has_side_effects=True, vmem_limit_bytes=VMEM_BYTES
+        ),
+        name="attention_backward",
+    )(branch, out_rows, own_cols, normed, heads_low, queries, pair, proj, lse, turn_cos, turn_sin, gains)
 
 
 def rms_norm(values, gain):
@@ -126,59 +562,6 @@
 
     outputs, log_totals = lax.map(one_block, jnp.arange(block_count))
     return (outputs.reshape(sequence_length, head_count, HEAD_SIZE), log_totals)
-
-
-def attend_backward(queries, keys_in, values_in, out_full, log_totals, grad_heads):
-    sequence_length, head_count = (queries.shape[0], queries.shape[1])
-    block_rows = min(QUERY_BLOCK, sequence_length)
-    block_count = sequence_length // block_rows
-    row_dots = jnp.sum(grad_heads.astype(jnp.float32) * out_full, axis=-1)
-
-    def one_block(carry, i):
-        query_block = block_slice(queries, i, block_rows)
-        grad_block = block_slice(grad_heads, i, block_rows)
-        dot_block = block_slice(row_dots, i, block_rows).T
-        block_totals = log_totals[i]
-
-        def step(j, inner):
-            grad_query, grad_keys, grad_values = inner
-            key_block = block_slice(keys_in, j, block_rows)
-            value_block = block_slice(values_in, j, block_rows)
-            scores = block_scores(query_block, key_block, i, j, block_rows)
-            probabilities = jnp.exp(scores - block_totals[..., None])
-            grad_probs = jnp.einsum(
-                "qhd,kd->hqk", grad_block, value_block, preferred_element_type=jnp.float32
-            )
-            grad_scores = (probabilities * (grad_probs - dot_block[..., None])).astype(jnp.bfloat16)
-            grad_query = grad_query + jnp.einsum(
-                "hqk,kd->qhd", grad_scores, key_block, preferred_element_type=jnp.float32
-            ) * HEAD_SIZE ** (-0.5)
-            key_part = jnp.einsum(
-                "hqk,qhd->kd", grad_scores, query_block, preferred_element_type=jnp.float32
-            ) * HEAD_SIZE ** (-0.5)
-            value_part = jnp.einsum(
-                "hqk,qhd->kd",
-                probabilities.astype(jnp.bfloat16),
-                grad_block,
-                preferred_element_type=jnp.float32,
-            )
-            grad_keys = lax.dynamic_update_slice_in_dim(
-                grad_keys, block_slice(grad_keys, j, block_rows) + key_part, j * block_rows, 0
-            )
-            grad_values = lax.dynamic_update_slice_in_dim(
-                grad_values, block_slice(grad_values, j, block_rows) + value_part, j * block_rows, 0
-            )
-            return (grad_query, grad_keys, grad_values)
-
-        start = (jnp.zeros((block_rows, head_count, HEAD_SIZE), jnp.float32), carry[0], carry[1])
-        grad_query, grad_keys, grad_values = lax.fori_loop(0, i + 1, step, start)
-        return ((grad_keys, grad_values), grad_query)
-
-    empty = jnp.zeros((sequence_length, HEAD_SIZE), jnp.float32)
-    (grad_keys, grad_values), grad_query = lax.scan(
-        one_block, (empty, empty), jnp.arange(block_count)
-    )
-    return (grad_query.reshape(sequence_length, head_count, HEAD_SIZE), grad_keys, grad_values)
 
 
 def masked_softmax(logits, mask):
@@ -373,47 +756,31 @@
     grad_hidden_norm, grad_gain_two = pull_two(grad_mixed)
     grad_hidden1 = grad_result + grad_hidden_norm
     grad_branch = grad_hidden1.astype(jnp.bfloat16)
-    branch_full = lax.all_gather(grad_branch, "seq", axis=0, tiled=True)
-    grad_out_rows = inner_rows(heads_low, branch_full)
-    shard_out = lax.psum_scatter(
-        grad_out_rows.astype(jnp.bfloat16), "dp", scatter_dimension=0, tiled=True
-    ).astype(jnp.float32)
-    grad_heads = (
-        outer_cols(branch_full, out_rows)
-        .astype(jnp.bfloat16)
-        .reshape(sequence_length, per_device, HEAD_SIZE)
-    )
-    grad_query, grad_keys, grad_values = attend_backward(
-        query_heads, key_heads, value_heads, out_full, log_totals, grad_heads
-    )
-    _, pull_prep = jax.vjp(
-        lambda proj_in, query_in, key_in: prepare_heads(
-            proj_in, query_in, key_in, cosine, sine_table
+    normed_total, shard_out, column_sums, gain_totals = attention_backward(
+        sequence_number,
+        planes,
+        per_device,
+        shard,
+        grad_branch,
+        out_rows,
+        own_cols,
+        normed_full,
+        jnp.transpose(
+            heads_low.reshape(sequence_length, planes, query_columns // planes), (1, 0, 2)
         ),
-        projected_rows,
-        gain_query,
-        gain_key,
-    )
-    grad_projected, grad_gain_query, grad_gain_key = pull_prep((grad_query, grad_keys, grad_values))
-    grad_proj_low = grad_projected.astype(jnp.bfloat16)
-    grad_normed = lax.psum_scatter(
-        outer_cols(grad_proj_low, own_cols).astype(jnp.bfloat16),
-        "seq",
-        scatter_dimension=0,
-        tiled=True,
-    ).astype(jnp.float32)
-    gradient_columns = inner_rows(normed_full, grad_proj_low).astype(jnp.bfloat16)
-    gradient_columns = jnp.transpose(
-        gradient_columns.reshape(sequence_number, planes, shard, own_width), (1, 0, 2, 3)
-    ).reshape(MODEL_WIDTH, own_width)
-    column_sums = lax.psum_scatter(gradient_columns, "dp", scatter_dimension=0, tiled=True)
-    column_sums = lax.all_to_all(
-        column_sums.reshape(sequence_number, shard, own_width),
-        "seq",
-        split_axis=0,
-        concat_axis=0,
-        tiled=True,
-    ).astype(jnp.float32)
+        jnp.transpose(query_heads, (1, 0, 2)),
+        jnp.stack([key_heads, value_heads]),
+        jnp.transpose(
+            projected_rows.reshape(sequence_length, per_device + 2, HEAD_SIZE), (1, 0, 2)
+        ),
+        log_totals.reshape(-1, per_device, sequence_length // log_totals.shape[0])
+        .transpose(1, 0, 2)
+        .reshape(per_device, 1, sequence_length),
+        jnp.concatenate([cosine, cosine], axis=1),
+        jnp.concatenate([sine_table, -sine_table], axis=1),
+        jnp.pad(jnp.stack([gain_query, gain_key]), ((0, 6), (0, 0))),
+    )
+    column_sums = column_sums.astype(jnp.float32)
     shard_query = jnp.transpose(column_sums[:, :, :query_columns], (1, 0, 2)).reshape(
         shard, QUERY_HEADS * HEAD_SIZE
     )
@@ -428,15 +795,15 @@
     )
     shard_qkv = jnp.concatenate([shard_query, shard_paired], axis=1)
     _, pull_one = jax.vjp(rms_norm, residual, gain_one)
-    grad_residual_norm, grad_gain_one = pull_one(grad_normed)
+    grad_residual_norm, grad_gain_one = pull_one(normed_total)
     grad_input = grad_hidden1 + grad_residual_norm
 
     small = jnp.concatenate(
         [
             grad_gain_one.reshape(devices, shard),
             grad_gain_two.reshape(devices, shard),
-            grad_gain_query.reshape(devices, small_shard),
-            grad_gain_key.reshape(devices, small_shard),
+            gain_totals[0].reshape(devices, small_shard),
+            gain_totals[1].reshape(devices, small_shard),
             grad_router_w.reshape(devices, shard * devices),
         ],
         axis=1,

time: 968 us -> 853 us (0.88)
  waiting for transfers between devices: 472 us -> 346 us
  Pallas kernels: 0 us -> 124 us
  blocking collectives: 218 us -> 155 us
  matrix products: 139 us -> 113 us
  other arithmetic: 50.5 us -> 35.6 us
    pallas_call x0 -> x1, Pallas kernels: none -> 124 us  [attention_backward(): pl.pallas_call(functools.partial(backward_kernel, count, planes, tokens,...]
    reduce_scatter x2, waiting for transfers between devices: 89.5 us -> 0.01 us  [combine(): lax.psum_scatter(sums, 'seq', scatter_dimension=0, tiled=True)]
    all_to_all x2 -> x1, blocking collectives: 119 us -> 61.1 us  [combine(): lax.all_to_all(rows.reshape(planes, slots, width), 'dp', split_axis=0, co...]
    reduce_scatter x3 -> x0, waiting for transfers between devices: 46.9 us -> none  [the longest x1 46.8 us: body(): lax.psum_scatter(grad_out_rows.astype(jnp.bfloat16), 'dp', scatter_dimens...]
    all_gather x1 -> x0, waiting for transfers between devices: 45.5 us -> none  [body(): branch_full = lax.all_gather(grad_branch, 'seq', axis=0, tiled=True)]
    all_to_all x1, waiting for transfers between devices: 0.01 us -> 33.6 us  [combine(): lax.all_to_all(rows.reshape(planes, slots, width), 'dp', split_axis=0, co...]
    dot_general x4 -> x0, matrix products: 12.9 us -> none  [the longest x1 5.32 us: step(): jnp.einsum('hqk,qhd->kd', probabilities.astype(jnp.bfloat16), grad_block,...]
    dot_general x5 -> x3, matrix products: 27.6 us -> 17 us  [outer_cols(): lax.dot_general(left, right, (((1,), (1,)), ((), ())), preferred_element_...]
  transfers between devices with their start and end apart: 16 -> 12, of which waited for: 11 -> 8; matrix products, arithmetic and copies ran while one was open for 15% -> 17% of each run, Pallas kernels for 0% -> 15%
where the time goes in v2:
time: 853 us; the launch traced here: 846 us
  waiting for transfers between devices  346 us (41%)
  blocking collectives  155 us (18%)
  Pallas kernels  124 us (15%)
  matrix products  113 us (13%)
  local copies, waits for them, and re-layouts  42.9 us (5%)
  other arithmetic  35.6 us (4%)
  between operations  15.2 us (2%)
  starting transfers between devices  14.7 us (2%)
    reduce_scatter x1, waiting for transfers between devices, body(): lax.psum_scatter(small.reshape(devices * small_rows, 128), ('seq', 'dp'),...  132 us
    pallas_call x1, Pallas kernels, attention_backward(): pl.pallas_call(functools.partial(backward_kernel, count, planes, tokens,...  124 us
    all_to_all x1, blocking collectives, combine(): lax.all_to_all(rows.reshape(planes, slots, width), 'dp', split_axis=0, co...  61.1 us
    all_to_all x2, waiting for transfers between devices, dispatch(): lax.all_to_all(sent.reshape(planes, slots, rows.shape[-1]), 'dp', split_a...  50.6 us
    all_gather x1, waiting for transfers between devices, body(): mixed_full = lax.all_gather(mixed_low, 'seq', axis=0, tiled=True)  45.4 us
    all_gather x1, blocking collectives, body(): packed = lax.all_gather(packed, ('seq', 'dp'), axis=0, tiled=True)  41 us
    all_to_all x1, blocking collectives, body(): lax.all_to_all(column_send, 'seq', split_axis=0, concat_axis=0, tiled=True)  39.5 us
    dot_general x5, matrix products, inner_rows(): lax.dot_general(left, right, (((0,), (0,)), ((), ())), preferred_element_...  39.2 us
  transfers between devices with their start and end apart: 12, of which 8 were waited for; matrix products, arithmetic and copies ran while one was open for 17% of the time, Pallas kernels for 15%

profile of v2, /device:TPU:0, one launch (start us, length us, event | category | flops | bytes accessed | tf_op | source)
XLA Modules:
  0.0 845.9 jit_solution(140025408906205447)
XLA Ops:
  10.4 39.5 %all_to_all.25 = bf16[4,64,1280]{2,1,0:T(8,128)(2,1)} all-to-all(bf16[4,64,1280]{2,1,0:T(8,128)(2,1)S(1)} %maximum_bitcast_fusion), channel_id=1, replica_groups=mesh['seq'=4,'dp'=8] {'seq'}, dimensions={0} | all-to-all | bytes 1310720 | tf_op jit(solution)/shard_map/all_to_all | solution.py:639
  51.7 41.0 %all_gather.22 = bf16[1024,128]{1,0:T(8,128)(2,1)S(1)} all-gather(bf16[32,128]{1,0:T(8,128)(2,1)S(1)} %pad_bitcast_fusion), channel_id=1, replica_groups=mesh['seq'=4,'dp'=8] {'seq','dp'}, dimensions={0}, use_global_device_ids=true | all-gather | bytes 270336 | tf_op jit(solution)/shard_map/all_gather | solution.py:612
  93.9 1.9 fusion.53
  95.8 2.2 fusion.9
  98.6 12.7 %all-gather.9.cloned.1.call-done = bf16[4,512,1280]{2,1,0:T(8,128)(2,1)} async-done(((bf16[4,64,1280]{2,1,0:T(8,128)(2,1)}), bf16[4,512,1280]{2,1,0:T(8,128)(2,1)}) %all-gather.9.cloned.1.call-update) | async-done | bytes 5242896 | tf_op jit(solution)/shard_map/all_gather | solution.py:640
  111.3 5.4 fusion.84
  116.6 1.8 slice.128
  118.9 2.0 copy.87
  121.2 1.8 copy.88
  123.0 1.1 multiply_bitcast_fusion
  124.2 1.2 fusion.46
  125.4 2.5 multiply_multiply_fusion
  128.8 2.3 fusion.3
  131.1 1.8 exponential_reduce_fusion
  132.8 4.8 fusion.26.heads_hbm
  137.6 2.3 copy.92
  139.9 10.0 %all-gather.11.cloned.1.call-done.out_rows_hbm = bf16[1024,2048]{1,0:T(8,128)(2,1)} async-done(((bf16[128,2048]{1,0:T(8,128)(2,1)}), bf16[1024,2048]{1,0:T(8,128)(2,1)}) %all-gather.11.cloned.1.call-update) | async-done | bytes 4194320 | tf_op jit(solution)/shard_map/all_gather | solution.py:641
  149.9 6.2 convolution_convert_fusion.4
  156.3 13.4 %all-gather.1 = s32[1,512,8]{1,2,0:T(8,128)S(1)} all-gather(s32[1,128,8]{1,2,0:T(8,128)S(1)} %copy-done.29), channel_id=3, replica_groups=mesh['seq'=4,'dp'=8] {'seq'}, dimensions={1}, use_global_device_ids=true | all-gather | bytes 20480 | tf_op jit(solution)/shard_map/all_gather | solution.py:643
  170.2 1.2 bitcast_compare_fusion
  171.4 26.0 %all-gather.17.cloned.1.call-done = bf16[1,512,2048]{2,1,0:T(8,128)(2,1)} async-done(((bf16[1,128,2048]{2,1,0:T(8,128)(2,1)}), bf16[1,512,2048]{2,1,0:T(8,128)(2,1)}) %all-gather.17.cloned.1.call-update) | async-done | bytes 2097168 | tf_op jit(solution)/shard_map/all_gather | solution.py:679
  197.4 7.0 convolution_convert_fusion
  204.4 4.8 all-to-all-start.1
  209.2 33.8 %reduce-scatter.5.cloned.1.call-done = bf16[128,2048]{1,0:T(8,128)(2,1)} async-done(((bf16[512,2048]{1,0:T(8,128)(2,1)}), bf16[128,2048]{1,0:T(8,128)(2,1)}) %reduce-scatter.5.cloned.1.call-update) | async-done | bytes 524304 | tf_op jit(solution)/shard_map/reduce_scatter | solution.py:696
  243.1 1.3 multiply_reduce_fusion.3
  244.4 2.0 multiply_convert_fusion.2
  246.4 45.4 %all-gather.13.cloned.1.call-done = bf16[512,2048]{1,0:T(8,128)(2,1)} async-done(((bf16[128,2048]{1,0:T(8,128)(2,1)}), bf16[512,2048]{1,0:T(8,128)(2,1)}) %all-gather.13.cloned.1.call-update) | async-done | bytes 2097168 | tf_op jit(solution)/shard_map/all_gather | solution.py:700
  291.9 6.6 convolution_convert_fusion.2
  298.5 5.0 all-to-all-start.2
  303.6 1.2 reshape.495
  304.8 1.7 slice.133
  306.4 1.1 copy.114
  307.6 50.6 %all-to-all-done.2 = bf16[8,144,2048]{2,1,0:T(8,128)(2,1)} async-done(((bf16[8,144,2048]{2,1,0:T(8,128)(2,1)}), bf16[8,144,2048]{2,1,0:T(8,128)(2,1)}, u32[]{:S(2)}, u32[]{:S(2)}) %all-to-all-start.2) | async-done | bytes 4718624 | tf_op jit(solution)/shard_map/all_to_all | solution.py:666
  358.2 3.9 fusion.80
  362.2 11.2 %fusion.5 = f32[1152,1536]{1,0:T(8,128)S(1)} fusion(bf16[1152,2048]{1,0:T(8,128)(2,1)} %bitcast.24, bf16[1,2048,1536]{2,1,0:T(8,128)(2,1)} %param.21), kind=kOutput, calls=%fused_computation.16 | convolution fusion | flops 7247757312 | bytes 18087936 | tf_op jit(solution)/shard_map/dot_general | solution.py:712
  373.6 8.2 fusion.16
  381.8 8.7 %fusion.2 = (f32[1152]{0:T(1024)S(1)}, bf16[1152,2048]{1,0:T(8,128)(2,1)}) fusion(bf16[1152,2176]{1,0:T(8,128)(2,1)} %bitcast.22, f32[1152]{0:T(1024)S(1)} %select_reduce_fusion, bf16[1152,768]{1,0:T(8,128)(2,1)S(1)} %get-tuple-element.273, bf16[1,768,2048]{2,1,0:T(8,128)(2,1)S(1)} %copy-done.36), kind=kOutput, calls=%fused_computation.6 | convolution fusion | flops 3640392704 | bytes 14361600 | tf_op jit(solution)/shard_map/dot_general | solution.py:715
  390.5 8.2 convolution_convert_fusion.3
  399.6 61.1 %all_to_all.26 = bf16[8,144,2176]{2,1,0:T(8,128)(2,1)} all-to-all(bf16[8,144,2176]{2,1,0:T(8,128)(2,1)S(1)} %bitcast.154), channel_id=1, replica_groups=mesh['seq'=4,'dp'=8] {'dp'}, dimensions={0} | all-to-all | bytes 10027008 | tf_op jit(solution)/shard_map/all_to_all | solution.py:672
  460.7 4.6 all-to-all-start.3
  465.4 7.0 fusion.7
  473.4 2.0 pad_maximum_fusion.7
  475.4 3.2 copy.101
  479.2 3.3 copy.102
  484.4 1.5 fusion.48.query_hbm
  486.5 33.6 %all-to-all-done.3 = bf16[8,144,2048]{2,1,0:T(8,128)(2,1)} async-done(((bf16[8,144,2048]{2,1,0:T(8,128)(2,1)}), bf16[8,144,2048]{2,1,0:T(8,128)(2,1)}, u32[]{:S(2)}, u32[]{:S(2)}) %all-to-all-start.3) | async-done | bytes 4718624 | tf_op jit(solution)/shard_map/all_to_all | solution.py:672
  520.1 6.5 bitcast_convert_fusion
  526.7 10.2 %convolution_bitcast_fusion.2 = f32[1,768,2048]{2,1,0:T(8,128)} fusion(bf16[1152,768]{1,0:T(8,128)(2,1)} %copy-done.37, f32[1152]{0:T(1024)S(1)} %copy-done.26, bf16[1152,2176]{1,0:T(8,128)(2,1)} %bitcast.22), kind=kOutput, calls=%fused_computation.32 | convolution fusion | flops 3630956544 | bytes 12784128 | tf_op jit(solution)/shard_map/dot_general | solution.py:496
  536.9 13.3 %convolution_bitcast_fusion = f32[1,2048,1536]{2,1,0:T(8,128)} fusion(bf16[1152,2048]{1,0:T(8,128)(2,1)} %bitcast.24, bf16[1152,768]{1,0:T(8,128)(2,1)S(1)} %copy-done.41, bf16[1152,768]{1,0:T(8,128)(2,1)S(1)} %copy-done.39), kind=kOutput, calls=%fused_computation.7 | convolution fusion | flops 7254835200 | bytes 20840448 | tf_op jit(solution)/shard_map/dot_general | solution.py:496
  550.2 1.2 convert_element_type.297
  553.5 1.3 fusion.76.branch_ref
  554.7 123.8 %attention_backward.1 = (f32[128,2048]{1,0:T(8,128)}, f32[128,2048]{1,0:T(8,128)}, bf16[4,64,1280]{2,1,0:T(8,128)(2,1)}, f32[8,128]{1,0:T(8,128)}) custom-call(bf16[128,2048]{1,0:T(8,128)(2,1)} %fusion.76.branch_ref, bf16[1024,2048]{1,0:T(8,128)(2,1)} %all-gather.11.cloned.1.call-done.out_rows_hbm, bf16[2048,1280]{1,0:T(8,128)(2,1)} %bitcast.159, ...), custom_call_target="tpu_custom_call" | custom-call | tf_op jit(solution)/shard_map/attention_backward/pallas_call | solution.py:409
  678.5 1.7 slice.146
  680.2 2.2 convert_element_type.303
  682.5 1.6 fusion.40
  685.2 2.3 fusion.83
  687.5 2.5 reshape.501
  690.1 1.1 concatenate.44
  692.0 1.9 reshape.502
  697.2 1.1 pad_maximum_fusion.4
  698.4 3.7 fusion.36
  702.1 131.6 %reduce-scatter.11.cloned.1.call-done = f32[32,128]{1,0:T(8,128)} async-done(((f32[1024,128]{1,0:T(8,128)}), f32[32,128]{1,0:T(8,128)}) %reduce-scatter.11.cloned.1.call-update) | async-done | bytes 16400 | tf_op jit(solution)/shard_map/reduce_scatter | solution.py:812
  833.7 1.3 fusion.78
  835.0 1.3 fusion.79
  (193 shorter events, 23.8 us)
Async XLA Ops:
  7.2 88.6 %all-gather.15.cloned.1.call-start = ((), (), s32[]{:S(2)}) async-start(), calls=%async_computation.16 | async-start | bytes 2621440 | tf_op jit(solution)/shard_map/all_gather | solution.py:682
  7.9 103.4 %all-gather.9.cloned.1.call-start = ((), (), s32[]{:S(2)}) async-start(), calls=%async_computation.9 | async-start | bytes 5898240 | tf_op jit(solution)/shard_map/all_gather | solution.py:640
  8.9 42.5 %copy-start.24 = (bf16[64,32]{0,1:T(8,128)(2,1)S(1)}, bf16[64,32]{0,1:T(8,128)(2,1)}, u32[]{:S(2)}) copy-start(bf16[64,32]{0,1:T(8,128)(2,1)} %param.20) | copy-start | bytes 12292
  8.9 42.7 %copy-start.32 = (bf16[64]{0:T(256)(128)(2,1)S(1)}, bf16[64]{0:T(256)(128)(2,1)}, u32[]{:S(2)}) copy-start(bf16[64]{0:T(256)(128)(2,1)} %param.14) | copy-start | bytes 388
  8.9 42.7 %copy-start.33 = (bf16[64]{0:T(256)(128)(2,1)S(1)}, bf16[64]{0:T(256)(128)(2,1)}, u32[]{:S(2)}) copy-start(bf16[64]{0:T(256)(128)(2,1)} %param.19) | copy-start | bytes 388
  8.9 42.7 %copy-start.34 = (bf16[4]{0:T(256)(128)(2,1)S(1)}, bf16[4]{0:T(256)(128)(2,1)}, u32[]{:S(2)}) copy-start(bf16[4]{0:T(256)(128)(2,1)} %param.15) | copy-start | bytes 28
  8.9 42.7 %copy-start.35 = (bf16[4]{0:T(256)(128)(2,1)S(1)}, bf16[4]{0:T(256)(128)(2,1)}, u32[]{:S(2)}) copy-start(bf16[4]{0:T(256)(128)(2,1)} %param.16) | copy-start | bytes 28
  50.0 100.0 %all-gather.11.cloned.1.call-start = ((), (), s32[]{:S(2)}) async-start(), calls=%async_computation.10 | async-start | bytes 4718592 | tf_op jit(solution)/shard_map/all_gather | solution.py:641
  50.7 146.7 %all-gather.17.cloned.1.call-start = ((), (), s32[]{:S(2)}) async-start(), calls=%async_computation.17 | async-start | bytes 2621440 | tf_op jit(solution)/shard_map/all_gather | solution.py:679
  51.3 191.8 %reduce-scatter.5.cloned.1.call-start = ((), (), s32[]{:S(2)}) async-start(), calls=%async_computation.11 | async-start | bytes 2621440 | tf_op jit(solution)/shard_map/reduce_scatter | solution.py:696
  92.8 5.2 copy-start.19
  93.7 4.9 copy-start.21
  95.8 2.2 copy-start.2
  98.6 18.0 %copy-start.6 = (bf16[512,2048]{1,0:T(8,128)(2,1)}, bf16[512,2048]{1,0:T(8,128)(2,1)S(1)}, u32[]{:S(2)}) copy-start(bf16[512,2048]{1,0:T(8,128)(2,1)S(1)} %fusion.11.normed_hbm) | copy-start | bytes 6291460
  116.6 2.1 copy-start.1
  123.0 4.9 copy-start.12
  123.0 4.9 copy-start.13
  125.4 3.3 copy-start.16
  149.9 6.4 copy-start.29
  204.4 38.7 %copy-start = (bf16[1,128,2048]{2,1,0:T(8,128)(2,1)S(1)}, bf16[1,128,2048]{2,1,0:T(8,128)(2,1)}, u32[]{:S(2)}) copy-start(bf16[1,128,2048]{2,1,0:T(8,128)(2,1)} %param.12) | copy-start | bytes 1572868
  204.4 94.1 %all-to-all-start.1 = ((bf16[8,144,2176]{2,1,0:T(8,128)(2,1)}), bf16[8,144,2176]{2,1,0:T(8,128)(2,1)}, u32[]{:S(2)}, u32[]{:S(2)}) async-start(bf16[8,144,2176]{2,1,0:T(8,128)(2,1)} %bitcast.160), calls=%async_computation.2 | async-start | bytes 10027008 | tf_op jit(solution)/shard_map/all_to_all | solution.py:666
  209.2 82.7 %all-gather.13.cloned.1.call-start = ((), (), s32[]{:S(2)}) async-start(), calls=%async_computation.12 | async-start | bytes 2621440 | tf_op jit(solution)/shard_map/all_gather | solution.py:700
  244.3 54.1 %copy-start.30 = (f32[128]{0:T(128)}, f32[128]{0:T(128)S(1)}, u32[]{:S(2)}) copy-start(f32[128]{0:T(128)S(1)} %multiply_reduce_fusion.3) | copy-start | bytes 1540
  244.4 54.1 %copy-start.27 = (f32[128]{0:T(128)}, f32[128]{0:T(128)S(1)}, u32[]{:S(2)}) copy-start(f32[128]{0:T(128)S(1)} %fusion.66) | copy-start | bytes 1540
  298.5 5.0 copy-start.20
  298.5 59.7 %all-to-all-start.2 = ((bf16[8,144,2048]{2,1,0:T(8,128)(2,1)}), bf16[8,144,2048]{2,1,0:T(8,128)(2,1)}, u32[]{:S(2)}, u32[]{:S(2)}) async-start(bf16[8,144,2048]{2,1,0:T(8,128)(2,1)} %bitcast.162), calls=%async_computation.3 | async-start | bytes 9437184 | tf_op jit(solution)/shard_map/all_to_all | solution.py:666
  362.2 11.3 %copy-start.36 = (bf16[1,768,2048]{2,1,0:T(8,128)(2,1)S(1)}, bf16[1,768,2048]{2,1,0:T(8,128)(2,1)}, u32[]{:S(2)}) copy-start(bf16[1,768,2048]{2,1,0:T(8,128)(2,1)} %param.22) | copy-start | bytes 9437188
  362.2 28.3 %slice-start = ((s8[6291456]{0:T(1024)(128)(4,1)}), s8[4194304]{0:T(1024)(128)(4,1)S(1)}, s32[]{:S(2)}) async-start(s8[6291456]{0:T(1024)(128)(4,1)} %bitcast.175), calls=%async_computation.18 | async-start | bytes 8388608
  373.5 8.2 copy-start.25
  373.5 17.0 %slice-start.1 = ((s8[6291456]{0:T(1024)(128)(4,1)}), s8[2097152]{0:T(1024)(128)(4,1)S(1)}, s32[]{:S(2)}) async-start(s8[6291456]{0:T(1024)(128)(4,1)} %bitcast.175), calls=%async_computation.19 | async-start | bytes 4194304
  381.7 8.7 %copy-start.37 = (bf16[1152,768]{1,0:T(8,128)(2,1)}, bf16[1152,768]{1,0:T(8,128)(2,1)S(1)}, u32[]{:S(2)}) copy-start(bf16[1152,768]{1,0:T(8,128)(2,1)S(1)} %get-tuple-element.273) | copy-start | bytes 5308420
  381.7 8.8 %copy-start.38 = (bf16[1152,768]{1,0:T(8,128)(2,1)}, bf16[1152,768]{1,0:T(8,128)(2,1)S(1)}, u32[]{:S(2)}) copy-start(bf16[1152,768]{1,0:T(8,128)(2,1)S(1)} %get-tuple-element.271) | copy-start | bytes 5308420
  381.7 8.8 %copy-start.40 = (bf16[1152,768]{1,0:T(8,128)(2,1)S(1)}, bf16[1152,768]{1,0:T(8,128)(2,1)}, u32[]{:S(2)}) copy-start(bf16[1152,768]{1,0:T(8,128)(2,1)} %get-tuple-element.272) | copy-start | bytes 5308420
  460.7 59.4 %all-to-all-start.3 = ((bf16[8,144,2048]{2,1,0:T(8,128)(2,1)}), bf16[8,144,2048]{2,1,0:T(8,128)(2,1)}, u32[]{:S(2)}, u32[]{:S(2)}) async-start(bf16[8,144,2048]{2,1,0:T(8,128)(2,1)} %bitcast.161), calls=%async_computation.4 | async-start | bytes 9437184 | tf_op jit(solution)/shard_map/all_to_all | solution.py:672
  465.4 7.2 copy-start.23
  465.4 8.1 copy-start.14
  465.4 84.8 %reduce-scatter.9.cloned.1.call-start = ((), (), s32[]{:S(2)}) async-start(), calls=%async_computation.14 | async-start | bytes 2785280 | tf_op jit(solution)/shard_map/reduce_scatter | solution.py:676
  472.4 226.0 %reduce-scatter.7.cloned.1.call-start = ((), (), s32[]{:S(2)}) async-start(), calls=%async_computation.13 | async-start | bytes 2621440 | tf_op jit(solution)/shard_map/reduce_scatter | solution.py:676
  478.6 3.9 copy-start.17
  482.5 3.4 copy-start.3
  482.5 3.4 copy-start.7
  486.5 40.1 %copy-start.26 = (f32[1152]{0:T(1024)S(1)}, f32[1152]{0:T(1024)}, u32[]{:S(2)}) copy-start(f32[1152]{0:T(1024)} %copy-done.25) | copy-start | bytes 13828
  526.6 307.1 %reduce-scatter.11.cloned.1.call-start = ((), (), s32[]{:S(2)}) async-start(), calls=%async_computation.15 | async-start | bytes 540672 | tf_op jit(solution)/shard_map/reduce_scatter | solution.py:812
  526.7 10.2 %copy-start.39 = (bf16[1152,768]{1,0:T(8,128)(2,1)S(1)}, bf16[1152,768]{1,0:T(8,128)(2,1)}, u32[]{:S(2)}) copy-start(bf16[1152,768]{1,0:T(8,128)(2,1)} %copy-done.38) | copy-start | bytes 5308420
  526.7 10.2 %copy-start.41 = (bf16[1152,768]{1,0:T(8,128)(2,1)S(1)}, bf16[1152,768]{1,0:T(8,128)(2,1)}, u32[]{:S(2)}) copy-start(bf16[1152,768]{1,0:T(8,128)(2,1)} %get-tuple-element.272) | copy-start | bytes 5308420
  536.9 14.8 %copy-start.5 = (bf16[128,2048]{1,0:T(8,128)(2,1)S(1)}, bf16[128,2048]{1,0:T(8,128)(2,1)}, u32[]{:S(2)}) copy-start(bf16[128,2048]{1,0:T(8,128)(2,1)} %reduce-scatter.5.cloned.1.call-done) | copy-start | bytes 1572868
  536.9 14.8 %copy-start.8 = (bf16[2048,32]{1,0:T(8,128)(2,1)S(1)}, bf16[2048,32]{1,0:T(8,128)(2,1)}, u32[]{:S(2)}) copy-start(bf16[2048,32]{1,0:T(8,128)(2,1)} %reshape.495) | copy-start | bytes 393220
  536.9 14.8 %copy-start.28 = (f32[128]{0:T(128)S(1)}, f32[128]{0:T(128)}, u32[]{:S(2)}) copy-start(f32[128]{0:T(128)} %copy-done.27) | copy-start | bytes 1540
  550.2 2.3 copy-start.31
  550.2 3.2 copy-start.9
  551.4 1.1 copy-start.15
  552.5 1.0 copy-start.11
  554.7 127.7 %copy-start.22 = (f32[2048]{0:T(1024)S(1)}, f32[2048]{0:T(1024)}, u32[]{:S(2)}) copy-start(f32[2048]{0:T(1024)} %copy-done.21) | copy-start | bytes 24580
  678.5 6.7 copy-start.4
  687.5 9.4 %copy-start.10 = (f32[4,64,1280]{2,1,0:T(8,128)S(1)}, f32[4,64,1280]{2,1,0:T(8,128)}, u32[]{:S(2)}) copy-start(f32[4,64,1280]{2,1,0:T(8,128)} %convert_element_type.303) | copy-start | bytes 3932164
  698.4 139.5 %copy-start.18 = (f32[128,2048]{1,0:T(8,128)S(1)}, f32[128,2048]{1,0:T(8,128)}, u32[]{:S(2)}) copy-start(f32[128,2048]{1,0:T(8,128)} %get-tuple-element.323) | copy-start | bytes 3145732
Sparse Core Ops, SparseCore 0:
  9.6 59.1 all-gather.14
  70.6 40.5 all-gather.8
  113.2 36.7 all-gather.10
  151.3 46.0 all-gather.16
  200.1 42.8 reduce-scatter.4
  246.6 45.2 all-gather.12
  472.5 45.1 reduce-scatter.8
  526.7 47.4 reduce-scatter.6
  697.4 136.3 reduce-scatter.10

commit v3 on v2

--- a/solution.py
+++ b/solution.py
@@ -22,7 +22,7 @@
 
 
 MESH = pl.DeviceIdType.MESH
-VMEM_BYTES = 62 * 1024 * 1024
+VMEM_BYTES = 63 * 1024 * 1024
 
 
 def dot_nn(left, right):
@@ -106,18 +106,18 @@
 
     @pl.when((turn >= 0) & (last > place))
     def _():
-        block = sums.at[0, last]
+        block = sums.at[last]
 
         @pl.when(place > 0)
         def _():
             remote(block, block, send_sems.at[0, last], recv_sems.at[0, last], (place, column)).wait_recv()
-            sums[0, last] = (
-                sums[0, last].astype(jnp.float32) + own[last].astype(jnp.float32)
+            sums[last] = (
+                sums[last].astype(jnp.float32) + own[last].astype(jnp.float32)
             ).astype(jnp.bfloat16)
 
         @pl.when(place == 0)
         def _():
-            sums[0, last] = own[last]
+            sums[last] = own[last]
 
         remote(block, block, send_sems.at[0, last], recv_sems.at[0, last], (place + 1, column)).start()
 
@@ -125,20 +125,21 @@
 
     @pl.when((first >= 0) & (first < place))
     def _():
-        block = sums.at[1, first]
+        block = sums.at[first]
 
         @pl.when(place < count - 1)
         def _():
             remote(block, block, send_sems.at[1, first], recv_sems.at[1, first], (place, column)).wait_recv()
-            sums[1, first] = (
-                sums[1, first].astype(jnp.float32) + own[first].astype(jnp.float32)
+            sums[first] = (
+                sums[first].astype(jnp.float32) + own[first].astype(jnp.float32)
             ).astype(jnp.bfloat16)
 
         @pl.when(place == count - 1)
         def _():
-            sums[1, first] = own[first]
-
-        remote(block, block, send_sems.at[1, first], recv_sems.at[1, first], (place - 1, column)).start()
+            sums[first] = own[first]
+
+        target = sums.at[jnp.where(first == place - 1, count, first)]
+        remote(block, target, send_sems.at[1, first], recv_sems.at[1, first], (place - 1, column)).start()
 
 
 def line_sum_end(count, place, column, own, sums, send_sems, recv_sems, total):
@@ -146,27 +147,27 @@
 
     @pl.when(place > 0)
     def _():
-        block = sums.at[0, place]
+        block = sums.at[place]
         remote(block, block, send_sems.at[0, place], recv_sems.at[0, place], (place, column)).wait_recv()
-        total[...] += sums[0, place].astype(jnp.float32)
+        total[...] += sums[place].astype(jnp.float32)
 
     @pl.when(place < count - 1)
     def _():
-        block = sums.at[1, place]
+        block = sums.at[count]
         remote(block, block, send_sems.at[1, place], recv_sems.at[1, place], (place, column)).wait_recv()
-        total[...] += sums[1, place].astype(jnp.float32)
+        total[...] += sums[count].astype(jnp.float32)
 
     for step in range(count - 1):
         last = count - 1 - step
 
         @pl.when(last > place)
         def _():
-            block = sums.at[0, last]
+            block = sums.at[last]
             remote(block, block, send_sems.at[0, last], recv_sems.at[0, last], (place + 1, column)).wait_send()
 
         @pl.when(step < place)
         def _():
-            block = sums.at[1, step]
+            block = sums.at[step]
             remote(block, block, send_sems.at[1, step], recv_sems.at[1, step], (place - 1, column)).wait_send()
 
 
@@ -441,7 +442,7 @@
             pltpu.VMEM((count, shard, width), low),
             dma((4, chips)),
             pltpu.VMEM((count, tokens, MODEL_WIDTH), low),
-            pltpu.VMEM((2, count, tokens, MODEL_WIDTH), low),
+            pltpu.VMEM((count + 1, tokens, MODEL_WIDTH), low),
             dma((2, count)),
             dma((2, count)),
             dma((2, count)),
@@ -451,6 +452,397 @@
         ),
         name="attention_backward",
     )(branch, out_rows, own_cols, normed, heads_low, queries, pair, proj, lse, turn_cos, turn_sin, gains)
+
+
+def expert_kernel(
+    count, planes, tokens, slots, chunks,
+    mixed_ref, masks_ref, spreader_hbm, grad_hbm, router_hbm, in_hbm, back_hbm,
+    total_ref, gate_total_ref, grad_in_hbm, grad_back_hbm, combined_hbm,
+    spreader, grad_rows, router, weight_in, weight_back, local_sems,
+    full, ag_send, ag_recv,
+    sent, arrived, x_send, x_recv,
+    gate_up, act, grad_gate_up, logits,
+    back_arrived, b_send, b_recv,
+    gate_sent, gate_arrived, gate_own, gate_sums, g_send, g_recv, gs_send, gs_recv,
+    sums, rs_send, rs_recv, tile_sems, combined_sems,
+):
+    place = lax.axis_index("seq")
+    member = lax.axis_index("dp")
+    rows = planes * slots
+    length = count * tokens
+    wide = MODEL_WIDTH // chunks
+    half = rows // 2
+    own_expert = place * planes + member
+    low = jnp.bfloat16
+
+    loads = [
+        pltpu.make_async_copy(spreader_hbm, spreader, local_sems.at[0]),
+        pltpu.make_async_copy(router_hbm, router, local_sems.at[1]),
+        pltpu.make_async_copy(in_hbm, weight_in, local_sems.at[2]),
+        pltpu.make_async_copy(grad_hbm, grad_rows, local_sems.at[3]),
+    ] + [
+        pltpu.make_async_copy(
+            back_hbm.at[:, pl.ds(c * wide, wide)], weight_back.at[c], local_sems.at[4 + c]
+        )
+        for c in range(chunks)
+    ]
+    for load in loads:
+        load.start()
+    for c in range(chunks):
+        full[c, place] = mixed_ref[:, c * wide : (c + 1) * wide]
+    greet(
+        [(place, lax.rem(member + j, planes)) for j in range(1, planes)]
+        + [(lax.rem(place + k, count), member) for k in range(1, count)]
+    )
+
+    def line(c):
+        return (count, place, member, full.at[c], ag_send.at[c], ag_recv.at[c])
+
+    def row_copy(c, j):
+        other = lax.rem(member + j, planes)
+        return remote(
+            sent.at[c, other], arrived.at[c, member], x_send.at[c, j], x_recv.at[c, j], (place, other)
+        )
+
+    for c in range(chunks):
+        line_gather_step(0, *line(c))
+    gate_up[...] = jnp.zeros_like(gate_up)
+    logits[...] = jnp.zeros_like(logits)
+    loads[0].wait()
+
+    def dispatch(c, carry):
+        for step in range(1, count):
+            line_gather_step(step, *line(c))
+        picked = dot_tn(spreader[...], full[c].reshape(length, wide)).astype(low)
+        sent[c] = picked.reshape(planes, slots, wide)
+        for j in range(1, planes):
+            row_copy(c, j).start()
+        arrived[c, member] = sent[c, member]
+        return carry
+
+    lax.fori_loop(0, chunks, dispatch, 0)
+    for load in loads[1:]:
+        load.wait()
+
+    def forward(c, carry):
+        for j in range(1, planes):
+            row_copy(c, j).wait_recv()
+        part = pl.ds(pl.multiple_of(c * wide, wide), wide)
+        x = arrived[c].reshape(rows, wide)
+        for piece in range(2):
+            at = slice(piece * half, (piece + 1) * half)
+            gate_up[at, :] += dot_nn(x[at], weight_in[part, :])
+            logits[at, :] += dot_nn(x[at], router[part, :])
+        return carry
+
+    lax.fori_loop(0, chunks, forward, 0)
+
+    def settle(c, carry):
+        for j in range(1, planes):
+            row_copy(c, j).wait_send()
+        line_gather_end(*line(c))
+        return carry
+
+    lax.fori_loop(0, chunks, settle, 0)
+
+    mask = masks_ref[:, : logits.shape[-1]].astype(jnp.float32)
+    shifted = jnp.where(mask > 0, logits[...], FILLER)
+    powers = jnp.where(mask > 0, jnp.exp(shifted - jnp.max(shifted, axis=-1, keepdims=True)), 0.0)
+    powers_total = jnp.sum(powers, axis=-1, keepdims=True)
+    lanes = lax.broadcasted_iota(jnp.int32, powers.shape, 1)
+    own = jnp.sum(jnp.where(lanes == own_expert, powers, 0.0), axis=-1, keepdims=True)
+    gate = own / jnp.where(powers_total > 0, powers_total, 1.0)
+    gate_column = logits
+    gate_column[...] = jnp.broadcast_to(gate, gate_column.shape)
+
+    blocks = 4 if rows % 64 == 0 else 2
+    step_rows = rows // blocks
+
+    def backward(index, carry):
+        at = pl.ds(pl.multiple_of(index * step_rows, step_rows), step_rows)
+        scale = gate_column[at, 0:1]
+        grad_act = jnp.zeros((step_rows, FF), jnp.float32)
+        for c in range(chunks):
+            scaled = (grad_rows[c, at, :].astype(jnp.float32) * scale).astype(low)
+            grad_act += dot_nt(scaled, weight_back[c])
+        gate_part = gate_up[at, :FF]
+        up_part = gate_up[at, FF:]
+        chance = jax.nn.sigmoid(gate_part)
+        silu = gate_part * chance
+        act[at, :] = (silu * up_part).astype(low)
+        slope = chance + silu * (1.0 - chance)
+        grad_gate_up[at, :FF] = (grad_act * up_part * slope).astype(low)
+        grad_gate_up[at, FF:] = (grad_act * silu).astype(low)
+        return carry
+
+    lax.fori_loop(0, blocks, backward, 0)
+
+    def back_copy(c, j):
+        other = lax.rem(member + j, planes)
+        return remote(
+            sent.at[c, other], back_arrived.at[c, member], b_send.at[c, j], b_recv.at[c, j], (place, other)
+        )
+
+    def gate_copy(j):
+        other = lax.rem(member + j, planes)
+        return remote(
+            gate_sent.at[other], gate_arrived.at[member], g_send.at[j], g_recv.at[j], (place, other)
+        )
+
+    def send_back(c, carry):
+        part = pl.ds(pl.multiple_of(c * wide, wide), wide)
+        back = dot_nt(grad_gate_up[...], weight_in[part, :]).astype(low)
+        sent[c] = back.reshape(planes, slots, wide)
+        for j in range(1, planes):
+            back_copy(c, j).start()
+        back_arrived[c, member] = sent[c, member]
+        return carry
+
+    lax.fori_loop(0, chunks, send_back, 0)
+
+    in_tiles = [gate_up.at[part * wide : (part + 1) * wide, :FF] for part in range(2)]
+    back_tile = gate_up.at[:FF, FF : FF + wide]
+
+    def in_copy(slot, c, part):
+        return pltpu.make_async_copy(
+            in_tiles[slot],
+            grad_in_hbm.at[pl.ds(pl.multiple_of(c * wide, wide), wide), pl.ds(part * FF, FF)],
+            tile_sems.at[slot],
+        )
+
+    def in_gradient(c, carry):
+        x = arrived[c].reshape(rows, wide)
+        for part in range(2):
+
+            @pl.when(c > 0)
+            def _():
+                in_copy(part, c, part).wait()
+
+            in_tiles[part][...] = dot_tn(x, grad_gate_up[:, part * FF : (part + 1) * FF])
+            in_copy(part, c, part).start()
+        return carry
+
+    lax.fori_loop(0, chunks, in_gradient, 0)
+
+    def combined_copy(c):
+        return pltpu.make_async_copy(arrived.at[c], combined_hbm.at[c], combined_sems.at[c])
+
+    def outputs(c, grad_gate):
+        result = dot_nn(act[...], weight_back[c]).astype(low).astype(jnp.float32)
+        grads = grad_rows[c].astype(jnp.float32)
+        scale = gate_column[:, 0:1]
+        grad_rows[c] = (grads * scale).astype(low)
+        arrived[c] = (result * scale).astype(low).reshape(planes, slots, wide)
+        combined_copy(c).start()
+        return grad_gate + jnp.sum(result * grads, axis=-1, keepdims=True)
+
+    grad_gate = lax.fori_loop(0, chunks, outputs, jnp.zeros((rows, 1), jnp.float32))
+    high = grad_gate.astype(low).astype(jnp.float32)
+    rest = grad_gate - high
+    experts = count * planes
+    wide_lanes = lax.broadcasted_iota(jnp.int32, (rows, gate_sent.shape[-1]), 1)
+    columns = jnp.where(
+        wide_lanes == own_expert, high, jnp.where(wide_lanes == own_expert + experts, rest, 0.0)
+    )
+    gate_sent[...] = columns.astype(low).reshape(gate_sent.shape)
+    for j in range(1, planes):
+        gate_copy(j).start()
+    gate_arrived[member] = gate_sent[member]
+
+    def back_tile_copy(c):
+        return pltpu.make_async_copy(
+            back_tile,
+            grad_back_hbm.at[:, pl.ds(pl.multiple_of(c * wide, wide), wide)],
+            tile_sems.at[2],
+        )
+
+    def back_gradient(c, carry):
+        result = dot_tn(act[...], grad_rows[c])
+
+        @pl.when(c > 0)
+        def _():
+            back_tile_copy(c).wait()
+
+        back_tile[...] = result
+        back_tile_copy(c).start()
+        return carry
+
+    lax.fori_loop(0, chunks, back_gradient, 0)
+
+    def sums_line(c):
+        return (count, place, member, full.at[c], sums.at[c], rs_send.at[c], rs_recv.at[c])
+
+    for c in range(chunks):
+        for j in range(1, planes):
+            back_copy(c, j).wait_recv()
+        own_sums = dot_nn(spreader[...], back_arrived[c].reshape(rows, wide)).astype(low)
+        full[c] = own_sums.reshape(count, tokens, wide)
+        for step in range(count - 1):
+            line_sum_step(step, *sums_line(c))
+    for j in range(1, planes):
+        gate_copy(j).wait_recv()
+    extra = gate_sent.shape[-1]
+    gate_own[...] = (
+        dot_nn(spreader[...], gate_arrived[...].reshape(rows, extra))
+        .astype(low)
+        .reshape(count, tokens, extra)
+    )
+    gate_line = (count, place, member, gate_own, gate_sums, gs_send, gs_recv)
+    for step in range(count - 1):
+        line_sum_step(step, *gate_line)
+    for c in range(chunks):
+        line_sum_end(*sums_line(c), total_ref.at[:, c * wide : (c + 1) * wide])
+    line_sum_end(*gate_line, gate_total_ref)
+    for c in range(chunks):
+        for j in range(1, planes):
+            back_copy(c, j).wait_send()
+        combined_copy(c).wait()
+    for j in range(1, planes):
+        gate_copy(j).wait_send()
+    in_copy(0, 0, 0).wait()
+    in_copy(1, 0, 1).wait()
+    back_tile_copy(0).wait()
+
+
+def expert_layer(
+    count, planes, mixed, masks, spreader, grad_rows, router, weight_in, weight_back
+):
+    tokens = mixed.shape[0]
+    length = count * tokens
+    chunks, rows, wide = grad_rows.shape
+    slots = rows // planes
+    extra = masks.shape[-1]
+    experts = router.shape[-1]
+    low = jnp.bfloat16
+    vmem = pl.BlockSpec(memory_space=pltpu.VMEM)
+    anywhere = pl.BlockSpec(memory_space=pl.ANY)
+    dma = pltpu.SemaphoreType.DMA
+    return pl.pallas_call(
+        functools.partial(expert_kernel, count, planes, tokens, slots, chunks),
+        out_shape=(
+            jax.ShapeDtypeStruct((tokens, MODEL_WIDTH), jnp.float32),
+            jax.ShapeDtypeStruct((tokens, extra), jnp.float32),
+            jax.ShapeDtypeStruct(weight_in.shape, jnp.float32),
+            jax.ShapeDtypeStruct(weight_back.shape, jnp.float32),
+            jax.ShapeDtypeStruct((chunks, planes, slots, wide), low),
+        ),
+        in_specs=[vmem] * 2 + [anywhere] * 5,
+        out_specs=(vmem, vmem, anywhere, anywhere, anywhere),
+        scratch_shapes=[
+            pltpu.VMEM(spreader.shape, low),
+            pltpu.VMEM(grad_rows.shape, low),
+            pltpu.VMEM(router.shape, low),
+            pltpu.VMEM(weight_in.shape, low),
+            pltpu.VMEM((chunks, FF, wide), low),
+            dma((4 + chunks,)),
+            pltpu.VMEM((chunks, count, tokens, wide), low),
+            dma((chunks, 2, count)),
+            dma((chunks, 2, count)),
+            pltpu.VMEM((chunks, planes, slots, wide), low),
+            pltpu.VMEM((chunks, planes, slots, wide), low),
+            dma((chunks, planes)),
+            dma((chunks, planes)),
+            pltpu.VMEM((rows, 2 * FF), jnp.float32),
+            pltpu.VMEM((rows, FF), low),
+            pltpu.VMEM((rows, 2 * FF), low),
+            pltpu.VMEM((rows, experts), jnp.float32),
+            pltpu.VMEM((chunks, planes, slots, wide), low),
+            dma((chunks, planes)),
+            dma((chunks, planes)),
+            pltpu.VMEM((planes, slots, extra), low),
+            pltpu.VMEM((planes, slots, extra), low),
+            pltpu.VMEM((count, tokens, extra), low),
+            pltpu.VMEM((count + 1, tokens, extra), low),
+            dma((planes,)),
+            dma((planes,)),
+            dma((2, count)),
+            dma((2, count)),
+            pltpu.VMEM((chunks, count + 1, tokens, wide), low),
+            dma((chunks, 2, count)),
+            dma((chunks, 2, count)),
+            dma((3,)),
+            dma((chunks,)),
+        ],
+        compiler_params=pltpu.CompilerParams(
+            collective_id=2, has_side_effects=True, vmem_limit_bytes=VMEM_BYTES
+        ),
+        name="expert_layer",
+    )(mixed, masks, spreader, grad_rows, router, weight_in, weight_back)
+
+
+def small_kernel(
+    count, chips, own_ref, total_ref, line_got, line_sum, chip_got, core_sum, core_got,
+    z_send, z_recv, c_send, c_recv, p_send, p_recv,
+):
+    place = lax.axis_index("seq")
+    member = lax.axis_index("dp")
+    core = lax.rem(member, 2)
+    chip = member // 2
+    partner = member + 1 - 2 * core
+    far_places = [lax.rem(place + k, count) for k in range(1, count)]
+    far_chips = [lax.rem(chip + k, chips) for k in range(1, chips)]
+    greet(
+        [(other, member) for other in far_places]
+        + [(place, 2 * other + core) for other in far_chips]
+        + [(place, partner)]
+    )
+    copies = [
+        remote(own_ref.at[other], line_got.at[k], z_send.at[k], z_recv.at[k], (other, member))
+        for k, other in enumerate(far_places)
+    ]
+    for copy in copies:
+        copy.start()
+    total = own_ref[place]
+    for k, copy in enumerate(copies):
+        copy.wait_recv()
+        total += line_got[k]
+    line_sum[...] = total
+    chip_copies = [
+        remote(line_sum.at[other], chip_got.at[k], c_send.at[k], c_recv.at[k], (place, 2 * other + core))
+        for k, other in enumerate(far_chips)
+    ]
+    for copy in chip_copies:
+        copy.start()
+    mine = line_sum[chip]
+    for k, copy in enumerate(chip_copies):
+        copy.wait_recv()
+        mine += chip_got[k]
+    core_sum[...] = mine
+    pair = remote(core_sum, core_got, p_send, p_recv, (place, partner))
+    pair.start()
+    pair.wait_recv()
+    total_ref[...] = core_sum[...] + core_got[...]
+    pair.wait_send()
+    for copy in copies + chip_copies:
+        copy.wait_send()
+
+
+def small_sums(count, chips, own):
+    shape = own.shape[2:]
+    vmem = pl.BlockSpec(memory_space=pltpu.VMEM)
+    dma = pltpu.SemaphoreType.DMA
+    kind = jnp.float32
+    return pl.pallas_call(
+        functools.partial(small_kernel, count, chips),
+        out_shape=jax.ShapeDtypeStruct(shape, kind),
+        in_specs=[vmem],
+        out_specs=vmem,
+        scratch_shapes=[
+            pltpu.VMEM((count - 1, chips) + shape, kind),
+            pltpu.VMEM((chips,) + shape, kind),
+            pltpu.VMEM((chips - 1,) + shape, kind),
+            pltpu.VMEM(shape, kind),
+            pltpu.VMEM(shape, kind),
+            dma((count - 1,)),
+            dma((count - 1,)),
+            dma((chips - 1,)),
+            dma((chips - 1,)),
+            dma(()),
+            dma(()),
+        ],
+        compiler_params=pltpu.CompilerParams(collective_id=4, has_side_effects=True),
+        name="small_sums",
+    )(own)
 
 
 def rms_norm(values, gain):
@@ -597,7 +989,9 @@
     own_width = query_columns + 2 * HEAD_SIZE
     head_replicas = sequence_number // KEY_VALUE_HEADS
     capacity = (tokens * TOP * 9 + 8 * devices - 1) // (8 * devices)
-    slots = sequence_number * capacity
+    slots = -(-sequence_number * capacity // 16) * 16
+    chunks = 4
+    wide = MODEL_WIDTH // chunks
     sequence_length = sequence_number * tokens
     extra = -(-2 * devices // 128) * 128
 
@@ -657,22 +1051,26 @@
     places = places + (jnp.arange(sequence_number, dtype=jnp.int32) * capacity)[:, None, None]
     places = jnp.where(route_mask > 0, places.reshape(sequence_length, devices), -1)
     plane_places = lax.dynamic_slice_in_dim(places, group * planes, planes, 1)
-    picker = (
-        plane_places.T[:, None, :] == jnp.arange(slots, dtype=jnp.int32)[None, :, None]
-    ).astype(jnp.bfloat16).reshape(planes * slots, sequence_length)
+    column_ids = jnp.arange(planes * slots, dtype=jnp.int32)
+    column_places = jnp.full((sequence_length, planes * slots), -2, jnp.int32)
+    for other in range(planes):
+        column_places = jnp.where(
+            (column_ids // slots == other)[None, :], plane_places[:, other : other + 1], column_places
+        )
+    spreader = (column_places == (column_ids % slots)[None, :]).astype(jnp.bfloat16)
 
     def dispatch(rows):
-        sent = jnp.dot(picker, rows, preferred_element_type=jnp.float32).astype(jnp.bfloat16)
+        sent = inner_rows(spreader, rows).astype(jnp.bfloat16)
         return lax.all_to_all(
             sent.reshape(planes, slots, rows.shape[-1]), "dp", split_axis=0, concat_axis=0, tiled=True
         ).reshape(planes * slots, rows.shape[-1])
 
     def combine(rows):
-        width = rows.shape[-1]
-        back = lax.all_to_all(
-            rows.reshape(planes, slots, width), "dp", split_axis=0, concat_axis=0, tiled=True
-        ).reshape(planes * slots, width)
-        sums = inner_rows(picker, back).astype(jnp.bfloat16)
+        back = lax.all_to_all(rows, "dp", split_axis=1, concat_axis=1, tiled=True)
+        back = jnp.transpose(
+            back.reshape(chunks, planes * slots, wide), (1, 0, 2)
+        ).reshape(planes * slots, MODEL_WIDTH)
+        sums = jnp.dot(spreader, back, preferred_element_type=jnp.float32).astype(jnp.bfloat16)
         return lax.psum_scatter(sums, "seq", scatter_dimension=0, tiled=True).astype(jnp.float32)
 
     mask_columns = jnp.pad(route_mask.astype(jnp.bfloat16), ((0, 0), (0, extra - devices)))
@@ -697,46 +1095,19 @@
         branch_part.astype(jnp.bfloat16), "seq", scatter_dimension=0, tiled=True
     ).astype(jnp.float32)
     mixed_low = rms_norm(hidden1, gain_two).astype(jnp.bfloat16)
-    mixed_full = lax.all_gather(mixed_low, "seq", axis=0, tiled=True)
-    arrived = dispatch(mixed_full)
-
-    weight_in = gate_up_weight[0]
-    weight_back = down_weight[0]
-    own_expert = group * planes + member
-    row_mask = grad_arrived[:, MODEL_WIDTH : MODEL_WIDTH + devices].astype(jnp.float32)
-    grad_rows = grad_arrived[:, :MODEL_WIDTH].astype(jnp.float32)
-    row_gates = masked_softmax(
-        jnp.dot(arrived, full_router, preferred_element_type=jnp.float32), row_mask
-    )
-    gate = jnp.sum(jnp.where(expert_ids[None, :] == own_expert, row_gates, 0.0), axis=1)[:, None]
-    gate_up = jnp.dot(arrived, weight_in, preferred_element_type=jnp.float32)
-    hidden = (jax.nn.silu(gate_up[:, :FF]) * gate_up[:, FF:]).astype(jnp.bfloat16)
-    expert_out = (
-        jnp.dot(hidden, weight_back, preferred_element_type=jnp.float32)
-        .astype(jnp.bfloat16)
-        .astype(jnp.float32)
-    )
-    grad_gate = jnp.sum(expert_out * grad_rows, axis=1, keepdims=True)
-    combined_rows = (gate * expert_out).astype(jnp.bfloat16)
-    back_rows = (gate * grad_rows).astype(jnp.bfloat16)
-    grad_weight_back = inner_rows(hidden, back_rows)
-    grad_hidden = outer_cols(back_rows, weight_back)
-    _, pull_act = jax.vjp(
-        lambda gate_in, up_in: jax.nn.silu(gate_in) * up_in, gate_up[:, :FF], gate_up[:, FF:]
-    )
-    grad_gate_in, grad_up_in = pull_act(grad_hidden)
-    grad_gate_up = jnp.concatenate([grad_gate_in, grad_up_in], axis=1).astype(jnp.bfloat16)
-    grad_weight_in = inner_rows(arrived, grad_gate_up)
-    grad_back = outer_cols(grad_gate_up, weight_in).astype(jnp.bfloat16)
-    high = grad_gate.astype(jnp.bfloat16)
-    rest = (grad_gate - high.astype(jnp.float32)).astype(jnp.bfloat16)
-    extra_ids = jnp.arange(extra, dtype=jnp.int32)[None, :]
-    gate_columns = jnp.where(
-        extra_ids == own_expert,
-        high,
-        jnp.where(extra_ids == own_expert + devices, rest, jnp.zeros((), jnp.bfloat16)),
-    )
-    grad_sent = combine(jnp.concatenate([grad_back, gate_columns], axis=1))
+    grad_sent, gate_sent, grad_weight_in, grad_weight_back, combined_rows = expert_layer(
+        sequence_number,
+        planes,
+        mixed_low,
+        grad_arrived[:, MODEL_WIDTH:],
+        spreader,
+        jnp.transpose(
+            grad_arrived[:, :MODEL_WIDTH].reshape(planes * slots, chunks, wide), (1, 0, 2)
+        ),
+        jnp.pad(full_router, ((0, 0), (0, -devices % 128))),
+        gate_up_weight[0],
+        down_weight[0],
+    )
     output = (hidden1 + combine(combined_rows)).astype(jnp.bfloat16)
 
     grad_result = cotangent[0].astype(jnp.float32)
@@ -744,14 +1115,13 @@
     logits = jnp.dot(mixed_low, full_router, preferred_element_type=jnp.float32)
     gates = masked_softmax(logits, own_mask)
     grad_gates = (
-        grad_sent[:, MODEL_WIDTH : MODEL_WIDTH + devices]
-        + grad_sent[:, MODEL_WIDTH + devices : MODEL_WIDTH + 2 * devices]
+        gate_sent[:, :devices] + gate_sent[:, devices : 2 * devices]
     )
     grad_logits = (
         gates * (grad_gates - jnp.sum(gates * grad_gates, axis=-1, keepdims=True))
     ).astype(jnp.bfloat16)
-    grad_mixed = grad_sent[:, :MODEL_WIDTH] + outer_cols(grad_logits, full_router)
-    grad_router_w = inner_rows(mixed_low, grad_logits)
+    grad_mixed = grad_sent + outer_cols(grad_logits, full_router)
+    grad_router_t = inner_rows(grad_logits, mixed_low)
     _, pull_two = jax.vjp(rms_norm, hidden1, gain_two)
     grad_hidden_norm, grad_gain_two = pull_two(grad_mixed)
     grad_hidden1 = grad_result + grad_hidden_norm
@@ -798,35 +1168,40 @@
     grad_residual_norm, grad_gain_one = pull_one(normed_total)
     grad_input = grad_hidden1 + grad_residual_norm
 
+    chips = planes // 2
+
+    def by_chip(values):
+        columns = values.reshape(-1, sequence_number, chips, values.shape[-1] // devices * 2)
+        columns = jnp.pad(columns, ((0, 0),) * 3 + ((0, 2 * shard - columns.shape[-1]),))
+        return jnp.transpose(columns, (1, 2, 0, 3))
+
     small = jnp.concatenate(
         [
-            grad_gain_one.reshape(devices, shard),
-            grad_gain_two.reshape(devices, shard),
-            gain_totals[0].reshape(devices, small_shard),
-            gain_totals[1].reshape(devices, small_shard),
-            grad_router_w.reshape(devices, shard * devices),
+            by_chip(grad_router_t),
+            by_chip(grad_gain_two),
+            by_chip(grad_gain_one),
+            by_chip(gain_totals[0]),
+            by_chip(gain_totals[1]),
+            jnp.zeros((sequence_number, chips, 4, 2 * shard), jnp.float32),
         ],
-        axis=1,
-    )
-    small = jnp.pad(small, ((0, 0), (0, small_rows * 128 - small_width)))
-    small = lax.psum_scatter(
-        small.reshape(devices * small_rows, 128), ("seq", "dp"), scatter_dimension=0, tiled=True
-    ).reshape(-1)
-    cut = 0
-    pieces = []
-    for width in (shard, shard, small_shard, small_shard, shard * devices):
-        pieces.append(small[cut : cut + width])
-        cut += width
+        axis=2,
+    )
+    small = small_sums(sequence_number, chips, small)
+    core = lax.rem(member, 2)
+    small_core = lax.dynamic_slice_in_dim(small, core * shard, shard, 1)
+    small_gains = lax.dynamic_slice_in_dim(
+        small[devices + 2 : devices + 4, : 2 * small_shard], core * small_shard, small_shard, 1
+    )
     return (
         output[None],
         grad_input[None],
-        pieces[0],
-        pieces[2],
-        pieces[3],
+        small_core[devices + 1],
+        small_gains[0],
+        small_gains[1],
         shard_qkv,
         shard_out,
-        pieces[1],
-        pieces[4].reshape(shard, devices),
+        small_core[devices],
+        small_core[:devices].T,
         grad_weight_in[None],
         grad_weight_back[None],
     )

time: 853 us -> 754 us (0.88)
  Pallas kernels: 124 us -> 328 us
  waiting for transfers between devices: 346 us -> 147 us
  matrix products: 113 us -> 35.2 us
  blocking collectives: 155 us -> 93.9 us
  local copies, waits for them, and re-layouts: 42.9 us -> 83.1 us
    pallas_call x0 -> x2, Pallas kernels: none -> 182 us  [the longest x1 163 us: expert_layer(): pl.pallas_call(functools.partial(expert_kernel, count, planes, tokens, sl...]
    reduce_scatter x1 -> x0, waiting for transfers between devices: 132 us -> none  [body(): lax.psum_scatter(small.reshape(devices * small_rows, 128), ('seq', 'dp'),...]
    all_to_all x1 -> x0, blocking collectives: 61.1 us -> none  [combine(): lax.all_to_all(rows.reshape(planes, slots, width), 'dp', split_axis=0, co...]
    all_to_all x2 -> x1, waiting for transfers between devices: 50.6 us -> 0.01 us  [dispatch(): lax.all_to_all(sent.reshape(planes, slots, rows.shape[-1]), 'dp', split_a...]
    all_gather x1, waiting for transfers between devices: 12.7 us -> 63.1 us  [body(): lax.all_gather(own_part, 'dp', axis=1, tiled=True)]
    all_gather x1 -> x0, waiting for transfers between devices: 45.4 us -> none  [body(): mixed_full = lax.all_gather(mixed_low, 'seq', axis=0, tiled=True)]
    dot_general x5 -> x2, matrix products: 39.2 us -> 7.94 us  [inner_rows(): lax.dot_general(left, right, (((0,), (0,)), ((), ())), preferred_element_...]
    dot_general x5 -> x1, matrix products: 37.4 us -> 7.54 us  [combine(): jnp.dot(spreader, back, preferred_element_type=jnp.float32)]
  transfers between devices with their start and end apart: 12 -> 8, of which waited for: 8 -> 4; matrix products, arithmetic and copies ran while one was open for 17% -> 14% of each run, Pallas kernels for 15% -> 22%
where the time goes in v3:
time: 754 us; the launch traced here: 745 us
  Pallas kernels  328 us (44%)
  waiting for transfers between devices  147 us (19%)
  blocking collectives  93.9 us (12%)
  local copies, waits for them, and re-layouts  83.1 us (11%)
  matrix products  35.2 us (5%)
  other arithmetic  32 us (4%)
  between operations  16.1 us (2%)
  starting transfers between devices  9.62 us (1%)
    pallas_call x1, Pallas kernels, expert_layer(): pl.pallas_call(functools.partial(expert_kernel, count, planes, tokens, sl...  163 us
    pallas_call x1, Pallas kernels, attention_backward(): pl.pallas_call(functools.partial(backward_kernel, count, planes, tokens,...  146 us
    all_gather x1, waiting for transfers between devices, body(): lax.all_gather(own_part, 'dp', axis=1, tiled=True)  63.1 us
    all_gather x1, blocking collectives, body(): packed = lax.all_gather(packed, ('seq', 'dp'), axis=0, tiled=True)  42.9 us
    all_to_all x1, waiting for transfers between devices, combine(): back = lax.all_to_all(rows, 'dp', split_axis=1, concat_axis=1, tiled=True)  41.5 us
    all_to_all x1, blocking collectives, body(): lax.all_to_all(column_send, 'seq', split_axis=0, concat_axis=0, tiled=True)  37.6 us
    all_gather x1, waiting for transfers between devices, body(): out_rows = lax.all_gather(out_weight, 'dp', axis=0, tiled=True)  22.5 us
    unnamed x203, local copies, waits for them, and re-layouts  18.8 us
  transfers between devices with their start and end apart: 8, of which 4 were waited for; matrix products, arithmetic and copies ran while one was open for 14% of the time, Pallas kernels for 22%

profile of v3, /device:TPU:0, one launch (start us, length us, event | category | flops | bytes accessed | tf_op | source)
XLA Modules:
  0.0 745.3 jit_solution(12178892986908487697)
XLA Ops:
  8.0 0.7 all-gather.12.cloned.1.call-update
  9.2 37.6 %all_to_all.15 = bf16[4,64,1280]{2,1,0:T(8,128)(2,1)} all-to-all(bf16[4,64,1280]{2,1,0:T(8,128)(2,1)S(1)} %maximum_bitcast_fusion), channel_id=1, replica_groups=mesh['seq'=4,'dp'=8] {'seq'}, dimensions={0} | all-to-all | bytes 1310720 | tf_op jit(solution)/shard_map/all_to_all | solution.py:1033
  48.0 42.9 %all_gather.19 = bf16[1024,128]{1,0:T(8,128)(2,1)S(1)} all-gather(bf16[32,128]{1,0:T(8,128)(2,1)S(1)} %pad_bitcast_fusion), channel_id=1, replica_groups=mesh['seq'=4,'dp'=8] {'seq','dp'}, dimensions={0}, use_global_device_ids=true | all-gather | bytes 270336 | tf_op jit(solution)/shard_map/all_gather | solution.py:1006
  91.0 0.7 slice_convert_fusion.2
  92.4 13.3 %all-gather.1 = s32[1,512,8]{1,2,0:T(8,128)S(1)} all-gather(s32[1,128,8]{1,2,0:T(8,128)S(1)} %copy-done.87), channel_id=3, replica_groups=mesh['seq'=4,'dp'=8] {'seq'}, dimensions={1}, use_global_device_ids=true | all-gather | bytes 20480 | tf_op jit(solution)/shard_map/all_gather | solution.py:1037
  106.6 1.8 fusion.34
  108.4 7.7 %convolution_convert_fusion = bf16[1152,2176]{1,0:T(8,128)(2,1)} fusion(bf16[512,32]{1,0:T(8,128)(2,1)S(1)} %copy.152, bf16[512,2048]{1,0:T(8,128)(2,1)} %bitcast.202, s32[1152]{0:T(1024)S(1)} %fusion.42, s32[512]{0:T(512)S(1)} %bitcast.199, s32[512]{0:T(512)S(1)} %bitcast.181, s32[512]{0:T(512)S(1)} %bitcast.184, s32[512]{0:T(512)S(1)} %bitcast.187, ...), kind=kOutput, calls=%fused_computation | convolution fusion | flops 2581413888 | bytes 7173632 | tf_op jit(solution)/shard_map/dot_general | solution.py:888
  116.2 4.6 all-to-all-start.1
  121.0 2.4 fusion.2
  124.1 63.1 %all-gather.8.cloned.1.call-done = bf16[4,512,1280]{2,1,0:T(8,128)(2,1)} async-done(((bf16[4,64,1280]{2,1,0:T(8,128)(2,1)}), bf16[4,512,1280]{2,1,0:T(8,128)(2,1)}) %all-gather.8.cloned.1.call-update) | async-done | bytes 5242896 | tf_op jit(solution)/shard_map/all_gather | solution.py:1034
  187.2 5.4 fusion.67
  192.5 1.5 copy-done.3
  194.0 1.6 slice.150
  195.6 2.1 copy.125
  197.7 1.8 copy.126
  199.5 1.2 multiply_reduce_fusion.4
  201.1 1.1 multiply_bitcast_fusion
  202.2 1.2 fusion.28
  203.4 0.7 multiply_multiply_fusion
  204.2 0.8 subtract_convert_fusion
  205.0 2.3 fusion
  207.3 1.8 exponential_reduce_fusion
  209.1 3.8 fusion.12.heads_hbm
  212.9 0.7 copy.130
  213.7 22.5 %all-gather.10.cloned.1.call-done.out_rows_hbm = bf16[1024,2048]{1,0:T(8,128)(2,1)} async-done(((bf16[128,2048]{1,0:T(8,128)(2,1)}), bf16[1024,2048]{1,0:T(8,128)(2,1)}) %all-gather.10.cloned.1.call-update) | async-done | bytes 4194320 | tf_op jit(solution)/shard_map/all_gather | solution.py:1035
  236.2 5.9 convolution_convert_fusion.2
  243.3 1.0 pad.27.router_hbm
  244.4 3.2 fusion.62.spreader_hbm
  247.7 1.8 slice.164.masks_ref
  249.4 5.2 slice.165
  254.7 6.6 copy.134
  261.3 6.7 copy.135
  268.0 18.2 %reduce-scatter.3.cloned.1.call-done = bf16[128,2048]{1,0:T(8,128)(2,1)} async-done(((bf16[512,2048]{1,0:T(8,128)(2,1)}), bf16[128,2048]{1,0:T(8,128)(2,1)}) %reduce-scatter.3.cloned.1.call-update) | async-done | bytes 524304 | tf_op jit(solution)/shard_map/reduce_scatter | solution.py:1094
  286.2 1.3 multiply_reduce_fusion.3
  287.5 2.0 multiply_convert_fusion.mixed_ref
  289.6 163.4 %expert_layer.1 = (f32[128,2048]{1,0:T(8,128)}, f32[128,128]{1,0:T(8,128)}, f32[2048,1536]{1,0:T(8,128)}, f32[768,2048]{1,0:T(8,128)}, bf16[4,8,144,512]{3,2,1,0:T(8,128)(2,1)}) custom-call(bf16[128,2048]{1,0:T(8,128)(2,1)} %multiply_convert_fusion.mixed_ref, bf16[1152,128]{1,0:T(8,128)(2,1)} %slice.164.masks_ref, bf16[512,1152]{1,0:T(8,128)(2,1)} %fusion.62.spreader_hbm, ...), custom_call_target="tpu_custom_call" | custom-call | tf_op jit(solution)/shard_map/expert_layer/pallas_call | solution.py:720
  452.9 5.0 copy.136
  457.9 4.7 all-to-all-start.2
  463.7 1.0 pad_maximum_fusion.3
  464.7 3.4 copy.141
  468.7 3.4 copy.142
  472.2 1.0 fusion.37
  473.3 0.7 pad_maximum_fusion.2.pair_hbm
  474.0 1.5 fusion.30.query_hbm
  475.9 41.5 %all-to-all-done.2 = bf16[4,8,144,512]{3,2,0,1:T(8,128)(2,1)} async-done(((bf16[4,8,144,512]{3,2,0,1:T(8,128)(2,1)}), bf16[4,8,144,512]{3,2,0,1:T(8,128)(2,1)}, u32[]{:S(2)}, u32[]{:S(2)}) %all-to-all-start.2) | async-done | bytes 4718624 | tf_op jit(solution)/shard_map/all_to_all | solution.py:1069
  517.4 4.9 copy.137
  522.5 6.6 copy.138
  529.3 7.5 %convolution_convert_fusion.1 = bf16[512,2048]{1,0:T(8,128)(2,1)} fusion(bf16[1152,2048]{0,1:T(8,128)(2,1)} %bitcast.162, s32[1152]{0:T(1024)S(1)} %copy-done.39, s32[512]{0:T(512)S(1)} %bitcast.201, s32[512]{0:T(512)S(1)} %bitcast.183, s32[512]{0:T(512)S(1)} %bitcast.186, s32[512]{0:T(512)S(1)} %bitcast.189, s32[512]{0:T(512)S(1)} %bitcast.192, ...), kind=kOutput, calls=%fused_computation.14 | convolution fusion | flops 2422276096 | bytes 6845952 | tf_op jit(solution)/shard_map/dot_general | solution.py:1073
  538.0 1.9 multiply_reduce_fusion.1
  539.9 1.3 fusion.61.branch_ref
  541.2 146.2 %attention_backward.1 = (f32[128,2048]{1,0:T(8,128)}, f32[128,2048]{1,0:T(8,128)}, bf16[4,64,1280]{2,1,0:T(8,128)(2,1)}, f32[8,128]{1,0:T(8,128)}) custom-call(bf16[128,2048]{1,0:T(8,128)(2,1)} %fusion.61.branch_ref, bf16[1024,2048]{1,0:T(8,128)(2,1)} %all-gather.10.cloned.1.call-done.out_rows_hbm, bf16[2048,1280]{1,0:T(8,128)(2,1)} %bitcast.160, ...), custom_call_target="tpu_custom_call" | custom-call | tf_op jit(solution)/shard_map/attention_backward/pallas_call | solution.py:410
  687.4 1.7 slice.168
  689.2 1.2 convert_element_type.234
  690.6 0.9 reshape.484
  691.5 1.0 copy.165
  692.6 0.8 slice_reduce_fusion
  694.0 1.4 concatenate.35.own_ref
  695.4 18.7 %small_sums.1 = f32[40,128]{1,0:T(8,128)} custom-call(f32[4,4,40,128]{3,2,1,0:T(8,128)} %concatenate.35.own_ref), custom_call_target="tpu_custom_call" | custom-call | tf_op jit(solution)/shard_map/small_sums/pallas_call | solution.py:825
  714.8 1.1 reduce_sum.161
  718.6 1.2 pad_maximum_fusion
  719.7 3.4 fusion.18
  723.1 1.0 copy.170
  724.1 11.3 %copy.171 = f32[1,2048,1536]{2,1,0:T(8,128)} copy(f32[1,2048,1536]{2,1,0:T(8,128)} %bitcast.152) | data formatting | bytes 25165824
  735.4 2.7 copy.172
  (287 shorter events, 13.5 us)
Async XLA Ops:
  7.2 101.2 %all-gather.14.cloned.1.call-start = ((), (), s32[]{:S(2)}) async-start(), calls=%async_computation.10 | async-start | bytes 2621440 | tf_op jit(solution)/shard_map/all_gather | solution.py:1077
  7.9 113.0 %all-gather.12.cloned.1.call-start = ((), (), s32[]{:S(2)}) async-start(), calls=%async_computation.9 | async-start | bytes 2621440 | tf_op jit(solution)/shard_map/all_gather | solution.py:1080
  8.7 178.5 %all-gather.8.cloned.1.call-start = ((), (), s32[]{:S(2)}) async-start(), calls=%async_computation.5 | async-start | bytes 5898240 | tf_op jit(solution)/shard_map/all_gather | solution.py:1034
  9.0 38.6 %copy-start.84 = (bf16[64,32]{0,1:T(8,128)(2,1)S(1)}, bf16[64,32]{0,1:T(8,128)(2,1)}, u32[]{:S(2)}) copy-start(bf16[64,32]{0,1:T(8,128)(2,1)} %param.20) | copy-start | bytes 12292
  9.0 38.8 %copy-start.92 = (bf16[64]{0:T(256)(128)(2,1)S(1)}, bf16[64]{0:T(256)(128)(2,1)}, u32[]{:S(2)}) copy-start(bf16[64]{0:T(256)(128)(2,1)} %param.14) | copy-start | bytes 388
  9.1 38.8 %copy-start.93 = (bf16[64]{0:T(256)(128)(2,1)S(1)}, bf16[64]{0:T(256)(128)(2,1)}, u32[]{:S(2)}) copy-start(bf16[64]{0:T(256)(128)(2,1)} %param.19) | copy-start | bytes 388
  9.1 38.8 %copy-start.94 = (bf16[4]{0:T(256)(128)(2,1)S(1)}, bf16[4]{0:T(256)(128)(2,1)}, u32[]{:S(2)}) copy-start(bf16[4]{0:T(256)(128)(2,1)} %param.15) | copy-start | bytes 28
  9.1 38.8 %copy-start.95 = (bf16[4]{0:T(256)(128)(2,1)S(1)}, bf16[4]{0:T(256)(128)(2,1)}, u32[]{:S(2)}) copy-start(bf16[4]{0:T(256)(128)(2,1)} %param.16) | copy-start | bytes 28
  9.1 83.3 %copy-start.87 = (s32[1,128,8]{1,2,0:T(8,128)S(1)}, s32[1,128,8]{1,2,0:T(8,128)}, u32[]{:S(2)}) copy-start(s32[1,128,8]{1,2,0:T(8,128)} %param.13) | copy-start | bytes 12292
  46.9 189.3 %all-gather.10.cloned.1.call-start = ((), (), s32[]{:S(2)}) async-start(), calls=%async_computation.6 | async-start | bytes 4718592 | tf_op jit(solution)/shard_map/all_gather | solution.py:1035
  47.5 68.7 %copy-start.42 = (f32[512]{0:T(512)}, f32[512]{0:T(512)S(1)}, u32[]{:S(2)}) copy-start(f32[512]{0:T(512)S(1)} %iota_convert_fusion) | copy-start | bytes 6148
  47.5 68.6 %copy-start.60 = (pred[1152]{0:T(1024)(128)(4,1)}, pred[1152]{0:T(1024)(128)(4,1)S(1)}, u32[]{:S(2)}) copy-start(pred[1152]{0:T(1024)(128)(4,1)S(1)} %get-tuple-element.286) | copy-start | bytes 3460
  47.5 68.6 %copy-start.63 = (pred[1152]{0:T(1024)(128)(4,1)}, pred[1152]{0:T(1024)(128)(4,1)S(1)}, u32[]{:S(2)}) copy-start(pred[1152]{0:T(1024)(128)(4,1)S(1)} %get-tuple-element.287) | copy-start | bytes 3460
  47.5 68.6 %copy-start.66 = (pred[1152]{0:T(1024)(128)(4,1)}, pred[1152]{0:T(1024)(128)(4,1)S(1)}, u32[]{:S(2)}) copy-start(pred[1152]{0:T(1024)(128)(4,1)S(1)} %get-tuple-element.284) | copy-start | bytes 3460
  47.6 68.6 %copy-start.69 = (pred[1152]{0:T(1024)(128)(4,1)}, pred[1152]{0:T(1024)(128)(4,1)S(1)}, u32[]{:S(2)}) copy-start(pred[1152]{0:T(1024)(128)(4,1)S(1)} %get-tuple-element.285) | copy-start | bytes 3460
  47.6 68.6 %copy-start.72 = (pred[1152]{0:T(1024)(128)(4,1)}, pred[1152]{0:T(1024)(128)(4,1)S(1)}, u32[]{:S(2)}) copy-start(pred[1152]{0:T(1024)(128)(4,1)S(1)} %get-tuple-element.282) | copy-start | bytes 3460
  47.6 68.6 %copy-start.75 = (pred[1152]{0:T(1024)(128)(4,1)}, pred[1152]{0:T(1024)(128)(4,1)S(1)}, u32[]{:S(2)}) copy-start(pred[1152]{0:T(1024)(128)(4,1)S(1)} %get-tuple-element.283) | copy-start | bytes 3460
  47.6 68.6 %copy-start.78 = (pred[1152]{0:T(1024)(128)(4,1)}, pred[1152]{0:T(1024)(128)(4,1)S(1)}, u32[]{:S(2)}) copy-start(pred[1152]{0:T(1024)(128)(4,1)S(1)} %get-tuple-element.280) | copy-start | bytes 3460
  47.6 68.6 %copy-start.81 = (pred[1152]{0:T(1024)(128)(4,1)}, pred[1152]{0:T(1024)(128)(4,1)S(1)}, u32[]{:S(2)}) copy-start(pred[1152]{0:T(1024)(128)(4,1)S(1)} %get-tuple-element.281) | copy-start | bytes 3460
  47.7 68.5 %copy-start.37 = (s32[1152]{0:T(1024)}, s32[1152]{0:T(1024)S(1)}, u32[]{:S(2)}) copy-start(s32[1152]{0:T(1024)S(1)} %fusion.42) | copy-start | bytes 13828
  106.2 17.2 %copy-start.31 = (f32[2048]{0:T(1024)}, f32[2048]{0:T(1024)S(1)}, u32[]{:S(2)}) copy-start(f32[2048]{0:T(1024)S(1)} %reshape.487) | copy-start | bytes 24580
  106.4 9.8 %copy-start.88 = (f32[64]{0:T(128)}, f32[64]{0:T(128)S(1)}, u32[]{:S(2)}) copy-start(f32[64]{0:T(128)S(1)} %negate_power_fusion) | copy-start | bytes 772
  106.6 137.7 %copy-start.44 = (s32[512,1]{0,1:T(1,128)}, s32[512,1]{0,1:T(1,128)S(1)}, u32[]{:S(2)}) copy-start(s32[512,1]{0,1:T(1,128)S(1)} %get-tuple-element.260) | copy-start | bytes 6148
  106.6 137.7 %copy-start.46 = (s32[512,1]{0,1:T(1,128)}, s32[512,1]{0,1:T(1,128)S(1)}, u32[]{:S(2)}) copy-start(s32[512,1]{0,1:T(1,128)S(1)} %get-tuple-element.261) | copy-start | bytes 6148
  106.6 137.7 %copy-start.48 = (s32[512,1]{0,1:T(1,128)}, s32[512,1]{0,1:T(1,128)S(1)}, u32[]{:S(2)}) copy-start(s32[512,1]{0,1:T(1,128)S(1)} %get-tuple-element.262) | copy-start | bytes 6148
  106.6 137.7 %copy-start.50 = (s32[512,1]{0,1:T(1,128)}, s32[512,1]{0,1:T(1,128)S(1)}, u32[]{:S(2)}) copy-start(s32[512,1]{0,1:T(1,128)S(1)} %get-tuple-element.263) | copy-start | bytes 6148
  106.6 137.7 %copy-start.52 = (s32[512,1]{0,1:T(1,128)}, s32[512,1]{0,1:T(1,128)S(1)}, u32[]{:S(2)}) copy-start(s32[512,1]{0,1:T(1,128)S(1)} %get-tuple-element.264) | copy-start | bytes 6148
  106.6 137.7 %copy-start.54 = (s32[512,1]{0,1:T(1,128)}, s32[512,1]{0,1:T(1,128)S(1)}, u32[]{:S(2)}) copy-start(s32[512,1]{0,1:T(1,128)S(1)} %get-tuple-element.265) | copy-start | bytes 6148
  106.6 137.7 %copy-start.56 = (s32[512,1]{0,1:T(1,128)}, s32[512,1]{0,1:T(1,128)S(1)}, u32[]{:S(2)}) copy-start(s32[512,1]{0,1:T(1,128)S(1)} %get-tuple-element.266) | copy-start | bytes 6148
  106.6 137.7 %copy-start.58 = (s32[512,1]{0,1:T(1,128)}, s32[512,1]{0,1:T(1,128)S(1)}, u32[]{:S(2)}) copy-start(s32[512,1]{0,1:T(1,128)S(1)} %get-tuple-element.267) | copy-start | bytes 6148
  108.4 95.7 %copy-start.22 = (f32[512,64]{1,0:T(8,128)}, f32[512,64]{1,0:T(8,128)S(1)}, u32[]{:S(2)}) copy-start(f32[512,64]{1,0:T(8,128)S(1)} %get-tuple-element.270) | copy-start | bytes 393220
  116.2 131.5 %all-to-all-start.1 = ((bf16[8,144,2176]{2,1,0:T(8,128)(2,1)}), bf16[8,144,2176]{2,1,0:T(8,128)(2,1)}, u32[]{:S(2)}, u32[]{:S(2)}) async-start(bf16[8,144,2176]{2,1,0:T(8,128)(2,1)} %bitcast.161), calls=%async_computation.2 | async-start | bytes 10027008 | tf_op jit(solution)/shard_map/all_to_all | solution.py:1064
  120.9 165.3 %reduce-scatter.3.cloned.1.call-start = ((), (), s32[]{:S(2)}) async-start(), calls=%async_computation.7 | async-start | bytes 2621440 | tf_op jit(solution)/shard_map/reduce_scatter | solution.py:1094
  124.1 68.4 %copy-start.17 = (bf16[512,2048]{1,0:T(8,128)(2,1)}, bf16[512,2048]{1,0:T(8,128)(2,1)S(1)}, u32[]{:S(2)}) copy-start(bf16[512,2048]{1,0:T(8,128)(2,1)S(1)} %fusion.4.normed_hbm) | copy-start | bytes 6291460
  212.9 29.2 %copy-start.20 = (bf16[8,512,128]{2,1,0:T(8,128)(2,1)}, bf16[8,512,128]{2,1,0:T(8,128)(2,1)S(1)}, u32[]{:S(2)}) copy-start(bf16[8,512,128]{2,1,0:T(8,128)(2,1)S(1)} %fusion.12.heads_hbm) | copy-start | bytes 3145732
  242.9 44.6 %copy-start.29 = (f32[2048]{0:T(1024)}, f32[2048]{0:T(1024)S(1)}, u32[]{:S(2)}) copy-start(f32[2048]{0:T(1024)S(1)} %reshape.490) | copy-start | bytes 24580
  243.2 11.4 %copy-start.14 = (bf16[2048,32]{1,0:T(8,128)(2,1)}, bf16[2048,32]{1,0:T(8,128)(2,1)S(1)}, u32[]{:S(2)}) copy-start(bf16[2048,32]{1,0:T(8,128)(2,1)S(1)} %reshape.480) | copy-start | bytes 393220
  261.3 24.9 %copy-start = (bf16[1,128,2048]{2,1,0:T(8,128)(2,1)S(1)}, bf16[1,128,2048]{2,1,0:T(8,128)(2,1)}, u32[]{:S(2)}) copy-start(bf16[1,128,2048]{2,1,0:T(8,128)(2,1)} %param.12) | copy-start | bytes 1572868
  457.9 5.8 copy-start.23
  457.9 5.8 copy-start.27
  457.9 59.5 %all-to-all-start.2 = ((bf16[4,8,144,512]{3,2,0,1:T(8,128)(2,1)}), bf16[4,8,144,512]{3,2,0,1:T(8,128)(2,1)}, u32[]{:S(2)}, u32[]{:S(2)}) async-start(bf16[4,8,144,512]{3,2,0,1:T(8,128)(2,1)} %copy.136), calls=%async_computation.3 | async-start | bytes 9437184 | tf_op jit(solution)/shard_map/all_to_all | solution.py:1069
  462.6 257.1 %reduce-scatter.5.cloned.1.call-start = ((), (), s32[]{:S(2)}) async-start(), calls=%async_computation.8 | async-start | bytes 2621440 | tf_op jit(solution)/shard_map/reduce_scatter | solution.py:1074
  522.3 6.8 copy-start.39
  522.3 6.8 copy-start.45
  522.3 6.8 copy-start.47
  522.3 6.8 copy-start.49
  522.3 6.8 copy-start.51
  522.3 6.8 copy-start.53
  522.4 6.8 copy-start.55
  522.4 6.8 copy-start.57
  522.4 6.8 copy-start.59
  522.4 6.8 copy-start.62
  522.4 6.8 copy-start.65
  522.4 6.8 copy-start.68
  522.4 6.8 copy-start.71
  522.4 6.8 copy-start.74
  522.4 6.8 copy-start.77
  522.4 6.8 copy-start.80
  522.5 6.8 copy-start.83
  529.3 7.8 %copy-start.28 = (f32[128,128]{1,0:T(8,128)S(1)}, f32[128,128]{1,0:T(8,128)}, u32[]{:S(2)}) copy-start(f32[128,128]{1,0:T(8,128)} %get-tuple-element.232) | copy-start | bytes 196612
  687.4 6.1 copy-start.21
  687.4 6.1 copy-start.32
  723.1 12.3 %slice-start = ((s8[6291456]{0:T(1024)(128)(4,1)}), s8[4194304]{0:T(1024)(128)(4,1)S(1)}, s32[]{:S(2)}) async-start(s8[6291456]{0:T(1024)(128)(4,1)} %bitcast.155), calls=%async_computation.11 | async-start | bytes 8388608
  724.1 11.3 %slice-start.1 = ((s8[6291456]{0:T(1024)(128)(4,1)}), s8[2097152]{0:T(1024)(128)(4,1)S(1)}, s32[]{:S(2)}) async-start(s8[6291456]{0:T(1024)(128)(4,1)} %bitcast.155), calls=%async_computation.12 | async-start | bytes 4194304
  (44 other events, 115.5 us)
Sparse Core Ops, SparseCore 0:
  9.6 57.9 all-gather.13
  69.2 45.2 all-gather.11
  116.4 70.7 all-gather.7
  188.9 47.2 all-gather.9
  242.3 43.8 reduce-scatter.2
  537.0 53.4 reduce-scatter.4

commit v4 on v3

--- a/solution.py
+++ b/solution.py
@@ -1,6 +1,7 @@
 import functools
 import jax
 import jax.numpy as jnp
+import numpy as np
 from jax import lax
 from jax.experimental import pallas as pl
 from jax.experimental.pallas import tpu as pltpu
@@ -174,14 +175,15 @@
 def backward_kernel(
     count, planes, tokens, heads, shard,
     branch_ref, out_rows_hbm, own_cols_hbm, normed_hbm, heads_hbm, query_hbm, pair_hbm,
-    proj_hbm, lse_ref, turn_cos_ref, turn_sin_ref, gain_ref,
-    normed_total, out_total, columns_out, gain_total,
+    proj_hbm, spreader_hbm, combined_hbm, lse_ref, turn_cos_ref, turn_sin_ref, gain_ref,
+    normed_total, out_total, columns_out, gain_total, mixed_total, mixed_arrived,
     out_rows, own_cols, normed, heads_low, queries, pair, proj, local_sems,
     branch_full, ag_send, ag_recv,
     grad_heads, grad_proj, grad_pair,
     grad_out, out_pair, out_far, out_sems,
     grad_cols, col_pair, col_far, col_sums, col_sems,
     normed_part, normed_sums, rs_send, rs_recv, z_sems,
+    spreader, mixed_rows, mixed_sums, mix_send, mix_recv, mix_local, ms_send, ms_recv,
 ):
     place = lax.axis_index("seq")
     member = lax.axis_index("dp")
@@ -205,6 +207,7 @@
                 (proj_hbm, proj),
                 (own_cols_hbm, own_cols),
                 (normed_hbm, normed),
+                (spreader_hbm, spreader),
             ]
         )
     ]
@@ -214,19 +217,31 @@
 
     far_chips = [lax.rem(chip + k, chips) for k in range(1, chips)]
     far_places = [lax.rem(place + k, count) for k in range(1, count)]
-    greet(
-        [(place, partner)]
-        + [(place, 2 * other + core) for other in far_chips]
-        + [(other, member) for other in far_places]
-    )
+    others = [(j, lax.rem(member + j, planes)) for j in range(1, planes)]
+    greet([(place, other) for _, other in others] + [(other, member) for other in far_places])
 
     line = (count, place, member, branch_full, ag_send, ag_recv)
     line_gather_step(0, *line)
+
+    def mixed_copy(j, other):
+        return remote(
+            combined_hbm.at[:, other], mixed_arrived.at[:, member], mix_send.at[j], mix_recv.at[j],
+            (place, other),
+        )
+
+    for j, other in others:
+        mixed_copy(j, other).start()
+    mixed_own = pltpu.make_async_copy(
+        combined_hbm.at[:, member], mixed_arrived.at[:, member], mix_local.at[0]
+    )
+    mixed_own.start()
     for load in loads:
         load.wait()
 
     def head_gradients(block):
-        partial_heads = dot_nt(branch_full[block], out_rows[...]).astype(jnp.bfloat16)
+        partial_heads = dot_nt(
+            branch_full[block], out_rows[...].reshape(query_columns, MODEL_WIDTH)
+        ).astype(jnp.bfloat16)
         for head in range(heads):
             grad_heads[head, pl.ds(pl.multiple_of(block * tokens, tokens), tokens), :] = (
                 partial_heads[:, head * HEAD_SIZE : (head + 1) * HEAD_SIZE]
@@ -279,13 +294,15 @@
     block_rows = min(256, length)
 
     def unprepare(grad, raw, gain):
-        turned = grad * turn_cos_ref[...] + pltpu.roll(grad, HEAD_SIZE // 2, 1) * turn_sin_ref[...]
+        turned = grad * turn_cos_ref[...] + pltpu.roll(grad, HEAD_SIZE // 2, 1) * -turn_sin_ref[...]
         inverse = lax.rsqrt(jnp.mean(raw * raw, axis=-1, keepdims=True) + EPSILON)
         unit = raw * inverse
         gain_part = jnp.sum(turned * unit, axis=0, keepdims=True)
         turned = turned * gain
         middle = jnp.mean(turned * unit, axis=-1, keepdims=True)
         return inverse * (turned - unit * middle), gain_part
+
+    key_turned = jnp.transpose(pair[0].astype(jnp.float32)).astype(jnp.bfloat16)
 
     def one_head(head, carry):
         lse = lse_ref[head]
@@ -305,14 +322,37 @@
             grad_scores = (probs * (grad_probs - delta)).astype(jnp.bfloat16)
             grad_pair[0, :high, :] += dot_nn(grad_scores, query) * scale
             grad_pair[1, :high, :] += dot_nn(probs.astype(jnp.bfloat16), grad)
-            grads.append(dot_tn(grad_scores, key) * scale)
+            grads.append(jnp.transpose(dot_nn(key_turned[:, :high], grad_scores)) * scale)
         grad_query = jnp.concatenate(grads, axis=0)
         grad_raw, gain_part = unprepare(grad_query, proj[head], gain_ref[0:1, :])
         gain_total[0:1, :] += gain_part
         grad_proj[head] = grad_raw.astype(jnp.bfloat16)
         return carry
 
-    lax.fori_loop(0, heads, one_head, 0)
+    lax.fori_loop(0, heads // 2, one_head, 0)
+
+    for j, other in others:
+        mixed_copy(j, other).wait_recv()
+    mixed_own.wait()
+    line_gather_end(*line)
+    chunks, _, slots, wide = mixed_arrived.shape
+
+    def mixed_load(c):
+        return pltpu.make_async_copy(mixed_arrived.at[c], mixed_rows.at[c % 2], mix_local.at[1 + c % 2])
+
+    mixed_load(0).start()
+    for c in range(chunks):
+        mixed_load(c).wait()
+        if c + 1 < chunks:
+            mixed_load(c + 1).start()
+        part = dot_nn(spreader[...], mixed_rows[c % 2].reshape(planes * slots, wide))
+        branch_full[:, :, c * wide : (c + 1) * wide] = part.astype(jnp.bfloat16).reshape(
+            count, tokens, wide
+        )
+    mixed_line = (count, place, member, branch_full, mixed_sums, ms_send, ms_recv)
+    line_sum_step(0, *mixed_line)
+    lax.fori_loop(heads // 2, heads, one_head, 0)
+    line_sum_step(1, *mixed_line)
     grad_raw, gain_part = unprepare(grad_pair[0], proj[heads], gain_ref[1:2, :])
     gain_total[1:2, :] += gain_part
     grad_proj[heads] = grad_raw.astype(jnp.bfloat16)
@@ -321,7 +361,8 @@
 
     for block in range(count):
         normed_part[block] = dot_nt(
-            grad_rows[block * tokens : (block + 1) * tokens, :], own_cols[...]
+            grad_rows[block * tokens : (block + 1) * tokens, :],
+            own_cols[...].reshape(MODEL_WIDTH, grad_rows.shape[-1]),
         ).astype(jnp.bfloat16)
     sums = (count, place, member, normed_part, normed_sums, rs_send, rs_recv)
     line_sum_step(0, *sums)
@@ -352,6 +393,8 @@
     for k in range(1, chips):
         col_far_copy(k).start()
 
+    for step in range(2, count - 1):
+        line_sum_step(step, *mixed_line)
     if count > 2:
         line_sum_step(1, *sums)
 
@@ -380,7 +423,10 @@
         z_copy(k).start()
     columns_out[place] = col_sums[place]
 
+    line_sum_end(*mixed_line, mixed_total)
     line_sum_end(*sums, normed_total)
+    for j, other in others:
+        mixed_copy(j, other).wait_send()
     for k in range(1, count):
         z_copy(k).wait_recv()
     for k in range(1, count):
@@ -391,12 +437,11 @@
     for k in range(1, chips):
         out_far_copy(k).wait_send()
         col_far_copy(k).wait_send()
-    line_gather_end(*line)
 
 
 def attention_backward(
     count, planes, heads, shard, branch, out_rows, own_cols, normed, heads_low, queries, pair, proj,
-    lse, turn_cos, turn_sin, gains,
+    spreader, combined, lse, turn_cos, turn_sin, gains,
 ):
     tokens = branch.shape[0]
     length = count * tokens
@@ -414,9 +459,11 @@
             jax.ShapeDtypeStruct((out_block, MODEL_WIDTH), jnp.float32),
             jax.ShapeDtypeStruct((count, shard, width), low),
             jax.ShapeDtypeStruct((8, HEAD_SIZE), jnp.float32),
+            jax.ShapeDtypeStruct((tokens, MODEL_WIDTH), jnp.float32),
+            jax.ShapeDtypeStruct(combined.shape, low),
         ),
-        in_specs=[vmem] + [anywhere] * 7 + [vmem] * 4,
-        out_specs=(vmem,) * 4,
+        in_specs=[vmem] + [anywhere] * 9 + [vmem] * 4,
+        out_specs=(vmem,) * 5 + (anywhere,),
         scratch_shapes=[
             pltpu.VMEM(out_rows.shape, low),
             pltpu.VMEM(own_cols.shape, low),
@@ -425,7 +472,7 @@
             pltpu.VMEM(queries.shape, low),
             pltpu.VMEM(pair.shape, low),
             pltpu.VMEM(proj.shape, jnp.float32),
-            dma((7,)),
+            dma((8,)),
             pltpu.VMEM((count, tokens, MODEL_WIDTH), low),
             dma((2, count)),
             dma((2, count)),
@@ -446,12 +493,466 @@
             dma((2, count)),
             dma((2, count)),
             dma((2, count)),
+            pltpu.VMEM(spreader.shape, low),
+            pltpu.VMEM((2,) + combined.shape[1:], low),
+            pltpu.VMEM((count + 1, tokens, MODEL_WIDTH), low),
+            dma((planes,)),
+            dma((planes,)),
+            dma((3,)),
+            dma((2, count)),
+            dma((2, count)),
         ],
         compiler_params=pltpu.CompilerParams(
             collective_id=3, has_side_effects=True, vmem_limit_bytes=VMEM_BYTES
         ),
         name="attention_backward",
-    )(branch, out_rows, own_cols, normed, heads_low, queries, pair, proj, lse, turn_cos, turn_sin, gains)
+    )(
+        branch, out_rows, own_cols, normed, heads_low, queries, pair, proj, spreader, combined,
+        lse, turn_cos, turn_sin, gains,
+    )
+
+
+def forward_kernel(
+    count, planes, tokens, heads, shard, capacity, chunks,
+    hidden_ref, routes_ref, small_ref, router_ref, qkv_ref, out_ref, cotangent_ref,
+    turn_cos_ref, turn_sin_ref,
+    hidden1_ref, mixed_ref, lse_ref, gains_ref, spreader_ref,
+    router_out, own_cols_hbm, out_rows_hbm, normed_hbm, heads_hbm, query_hbm, pair_hbm, proj_hbm,
+    grad_hbm, masks_hbm,
+    column_send, own_cols, c_send, c_recv,
+    out_rows, o_send, o_recv,
+    hidden_full, h_send, h_recv,
+    gains_all, gz_send, gz_recv, gd_send, gd_recv,
+    router_all, rz_send, rz_recv, rd_send, rd_recv,
+    places_all, p_send, p_recv,
+    normed, proj, queries, pair, heads_low,
+    grad_full, dy_send, dy_recv,
+    grad_sent, d_send, d_recv, mask_sent, m_send, m_recv,
+    branch, sums, rs_send, rs_recv, local_sems,
+):
+    place = lax.axis_index("seq")
+    member = lax.axis_index("dp")
+    core = lax.rem(member, 2)
+    chip = member // 2
+    chips = planes // 2
+    partner = member + 1 - 2 * core
+    length = count * tokens
+    query_columns = heads * HEAD_SIZE
+    replicas = count // KEY_VALUE_HEADS
+    wide = MODEL_WIDTH // chunks
+    slots = grad_sent.shape[2]
+    rows = planes * slots
+    low = jnp.bfloat16
+    scale = HEAD_SIZE ** (-0.5)
+    far_places = [(k, lax.rem(place + k, count)) for k in range(1, count)]
+    far_chips = [(k, lax.rem(chip + k, chips)) for k in range(1, chips)]
+    others = [(j, lax.rem(member + j, planes)) for j in range(1, planes)]
+
+    hidden_full[place] = hidden_ref[...]
+    gains_all[place, member] = small_ref[...]
+    router_all[place, member] = router_ref[...]
+    for part in range(count):
+        head = part // replicas
+        keys = QUERY_HEADS * HEAD_SIZE + head * HEAD_SIZE
+        values = keys + KEY_VALUE_HEADS * HEAD_SIZE
+        column_send[part, :, :query_columns] = qkv_ref[
+            :, part * query_columns : (part + 1) * query_columns
+        ]
+        column_send[part, :, query_columns : query_columns + HEAD_SIZE] = qkv_ref[
+            :, keys : keys + HEAD_SIZE
+        ]
+        column_send[part, :, query_columns + HEAD_SIZE :] = qkv_ref[:, values : values + HEAD_SIZE]
+    lanes = lax.broadcasted_iota(jnp.int32, (tokens, places_all.shape[-1]), 1)
+    named = jnp.zeros(lanes.shape, jnp.float32)
+    for k in range(TOP):
+        named += jnp.where(routes_ref[:, k : k + 1] == lanes, 1.0, 0.0)
+    row_ids = lax.broadcasted_iota(jnp.int32, (tokens, tokens), 0)
+    col_ids = lax.broadcasted_iota(jnp.int32, (tokens, tokens), 1)
+    before = jnp.where(row_ids > col_ids, 1.0, 0.0).astype(low)
+    earlier = dot_nn(before, named.astype(low)) + (place * capacity).astype(jnp.float32)
+    places_all[place] = jnp.where(named > 0, earlier, -1.0).astype(low)
+    for c in range(chunks):
+        grad_full[c, place] = cotangent_ref[:, c * wide : (c + 1) * wide]
+
+    greet([(place, other) for _, other in others] + [(other, member) for _, other in far_places])
+
+    def column_copy(k, other):
+        return remote(
+            column_send.at[other], own_cols.at[place, member], c_send.at[0, k], c_recv.at[0, k],
+            (other, member),
+        )
+
+    def gain_line(k, other):
+        mine = gains_all.at[place, member]
+        return remote(mine, mine, gz_send.at[k], gz_recv.at[k], (other, member))
+
+    def router_line(k, other):
+        mine = router_all.at[place, member]
+        return remote(mine, mine, rz_send.at[k], rz_recv.at[k], (other, member))
+
+    def places_line(k, other):
+        mine = places_all.at[place]
+        return remote(mine, mine, p_send.at[k], p_recv.at[k], (other, member))
+
+    def out_copy(k, other):
+        return remote(
+            out_ref, out_rows.at[member], o_send.at[0, k], o_recv.at[0, k], (place, 2 * other + core)
+        )
+
+    def out_pair(k, other):
+        source = out_ref if k == 0 else out_rows.at[2 * other + core]
+        return remote(
+            source, out_rows.at[2 * other + core], o_send.at[1, k], o_recv.at[1, k], (place, partner)
+        )
+
+    def block_copy(k, other):
+        mine = own_cols.at[:, member]
+        return remote(mine, mine, c_send.at[1, k], c_recv.at[1, k], (place, 2 * other + core))
+
+    def block_pair(k, other):
+        block = own_cols.at[:, 2 * other + core]
+        return remote(block, block, c_send.at[2, k], c_recv.at[2, k], (place, partner))
+
+    for k, other in far_places:
+        gain_line(k, other).start()
+        column_copy(k, other).start()
+    for k, other in far_chips:
+        out_copy(k, other).start()
+    out_pair(0, chip).start()
+    hidden_line = (count, place, member, hidden_full, h_send, h_recv)
+    line_gather_step(0, *hidden_line)
+    for k, other in far_places:
+        places_line(k, other).start()
+        router_line(k, other).start()
+    own_cols[place, member] = column_send[place]
+    out_rows[member] = out_ref[...]
+
+    def gain_plane(j, other):
+        mine = gains_all.at[:, member]
+        return remote(mine, mine, gd_send.at[j], gd_recv.at[j], (place, other))
+
+    def router_plane(j, other):
+        mine = router_all.at[:, member]
+        return remote(mine, mine, rd_send.at[j], rd_recv.at[j], (place, other))
+
+    for k, other in far_places:
+        gain_line(k, other).wait_recv()
+    for j, other in others:
+        gain_plane(j, other).start()
+    for k, other in far_places:
+        column_copy(k, other).wait_recv()
+    for k, other in far_chips:
+        block_copy(k, other).start()
+    block_pair(0, chip).start()
+    line_gather_step(1, *hidden_line)
+
+    for k, other in far_places:
+        places_line(k, other).wait_recv()
+    experts = places_all.shape[-1]
+    pick_rows = lax.broadcasted_iota(jnp.int32, (experts, rows), 0)
+    pick_cols = lax.broadcasted_iota(jnp.int32, (experts, rows), 1)
+    slot_ids = lax.broadcasted_iota(jnp.int32, (length, rows), 1)
+    slot_base = jnp.zeros((length, rows), jnp.int32)
+    choose = jnp.zeros((experts, rows), jnp.float32)
+    for other in range(planes):
+        inside = (pick_cols >= other * slots) & (pick_cols < (other + 1) * slots)
+        choose += jnp.where(inside & (pick_rows == place * planes + other), 1.0, 0.0)
+        slot_base = jnp.where(slot_ids >= other * slots, other * slots, slot_base)
+    wanted = dot_nn(places_all[...].reshape(length, experts), choose.astype(low))
+    spreader_ref[...] = jnp.where(
+        wanted == (slot_ids - slot_base).astype(jnp.float32), 1.0, 0.0
+    ).astype(low)
+    mask_full = jnp.where(places_all[...].reshape(length, experts).astype(jnp.float32) >= 0, 1.0, 0.0)
+    mask_sent[...] = (
+        dot_tn(spreader_ref[...], mask_full.astype(low)).astype(low).reshape(mask_sent.shape)
+    )
+
+    for k, other in far_places:
+        router_line(k, other).wait_recv()
+    for j, other in others:
+        router_plane(j, other).start()
+
+    def mask_copy(j, other):
+        return remote(
+            mask_sent.at[other], masks_hbm.at[member], m_send.at[j], m_recv.at[j], (place, other)
+        )
+
+    for j, other in others:
+        mask_copy(j, other).start()
+    masks_own = pltpu.make_async_copy(mask_sent.at[member], masks_hbm.at[member], local_sems.at[0])
+    masks_own.start()
+
+    for k, other in far_chips:
+        out_copy(k, other).wait_recv()
+    for k, other in far_chips:
+        out_pair(k, lax.rem(chip + chips - k, chips)).start()
+    for step in range(2, count):
+        line_gather_step(step, *hidden_line)
+
+    def grad_line(c):
+        return (count, place, member, grad_full.at[c], dy_send.at[c], dy_recv.at[c])
+
+    def grad_copy(c, j, other):
+        return remote(
+            grad_sent.at[c, other], grad_hbm.at[c, member], d_send.at[c, j], d_recv.at[c, j], (place, other)
+        )
+
+    def grad_own(c):
+        return pltpu.make_async_copy(
+            grad_sent.at[c, member], grad_hbm.at[c, member], local_sems.at[16 + c]
+        )
+
+    def grad_tick(tick):
+        for c in range(chunks):
+            step = tick - c
+            if 0 <= step < count:
+                line_gather_step(step, *grad_line(c))
+            if step == count - 1:
+                picked = dot_tn(spreader_ref[...], grad_full[c].reshape(length, wide)).astype(low)
+                grad_sent[c] = picked.reshape(planes, slots, wide)
+                for j, other in others:
+                    grad_copy(c, j, other).start()
+                grad_own(c).start()
+
+    ticks = list(range(chunks + count - 1))
+    grad_tick(ticks.pop(0))
+
+    for j, other in others:
+        gain_plane(j, other).wait_recv()
+    per_row = HEAD_SIZE // shard
+    small_total = jnp.sum(gains_all[...].astype(jnp.float32), axis=(0, 1))
+    gain_rows = []
+    for row in range(2):
+        parts = []
+        for group in range(MODEL_WIDTH // HEAD_SIZE):
+            part = jnp.zeros((1, HEAD_SIZE), jnp.float32)
+            for index in range(group * per_row, (group + 1) * per_row):
+                part += gains_all[index // planes, index % planes, row : row + 1, :].astype(jnp.float32)
+            parts.append(part)
+        gain_rows.append(jnp.concatenate(parts, axis=1))
+    gains_ref[0:1, :] = gain_rows[0]
+    gains_ref[1:2, :] = gain_rows[1]
+    gain_query = small_total[2:3, :]
+    gain_key = small_total[3:4, :]
+    gains_ref[2:3, :HEAD_SIZE] = gain_query
+    gains_ref[3:4, :HEAD_SIZE] = gain_key
+
+    def normalize(values, gain):
+        return (
+            values
+            * lax.rsqrt(jnp.mean(values * values, axis=-1, keepdims=True) + EPSILON)
+            * gain
+        )
+
+    for block in range(count):
+        values = hidden_full[block].astype(jnp.float32)
+        normed[block * tokens : (block + 1) * tokens, :] = normalize(values, gain_rows[0]).astype(low)
+    stores = [pltpu.make_async_copy(normed, normed_hbm, local_sems.at[1])]
+    stores[-1].start()
+
+    for k, other in far_chips:
+        block_copy(k, other).wait_recv()
+    for k, other in far_chips:
+        block_pair(k, lax.rem(chip + chips - k, chips)).start()
+    block_pair(0, chip).wait_recv()
+    for k, other in far_chips:
+        block_pair(k, lax.rem(chip + chips - k, chips)).wait_recv()
+    weights = own_cols[...].reshape(MODEL_WIDTH, query_columns + 2 * HEAD_SIZE)
+    stores.append(pltpu.make_async_copy(own_cols, own_cols_hbm, local_sems.at[2]))
+    stores[-1].start()
+
+    def prepare(values, gain):
+        turned = normalize(values, gain)
+        return turned * turn_cos_ref[...] + pltpu.roll(turned, HEAD_SIZE // 2, 1) * turn_sin_ref[...]
+
+    paired = dot_nn(normed[...], weights[:, query_columns:])
+    proj[heads] = paired[:, :HEAD_SIZE]
+    proj[heads + 1] = paired[:, HEAD_SIZE:]
+    pair[0] = prepare(paired[:, :HEAD_SIZE], gain_key).astype(low)
+    pair[1] = paired[:, HEAD_SIZE:].astype(low)
+    projected = dot_nn(normed[...], weights[:, :query_columns])
+    for head in range(heads):
+        proj[head] = projected[:, head * HEAD_SIZE : (head + 1) * HEAD_SIZE]
+    value_turned = jnp.transpose(paired[:, HEAD_SIZE:]).astype(low)
+    stores.append(pltpu.make_async_copy(proj, proj_hbm, local_sems.at[3]))
+    stores[-1].start()
+    stores.append(pltpu.make_async_copy(pair, pair_hbm, local_sems.at[4]))
+    stores[-1].start()
+    block_rows = min(256, length)
+
+    def one_head(head, carry):
+        queries[head] = prepare(proj[head], gain_query).astype(low)
+        for block in range(length // block_rows):
+            begin, end = block * block_rows, (block + 1) * block_rows
+            scores = dot_nt(pair[0, :end, :], queries[head, begin:end, :]) * scale
+            key_ids = lax.broadcasted_iota(jnp.int32, (end, block_rows), 0)
+            query_ids = lax.broadcasted_iota(jnp.int32, (end, block_rows), 1) + begin
+            scores = jnp.where(key_ids <= query_ids, scores, FILLER)
+            top = jnp.max(scores, axis=0, keepdims=True)
+            powers = jnp.exp(scores - top)
+            total = jnp.sum(powers, axis=0, keepdims=True)
+            lse_ref[head, :, begin:end] = top + jnp.log(total)
+            probs = (powers * (1.0 / total)).astype(low)
+            mixed = dot_nn(value_turned[:, :end], probs)
+            heads_low[head, begin:end, :] = jnp.transpose(mixed).astype(low)
+        return carry
+
+    halves = 4
+    for part in range(halves):
+        lax.fori_loop(part * heads // halves, (part + 1) * heads // halves, one_head, 0)
+        if ticks:
+            grad_tick(ticks.pop(0))
+    stores.append(pltpu.make_async_copy(queries, query_hbm, local_sems.at[5]))
+    stores[-1].start()
+    stores.append(pltpu.make_async_copy(heads_low, heads_hbm, local_sems.at[6]))
+    stores[-1].start()
+
+    out_pair(0, chip).wait_recv()
+    for k, other in far_chips:
+        out_pair(k, lax.rem(chip + chips - k, chips)).wait_recv()
+    out_all = out_rows[...].reshape(query_columns, MODEL_WIDTH)
+    stores.append(pltpu.make_async_copy(out_rows, out_rows_hbm, local_sems.at[7]))
+    stores[-1].start()
+
+    def project(block, carry):
+        at = pl.ds(pl.multiple_of(block * tokens, tokens), tokens)
+        mixed = jnp.concatenate([heads_low[head, at, :] for head in range(heads)], axis=1)
+        branch[block] = dot_nn(mixed, out_all).astype(low)
+        return carry
+
+    lax.fori_loop(0, count, project, 0)
+    line = (count, place, member, branch, sums, rs_send, rs_recv)
+    for step in range(count - 1):
+        line_sum_step(step, *line)
+        for _ in range(-(-len(ticks) // (count - 1 - step))):
+            grad_tick(ticks.pop(0))
+    line_sum_end(*line, hidden1_ref)
+    hidden1 = hidden_ref[...].astype(jnp.float32) + hidden1_ref[...]
+    hidden1_ref[...] = hidden1
+    mixed_ref[...] = normalize(hidden1, gain_rows[1]).astype(low)
+
+    for j, other in others:
+        router_plane(j, other).wait_recv()
+    router_out[...] = router_all[...].reshape(router_out.shape)
+    for j, other in others:
+        mask_copy(j, other).wait_recv()
+        for c in range(chunks):
+            grad_copy(c, j, other).wait_recv()
+    for k, other in far_places:
+        gain_line(k, other).wait_send()
+        column_copy(k, other).wait_send()
+        places_line(k, other).wait_send()
+        router_line(k, other).wait_send()
+    for k, other in far_chips:
+        out_copy(k, other).wait_send()
+        block_copy(k, other).wait_send()
+        out_pair(k, other).wait_send()
+        block_pair(k, other).wait_send()
+    out_pair(0, chip).wait_send()
+    block_pair(0, chip).wait_send()
+    for j, other in others:
+        gain_plane(j, other).wait_send()
+        router_plane(j, other).wait_send()
+        mask_copy(j, other).wait_send()
+        for c in range(chunks):
+            grad_copy(c, j, other).wait_send()
+    for c in range(chunks):
+        grad_own(c).wait()
+        line_gather_end(*grad_line(c))
+    line_gather_end(*hidden_line)
+    masks_own.wait()
+    for store in stores:
+        store.wait()
+
+
+def attention_forward(
+    count, planes, heads, shard, capacity, slots, chunks,
+    hidden, routes, small, router, qkv, out_weight, cotangent, turn_cos, turn_sin,
+):
+    tokens = hidden.shape[0]
+    length = count * tokens
+    width = (heads + 2) * HEAD_SIZE
+    chips = planes // 2
+    rows = planes * slots
+    wide = MODEL_WIDTH // chunks
+    experts = router.shape[-1]
+    small_rows = small.shape[0]
+    out_block = out_weight.shape[0]
+    low, full = jnp.bfloat16, jnp.float32
+    vmem = pl.BlockSpec(memory_space=pltpu.VMEM)
+    anywhere = pl.BlockSpec(memory_space=pl.ANY)
+    dma = pltpu.SemaphoreType.DMA
+    shape = jax.ShapeDtypeStruct
+    return pl.pallas_call(
+        functools.partial(forward_kernel, count, planes, tokens, heads, shard, capacity, chunks),
+        out_shape=(
+            shape((tokens, MODEL_WIDTH), full),
+            shape((tokens, MODEL_WIDTH), low),
+            shape((heads, 1, length), full),
+            shape((8, MODEL_WIDTH), full),
+            shape((length, rows), low),
+            shape((MODEL_WIDTH, experts), low),
+            shape((count, planes, shard, width), low),
+            shape((planes, out_block, MODEL_WIDTH), low),
+            shape((length, MODEL_WIDTH), low),
+            shape((heads, length, HEAD_SIZE), low),
+            shape((heads, length, HEAD_SIZE), low),
+            shape((2, length, HEAD_SIZE), low),
+            shape((heads + 2, length, HEAD_SIZE), full),
+            shape((chunks, planes, slots, wide), low),
+            shape((planes, slots, experts), low),
+        ),
+        in_specs=[vmem] * 9,
+        out_specs=(vmem,) * 6 + (anywhere,) * 9,
+        scratch_shapes=[
+            pltpu.VMEM((count, shard, width), low),
+            pltpu.VMEM((count, planes, shard, width), low),
+            dma((3, max(count, chips))),
+            dma((3, max(count, chips))),
+            pltpu.VMEM((planes, out_block, MODEL_WIDTH), low),
+            dma((2, chips)),
+            dma((2, chips)),
+            pltpu.VMEM((count, tokens, MODEL_WIDTH), low),
+            dma((2, count)),
+            dma((2, count)),
+            pltpu.VMEM((count, planes, small_rows, HEAD_SIZE), low),
+            dma((count,)),
+            dma((count,)),
+            dma((planes,)),
+            dma((planes,)),
+            pltpu.VMEM((count, planes, shard, experts), low),
+            dma((count,)),
+            dma((count,)),
+            dma((planes,)),
+            dma((planes,)),
+            pltpu.VMEM((count, tokens, experts), low),
+            dma((count,)),
+            dma((count,)),
+            pltpu.VMEM((length, MODEL_WIDTH), low),
+            pltpu.VMEM((heads + 2, length, HEAD_SIZE), full),
+            pltpu.VMEM((heads, length, HEAD_SIZE), low),
+            pltpu.VMEM((2, length, HEAD_SIZE), low),
+            pltpu.VMEM((heads, length, HEAD_SIZE), low),
+            pltpu.VMEM((chunks, count, tokens, wide), low),
+            dma((chunks, 2, count)),
+            dma((chunks, 2, count)),
+            pltpu.VMEM((chunks, planes, slots, wide), low),
+            dma((chunks, planes)),
+            dma((chunks, planes)),
+            pltpu.VMEM((planes, slots, experts), low),
+            dma((planes,)),
+            dma((planes,)),
+            pltpu.VMEM((count, tokens, MODEL_WIDTH), low),
+            pltpu.VMEM((count + 1, tokens, MODEL_WIDTH), low),
+            dma((2, count)),
+            dma((2, count)),
+            dma((16 + chunks,)),
+        ],
+        compiler_params=pltpu.CompilerParams(
+            collective_id=1, has_side_effects=True, vmem_limit_bytes=VMEM_BYTES
+        ),
+        name="attention_forward",
+    )(hidden, routes, small, router, qkv, out_weight, cotangent, turn_cos, turn_sin)
 
 
 def expert_kernel(
@@ -711,7 +1212,7 @@
     length = count * tokens
     chunks, rows, wide = grad_rows.shape
     slots = rows // planes
-    extra = masks.shape[-1]
+    extra = -(-2 * count * planes // 128) * 128
     experts = router.shape[-1]
     low = jnp.bfloat16
     vmem = pl.BlockSpec(memory_space=pltpu.VMEM)
@@ -849,111 +1350,23 @@
     return values * lax.rsqrt(jnp.mean(values * values, axis=-1, keepdims=True) + EPSILON) * gain
 
 
-def rope_tables(positions, width):
-    half_width = width // 2
-    freqs = ROPE_BASE ** (-(jnp.arange(half_width, dtype=jnp.float32) * (2.0 / width)))
-    angles = positions[:, None] * freqs[None, :]
-    return (jnp.cos(angles), jnp.sin(angles))
-
-
-def rotate(values, cosine, sine_table):
-    half_width = values.shape[-1] // 2
-    first = values[..., :half_width]
-    second = values[..., half_width:]
-    cosine = cosine[:, None, :]
-    sine_table = sine_table[:, None, :]
-    return jnp.concatenate(
-        [first * cosine - second * sine_table, second * cosine + first * sine_table], axis=-1
-    )
-
-
-def prepare_heads(projected_rows, gain_query, gain_key, cosine, sine_table):
-    row_count = projected_rows.shape[0]
-    query_columns = projected_rows.shape[1] - 2 * HEAD_SIZE
-    queries = projected_rows[:, :query_columns].reshape(
-        row_count, query_columns // HEAD_SIZE, HEAD_SIZE
-    )
-    key_head = projected_rows[:, query_columns : query_columns + HEAD_SIZE].reshape(
-        row_count, 1, HEAD_SIZE
-    )
-    value_head = projected_rows[:, query_columns + HEAD_SIZE :]
-    queries = rotate(rms_norm(queries, gain_query), cosine, sine_table)
-    key_head = rotate(rms_norm(key_head, gain_key), cosine, sine_table).reshape(
-        row_count, HEAD_SIZE
-    )
-    return (queries, key_head, value_head)
+def turn_tables(length):
+    half = HEAD_SIZE // 2
+    freqs = np.float32(ROPE_BASE) ** (-(np.arange(half, dtype=np.float32) * np.float32(2 / HEAD_SIZE)))
+    angles = np.arange(length, dtype=np.float32)[:, None] * freqs[None, :]
+    cosine, sine = np.cos(angles), np.sin(angles)
+    return (
+        jnp.asarray(np.concatenate([cosine, cosine], axis=1), jnp.float32),
+        jnp.asarray(np.concatenate([-sine, sine], axis=1), jnp.float32),
+    )
 
 
 def inner_rows(left, right):
-    return lax.dot_general(
-        left, right, (((0,), (0,)), ((), ())), preferred_element_type=jnp.float32
-    )
+    return dot_tn(left, right)
 
 
 def outer_cols(left, right):
-    return lax.dot_general(
-        left, right, (((1,), (1,)), ((), ())), preferred_element_type=jnp.float32
-    )
-
-
-def block_slice(array, index, block_rows):
-    return lax.dynamic_slice_in_dim(array, index * block_rows, block_rows, 0)
-
-
-def block_scores(query_block, key_block, i, j, block_rows):
-    scores = jnp.einsum(
-        "qhd,kd->hqk", query_block, key_block, preferred_element_type=jnp.float32
-    ) * HEAD_SIZE ** (-0.5)
-    row_ids = i * block_rows + jnp.arange(block_rows)
-    col_ids = j * block_rows + jnp.arange(block_rows)
-    return jnp.where((row_ids[:, None] >= col_ids[None, :])[None], scores, FILLER)
-
-
-def attend_forward(queries, keys_in, values_in):
-    sequence_length, head_count = (queries.shape[0], queries.shape[1])
-    block_rows = min(QUERY_BLOCK, sequence_length)
-    block_count = sequence_length // block_rows
-
-    def one_block(i):
-        query_block = block_slice(queries, i, block_rows)
-
-        def max_step(j, carry):
-            row_top, row_total = carry
-            scores = block_scores(
-                query_block, block_slice(keys_in, j, block_rows), i, j, block_rows
-            )
-            new_top = jnp.maximum(row_top, jnp.max(scores, axis=-1))
-            row_total = row_total * jnp.exp(row_top - new_top) + jnp.sum(
-                jnp.exp(scores - new_top[..., None]), axis=-1
-            )
-            return (new_top, row_total)
-
-        start = (
-            jnp.full((head_count, block_rows), FILLER, jnp.float32),
-            jnp.zeros((head_count, block_rows), jnp.float32),
-        )
-        row_top, row_total = lax.fori_loop(0, i + 1, max_step, start)
-        log_totals = row_top + jnp.log(row_total)
-
-        def out_step(j, accum_out):
-            scores = block_scores(
-                query_block, block_slice(keys_in, j, block_rows), i, j, block_rows
-            )
-            probabilities = jnp.exp(scores - log_totals[..., None]).astype(jnp.bfloat16)
-            return accum_out + jnp.einsum(
-                "hqk,kd->qhd",
-                probabilities,
-                block_slice(values_in, j, block_rows),
-                preferred_element_type=jnp.float32,
-            )
-
-        accum_out = lax.fori_loop(
-            0, i + 1, out_step, jnp.zeros((block_rows, head_count, HEAD_SIZE), jnp.float32)
-        )
-        return (accum_out, log_totals)
-
-    outputs, log_totals = lax.map(one_block, jnp.arange(block_count))
-    return (outputs.reshape(sequence_length, head_count, HEAD_SIZE), log_totals)
+    return dot_nt(left, right)
 
 
 def masked_softmax(logits, mask):
@@ -984,134 +1397,69 @@
     devices = sequence_number * planes
     group = lax.axis_index("seq")
     member = lax.axis_index("dp")
-    per_device = QUERY_HEADS // sequence_number
-    query_columns = per_device * HEAD_SIZE
-    own_width = query_columns + 2 * HEAD_SIZE
+    index = group * planes + member
+    heads = QUERY_HEADS // sequence_number
+    query_columns = heads * HEAD_SIZE
     head_replicas = sequence_number // KEY_VALUE_HEADS
     capacity = (tokens * TOP * 9 + 8 * devices - 1) // (8 * devices)
     slots = -(-sequence_number * capacity // 16) * 16
     chunks = 4
-    wide = MODEL_WIDTH // chunks
     sequence_length = sequence_number * tokens
-    extra = -(-2 * devices // 128) * 128
-
     shard = norm1_gain.shape[0]
     small_shard = query_gain.shape[0]
-    small_width = 2 * shard + 2 * small_shard + shard * devices
-    small_rows = -(-small_width // 2048) * 16
-    packed = jnp.concatenate(
-        [norm1_gain, norm2_gain, query_gain, key_gain, router.reshape(-1)]
-    )
-    packed = jnp.pad(packed, (0, small_rows * 128 - small_width)).reshape(small_rows, 128)
-    packed = lax.all_gather(packed, ("seq", "dp"), axis=0, tiled=True)
-    packed = packed.reshape(devices, small_rows * 128)
-    cut = 0
-    pieces = []
-    for width in (shard, shard, small_shard, small_shard, shard * devices):
-        pieces.append(packed[:, cut : cut + width])
-        cut += width
-    gain_one = pieces[0].reshape(-1).astype(jnp.float32)
-    gain_two = pieces[1].reshape(-1).astype(jnp.float32)
-    gain_query = pieces[2].reshape(-1).astype(jnp.float32)
-    gain_key = pieces[3].reshape(-1).astype(jnp.float32)
-    full_router = pieces[4].reshape(MODEL_WIDTH, devices)
-
-    query_part = qkv_weight[:, : QUERY_HEADS * HEAD_SIZE].reshape(
-        shard, sequence_number, query_columns
-    )
-    paired_portion = jnp.repeat(
-        qkv_weight[:, QUERY_HEADS * HEAD_SIZE :].reshape(shard, 2, KEY_VALUE_HEADS, HEAD_SIZE),
-        head_replicas,
-        axis=2,
-    )
-    paired_portion = jnp.transpose(paired_portion, (0, 2, 1, 3)).reshape(
-        shard, sequence_number, 2 * HEAD_SIZE
-    )
-    column_send = jnp.transpose(
-        jnp.concatenate([query_part, paired_portion], axis=-1), (1, 0, 2)
-    )
-    own_part = lax.all_to_all(column_send, "seq", split_axis=0, concat_axis=0, tiled=True)
-    own_cols = lax.all_gather(own_part, "dp", axis=1, tiled=True).reshape(MODEL_WIDTH, own_width)
-    out_rows = lax.all_gather(out_weight, "dp", axis=0, tiled=True)
-
-    full_routes = lax.all_gather(routes[0], "seq", axis=0, tiled=True)
-    expert_ids = jnp.arange(devices, dtype=jnp.int32)
-    route_mask = jnp.sum(
-        (full_routes[:, :, None] == expert_ids[None, None, :]).astype(jnp.float32), axis=1
-    )
-    before = (
-        jnp.arange(tokens)[:, None] > jnp.arange(tokens)[None, :]
-    ).astype(jnp.bfloat16)
-    places = jnp.einsum(
-        "tu,sue->ste",
-        before,
-        route_mask.astype(jnp.bfloat16).reshape(sequence_number, tokens, devices),
-        preferred_element_type=jnp.float32,
-    ).astype(jnp.int32)
-    places = places + (jnp.arange(sequence_number, dtype=jnp.int32) * capacity)[:, None, None]
-    places = jnp.where(route_mask > 0, places.reshape(sequence_length, devices), -1)
-    plane_places = lax.dynamic_slice_in_dim(places, group * planes, planes, 1)
-    column_ids = jnp.arange(planes * slots, dtype=jnp.int32)
-    column_places = jnp.full((sequence_length, planes * slots), -2, jnp.int32)
-    for other in range(planes):
-        column_places = jnp.where(
-            (column_ids // slots == other)[None, :], plane_places[:, other : other + 1], column_places
-        )
-    spreader = (column_places == (column_ids % slots)[None, :]).astype(jnp.bfloat16)
-
-    def dispatch(rows):
-        sent = inner_rows(spreader, rows).astype(jnp.bfloat16)
-        return lax.all_to_all(
-            sent.reshape(planes, slots, rows.shape[-1]), "dp", split_axis=0, concat_axis=0, tiled=True
-        ).reshape(planes * slots, rows.shape[-1])
-
-    def combine(rows):
-        back = lax.all_to_all(rows, "dp", split_axis=1, concat_axis=1, tiled=True)
-        back = jnp.transpose(
-            back.reshape(chunks, planes * slots, wide), (1, 0, 2)
-        ).reshape(planes * slots, MODEL_WIDTH)
-        sums = jnp.dot(spreader, back, preferred_element_type=jnp.float32).astype(jnp.bfloat16)
-        return lax.psum_scatter(sums, "seq", scatter_dimension=0, tiled=True).astype(jnp.float32)
-
-    mask_columns = jnp.pad(route_mask.astype(jnp.bfloat16), ((0, 0), (0, extra - devices)))
-    cotangent_full = lax.all_gather(cotangent[0], "seq", axis=0, tiled=True)
-    grad_arrived = dispatch(jnp.concatenate([cotangent_full, mask_columns], axis=1))
-
-    hidden_full = lax.all_gather(hidden_in[0], "seq", axis=0, tiled=True)
+    lane_count = -(-devices // 128) * 128
+
+    def placed(values):
+        width = values.shape[0]
+        at = jnp.arange(HEAD_SIZE, dtype=jnp.int32) // width == index % (HEAD_SIZE // width)
+        return jnp.where(at, jnp.tile(values, HEAD_SIZE // width), jnp.zeros((), values.dtype))
+
+    small = jnp.stack([placed(value) for value in (norm1_gain, norm2_gain, query_gain, key_gain)])
+    small = jnp.pad(small, ((0, 12), (0, 0)))
+    turn_cos, turn_sin = turn_tables(sequence_length)
+    (
+        hidden1, mixed_low, lse, gains, spreader, full_router, own_cols, out_rows, normed_full,
+        heads_low, queries, pair, projected, grad_rows, masks,
+    ) = attention_forward(
+        sequence_number,
+        planes,
+        heads,
+        shard,
+        capacity,
+        slots,
+        chunks,
+        hidden_in[0],
+        routes[0],
+        small,
+        jnp.pad(router, ((0, 0), (0, lane_count - devices))),
+        qkv_weight,
+        out_weight,
+        cotangent[0],
+        turn_cos,
+        turn_sin,
+    )
+    gain_one, gain_two = gains[0], gains[1]
     residual = hidden_in[0].astype(jnp.float32)
-    normed_full = rms_norm(hidden_full.astype(jnp.float32), gain_one).astype(jnp.bfloat16)
-    cosine, sine_table = rope_tables(jnp.arange(sequence_length).astype(jnp.float32), HEAD_SIZE)
-    projected_rows = jnp.dot(normed_full, own_cols, preferred_element_type=jnp.float32)
-    queries, key_head, value_head = prepare_heads(
-        projected_rows, gain_query, gain_key, cosine, sine_table
-    )
-    query_heads = queries.astype(jnp.bfloat16)
-    key_heads = key_head.astype(jnp.bfloat16)
-    value_heads = value_head.astype(jnp.bfloat16)
-    out_full, log_totals = attend_forward(query_heads, key_heads, value_heads)
-    heads_low = out_full.astype(jnp.bfloat16).reshape(sequence_length, query_columns)
-    branch_part = jnp.dot(heads_low, out_rows, preferred_element_type=jnp.float32)
-    hidden1 = residual + lax.psum_scatter(
-        branch_part.astype(jnp.bfloat16), "seq", scatter_dimension=0, tiled=True
-    ).astype(jnp.float32)
-    mixed_low = rms_norm(hidden1, gain_two).astype(jnp.bfloat16)
+
     grad_sent, gate_sent, grad_weight_in, grad_weight_back, combined_rows = expert_layer(
         sequence_number,
         planes,
         mixed_low,
-        grad_arrived[:, MODEL_WIDTH:],
+        masks.reshape(planes * slots, lane_count),
         spreader,
-        jnp.transpose(
-            grad_arrived[:, :MODEL_WIDTH].reshape(planes * slots, chunks, wide), (1, 0, 2)
-        ),
-        jnp.pad(full_router, ((0, 0), (0, -devices % 128))),
+        grad_rows.reshape(chunks, planes * slots, MODEL_WIDTH // chunks),
+        full_router,
         gate_up_weight[0],
         down_weight[0],
     )
-    output = (hidden1 + combine(combined_rows)).astype(jnp.bfloat16)
-
     grad_result = cotangent[0].astype(jnp.float32)
-    own_mask = lax.dynamic_slice_in_dim(route_mask, group * tokens, tokens, 0)
+    own_mask = jnp.sum(
+        (routes[0][:, :, None] == jnp.arange(devices, dtype=jnp.int32)[None, None, :]).astype(
+            jnp.float32
+        ),
+        axis=1,
+    )
+    full_router = full_router[:, :devices]
     logits = jnp.dot(mixed_low, full_router, preferred_element_type=jnp.float32)
     gates = masked_softmax(logits, own_mask)
     grad_gates = (
@@ -1126,30 +1474,33 @@
     grad_hidden_norm, grad_gain_two = pull_two(grad_mixed)
     grad_hidden1 = grad_result + grad_hidden_norm
     grad_branch = grad_hidden1.astype(jnp.bfloat16)
-    normed_total, shard_out, column_sums, gain_totals = attention_backward(
+    out_block = query_columns // planes
+    heads_low = jnp.transpose(
+        heads_low.reshape(heads, sequence_length, HEAD_SIZE // out_block, out_block), (0, 2, 1, 3)
+    ).reshape(planes, sequence_length, out_block)
+    (
+        normed_total, shard_out, column_sums, gain_totals, mixed_total, _,
+    ) = attention_backward(
         sequence_number,
         planes,
-        per_device,
+        heads,
         shard,
         grad_branch,
         out_rows,
         own_cols,
         normed_full,
-        jnp.transpose(
-            heads_low.reshape(sequence_length, planes, query_columns // planes), (1, 0, 2)
-        ),
-        jnp.transpose(query_heads, (1, 0, 2)),
-        jnp.stack([key_heads, value_heads]),
-        jnp.transpose(
-            projected_rows.reshape(sequence_length, per_device + 2, HEAD_SIZE), (1, 0, 2)
-        ),
-        log_totals.reshape(-1, per_device, sequence_length // log_totals.shape[0])
-        .transpose(1, 0, 2)
-        .reshape(per_device, 1, sequence_length),
-        jnp.concatenate([cosine, cosine], axis=1),
-        jnp.concatenate([sine_table, -sine_table], axis=1),
-        jnp.pad(jnp.stack([gain_query, gain_key]), ((0, 6), (0, 0))),
-    )
+        heads_low,
+        queries,
+        pair,
+        projected,
+        spreader,
+        combined_rows,
+        lse,
+        turn_cos,
+        turn_sin,
+        gains[2:4, :HEAD_SIZE],
+    )
+    output = (hidden1 + mixed_total).astype(jnp.bfloat16)
     column_sums = column_sums.astype(jnp.float32)
     shard_query = jnp.transpose(column_sums[:, :, :query_columns], (1, 0, 2)).reshape(
         shard, QUERY_HEADS * HEAD_SIZE

time: 754 us -> 524 us (0.69)
  waiting for transfers between devices: 147 us -> 0 us
  Pallas kernels: 328 us -> 464 us
  blocking collectives: 93.9 us -> 0 us
  local copies, waits for them, and re-layouts: 83.1 us -> 28.7 us
  matrix products: 35.2 us -> 3.84 us
  other arithmetic: 32 us -> 15.4 us
  between operations: 16.1 us -> 1.38 us
  starting transfers between devices: 9.62 us -> 0 us
    pallas_call x0 -> x1, Pallas kernels: none -> 136 us  [attention_forward(): pl.pallas_call(functools.partial(forward_kernel, count, planes, tokens, h...]
    all_gather x4 -> x0, waiting for transfers between devices: 85.6 us -> none  [the longest x1 63.1 us: body(): lax.all_gather(own_part, 'dp', axis=1, tiled=True)]
    all_gather x2 -> x0, blocking collectives: 56.3 us -> none  [the longest x1 42.9 us: body(): packed = lax.all_gather(packed, ('seq', 'dp'), axis=0, tiled=True)]
    all_to_all x2 -> x0, waiting for transfers between devices: 41.5 us -> none  [the longest x1 41.5 us: combine(): back = lax.all_to_all(rows, 'dp', split_axis=1, concat_axis=1, tiled=True)]
    all_to_all x1 -> x0, blocking collectives: 37.6 us -> none  [body(): lax.all_to_all(column_send, 'seq', split_axis=0, concat_axis=0, tiled=True)]
    dot_general x9 -> x2, matrix products: 34.8 us -> 2.28 us  [the longest x1 2.05 us: dot_nt(): lax.dot_general(left, right, (((1,), (1,)), ((), ())), preferred_element_...]
    reduce_scatter x2 -> x0, waiting for transfers between devices: 18.2 us -> none  [the longest x1 18.2 us: body(): lax.psum_scatter(branch_part.astype(jnp.bfloat16), 'seq', scatter_dimensi...]
    slice x11 -> x2, local copies, waits for them, and re-layouts: 17.5 us -> 2.18 us  [the longest x1 1.25 us: body(): gains[2:4, :HEAD_SIZE]]
  transfers between devices with their start and end apart: 8 -> 0, of which waited for: 4 -> 0; matrix products, arithmetic and copies ran while one was open for 14% -> 0% of each run, Pallas kernels for 22% -> 0%
where the time goes in v4:
time: 524 us; the launch traced here: 514 us
  Pallas kernels  464 us (89%)
  local copies, waits for them, and re-layouts  28.7 us (5%)
  other arithmetic  15.4 us (3%)
    pallas_call x1, Pallas kernels, expert_layer(): pl.pallas_call(functools.partial(expert_kernel, count, planes, tokens, sl...  166 us
    pallas_call x1, Pallas kernels, attention_backward(): pl.pallas_call(functools.partial(backward_kernel, count, planes, tokens,...  148 us
    pallas_call x1, Pallas kernels, attention_forward(): pl.pallas_call(functools.partial(forward_kernel, count, planes, tokens, h...  136 us
    unnamed x26, local copies, waits for them, and re-layouts  17.7 us
    pallas_call x1, Pallas kernels, small_sums(): pl.pallas_call(functools.partial(small_kernel, count, chips), out_shape=j...  14.4 us

profile of v4, /device:TPU:0, one launch (start us, length us, event | category | flops | bytes accessed | tf_op | source)
XLA Modules:
  0.0 513.7 jit_solution(10158202170680398514)
XLA Ops:
  0.7 1.2 fusion.3
  1.9 0.7 tile.16
  2.6 0.1 tile.17
  2.7 0.7 tile.18
  3.3 0.1 tile.19
  3.4 0.7 tile.40
  4.1 0.1 tile.41
  4.2 0.7 tile.42
  4.9 0.1 tile.43
  5.0 0.6 fusion.18.small_ref
  5.6 0.8 copy.36
  6.4 0.6 pad.16.router_ref
  7.0 0.7 convert_reduce_fusion
  7.7 0.1 copy.38
  7.8 1.4 copy.35
  9.2 136.1 %attention_forward.1 = (f32[128,2048]{1,0:T(8,128)}, bf16[128,2048]{1,0:T(8,128)(2,1)}, f32[8,1,512]{2,1,0:T(1,128)}, f32[8,2048]{1,0:T(8,128)}, bf16[512,1152]{...) custom-call(bf16[128,2048]{1,0:T(8,128)(2,1)} %bitcast.52, ...), custom_call_target="tpu_custom_call" | custom-call | tf_op jit(solution)/shard_map/attention_forward/pallas_call | solution.py:886
  145.4 1.4 multiply_reduce_fusion.2
  146.8 1.3 slice.52.gain_ref
  148.0 0.9 fusion.22
  148.9 1.6 fusion.23
  150.5 0.2 fusion.11
  150.7 0.0 copy-start.4
  150.7 165.8 %expert_layer.1 = (f32[128,2048]{1,0:T(8,128)}, f32[128,128]{1,0:T(8,128)}, f32[2048,1536]{1,0:T(8,128)}, f32[768,2048]{1,0:T(8,128)}, bf16[4,8,144,512]{3,2,1,0:T(8,128)(2,1)}) custom-call(bf16[128,2048]{1,0:T(8,128)(2,1)} %get-tuple-element.37.mixed_ref, bf16[1152,128]{1,0:T(8,128)(2,1)} %bitcast.63, bf16[512,1152]{1,0:T(8,128)(2,1)} %get-tuple-element.39.spreader_hbm, ...), custom_call_target="tpu_custom_call" | custom-call | tf_op jit(solution)/shard_map/expert_layer/pallas_call | solution.py:1221
  316.6 0.0 copy-start.3
  316.6 0.0 copy-start
  316.6 1.2 multiply_reduce_fusion.3
  317.8 1.1 multiply_convert_fusion
  318.8 0.0 copy-done.4
  318.9 2.0 multiply_reduce_fusion
  320.9 0.0 copy-done.3
  320.9 0.0 copy-start.1
  320.9 0.2 fusion.24
  321.2 0.2 reshape.208
  321.4 0.1 copy.47
  321.5 0.4 copy-done.1
  321.9 0.0 copy-done
  321.9 2.2 fusion.21.branch_ref
  324.1 147.9 %attention_backward.1 = (f32[128,2048]{1,0:T(8,128)}, f32[128,2048]{1,0:T(8,128)}, bf16[4,64,1280]{2,1,0:T(8,128)(2,1)}, f32[8,128]{1,0:T(8,128)}, f32[128,2048]...) custom-call(bf16[128,2048]{1,0:T(8,128)(2,1)} %fusion.21.branch_ref, bf16[8,128,2048]{2,1,0:T(8,128)(2,1)} %get-tuple-element.45.out_rows_hbm, ...), custom_call_target="tpu_custom_call" | custom-call | tf_op jit(solution)/shard_map/attention_backward/pallas_call | solution.py:455
  471.9 0.8 slice_reduce_fusion
  472.7 0.1 reshape_squeeze.7
  472.8 0.1 reshape_squeeze.6
  472.9 0.0 copy-done.2
  472.9 1.6 fusion.6
  474.6 1.4 concatenate.6.own_ref
  476.0 14.4 %small_sums.1 = f32[40,128]{1,0:T(8,128)} custom-call(f32[4,4,40,128]{3,2,1,0:T(8,128)} %concatenate.6.own_ref), custom_call_target="tpu_custom_call" | custom-call | tf_op jit(solution)/shard_map/small_sums/pallas_call | solution.py:1326
  490.4 0.0 copy-start.7
  490.5 3.9 fusion.2
  494.4 0.0 copy-done.7
  494.4 0.6 dynamic-slice_bitcast_fusion.1
  495.0 0.7 dynamic-slice_bitcast_fusion
  495.7 0.1 constant_dynamic-slice_fusion
  495.8 0.5 slice_bitcast_fusion.1
  496.3 0.0 copy-done.5
  496.3 0.1 reduce_sum.112
  496.5 0.2 copy.42
  496.6 0.1 reshape.210
  496.7 0.0 copy-start.6
  496.8 0.1 convert_element_type.34
  496.9 0.1 slice_bitcast_fusion
  497.0 0.1 copy.45
  497.1 1.2 pad_maximum_fusion
  498.3 1.0 copy.51
  499.2 11.3 %copy.52 = f32[1,2048,1536]{2,1,0:T(8,128)} copy(f32[1,2048,1536]{2,1,0:T(8,128)} %bitcast.51) | data formatting | bytes 25165824
  510.5 2.7 copy.53
  (20 shorter events, 0.1 us)
Async XLA Ops:
  150.7 168.1 %copy-start.4 = (bf16[2048,128]{1,0:T(8,128)(2,1)S(1)}, bf16[2048,128]{1,0:T(8,128)(2,1)}, u32[]{:S(2)}) copy-start(bf16[2048,128]{1,0:T(8,128)(2,1)} %get-tuple-element.41.router_hbm) | copy-start | bytes 1572868
  316.6 4.3 copy-start.3
  316.6 5.3 %copy-start = (f32[128,2048]{1,0:T(8,128)S(1)}, f32[128,2048]{1,0:T(8,128)}, u32[]{:S(2)}) copy-start(f32[128,2048]{1,0:T(8,128)} %get-tuple-element.36) | copy-start | bytes 3145732
  320.9 1.0 copy-start.1
  324.1 148.8 %copy-start.2 = (bf16[1,128,2048]{2,1,0:T(8,128)(2,1)S(1)}, bf16[1,128,2048]{2,1,0:T(8,128)(2,1)}, u32[]{:S(2)}) copy-start(bf16[1,128,2048]{2,1,0:T(8,128)(2,1)} %param.14) | copy-start | bytes 1572868
  474.6 21.7 %copy-start.5 = (bf16[4,64,1280]{2,1,0:T(8,128)(2,1)S(1)}, bf16[4,64,1280]{2,1,0:T(8,128)(2,1)}, u32[]{:S(2)}) copy-start(bf16[4,64,1280]{2,1,0:T(8,128)(2,1)} %get-tuple-element.57) | copy-start | bytes 1966084
  490.4 4.0 copy-start.7
  496.7 1.5 copy-start.6
  498.3 12.2 %slice-start = ((s8[6291456]{0:T(1024)(128)(4,1)}), s8[4194304]{0:T(1024)(128)(4,1)S(1)}, s32[]{:S(2)}) async-start(s8[6291456]{0:T(1024)(128)(4,1)} %bitcast.53), calls=%async_computation | async-start | bytes 8388608
  499.2 11.3 %slice-start.1 = ((s8[6291456]{0:T(1024)(128)(4,1)}), s8[2097152]{0:T(1024)(128)(4,1)S(1)}, s32[]{:S(2)}) async-start(s8[6291456]{0:T(1024)(128)(4,1)} %bitcast.53), calls=%async_computation.1 | async-start | bytes 4194304

commit v5 on v4

v5 whole, which is shorter than its diff:
```python
import functools
import jax
import jax.numpy as jnp
import numpy as np
from jax import lax
from jax.experimental import pallas as pl
from jax.experimental.pallas import tpu as pltpu
from jax.sharding import PartitionSpec as P


MODEL_WIDTH = 2048
QUERY_HEADS = 32
KEY_VALUE_HEADS = 4
HEAD_SIZE = 128
FF = 768
TOP = 8


EPSILON = 1e-06
ROPE_BASE = 1000000.0
FILLER = -1e30
QUERY_BLOCK = 512


MESH = pl.DeviceIdType.MESH
VMEM_BYTES = 63 * 1024 * 1024


def dot_nn(left, right):
    return jnp.dot(left, right, preferred_element_type=jnp.float32)


def dot_nt(left, right):
    return lax.dot_general(
        left, right, (((1,), (1,)), ((), ())), preferred_element_type=jnp.float32
    )


def dot_tn(left, right):
    return lax.dot_general(
        left, right, (((0,), (0,)), ((), ())), preferred_element_type=jnp.float32
    )


def greet(peers):
    barrier = pltpu.get_barrier_semaphore()
    for peer in peers:
        pl.semaphore_signal(barrier, inc=1, device_id=peer, device_id_type=MESH)
    pl.semaphore_wait(barrier, len(peers))


def remote(source, target, send_sem, recv_sem, device):
    return pltpu.make_async_remote_copy(
        src_ref=source,
        dst_ref=target,
        send_sem=send_sem,
        recv_sem=recv_sem,
        device_id=device,
        device_id_type=MESH,
    )


def line_gather_step(step, count, place, column, blocks, send_sems, recv_sems):
    right, left = place + 1, place - 1
    if step > 0:

        @pl.when(place - step >= 0)
        def _():
            block = blocks.at[place - step]
            remote(block, block, send_sems.at[0, step], recv_sems.at[0, step], (right, column)).wait_recv()

        @pl.when(place + step < count)
        def _():
            block = blocks.at[place + step]
            remote(block, block, send_sems.at[1, step], recv_sems.at[1, step], (left, column)).wait_recv()

    if step < count - 1:

        @pl.when((place - step >= 0) & (place + 1 < count))
        def _():
            block = blocks.at[place - step]
            remote(block, block, send_sems.at[0, step], recv_sems.at[0, step + 1], (right, column)).start()

        @pl.when((place + step < count) & (place - 1 >= 0))
        def _():
            block = blocks.at[place + step]
            remote(block, block, send_sems.at[1, step], recv_sems.at[1, step + 1], (left, column)).start()


def line_gather_end(count, place, column, blocks, send_sems, recv_sems):
    for step in range(count - 1):

        @pl.when((place - step >= 0) & (place + 1 < count))
        def _():
            block = blocks.at[place - step]
            remote(block, block, send_sems.at[0, step], recv_sems.at[0, step], (place + 1, column)).wait_send()

        @pl.when((place + step < count) & (place - 1 >= 0))
        def _():
            block = blocks.at[place + step]
            remote(block, block, send_sems.at[1, step], recv_sems.at[1, step], (place - 1, column)).wait_send()


def line_sum_step(step, count, place, column, own, sums, send_sems, recv_sems):
    turn = step - place
    last = count - 1 - turn

    @pl.when((turn >= 0) & (last > place))
    def _():
        block = sums.at[last]

        @pl.when(place > 0)
        def _():
            remote(block, block, send_sems.at[0, last], recv_sems.at[0, last], (place, column)).wait_recv()
            sums[last] = (
                sums[last].astype(jnp.float32) + own[last].astype(jnp.float32)
            ).astype(jnp.bfloat16)

        @pl.when(place == 0)
        def _():
            sums[last] = own[last]

        remote(block, block, send_sems.at[0, last], recv_sems.at[0, last], (place + 1, column)).start()

    first = step - (count - 1 - place)

    @pl.when((first >= 0) & (first < place))
    def _():
        block = sums.at[first]

        @pl.when(place < count - 1)
        def _():
            remote(block, block, send_sems.at[1, first], recv_sems.at[1, first], (place, column)).wait_recv()
            sums[first] = (
                sums[first].astype(jnp.float32) + own[first].astype(jnp.float32)
            ).astype(jnp.bfloat16)

        @pl.when(place == count - 1)
        def _():
            sums[first] = own[first]

        target = sums.at[jnp.where(first == place - 1, count, first)]
        remote(block, target, send_sems.at[1, first], recv_sems.at[1, first], (place - 1, column)).start()


def line_sum_end(count, place, column, own, sums, send_sems, recv_sems, total):
    total[...] = own[place].astype(jnp.float32)

    @pl.when(place > 0)
    def _():
        block = sums.at[place]
        remote(block, block, send_sems.at[0, place], recv_sems.at[0, place], (place, column)).wait_recv()
        total[...] += sums[place].astype(jnp.float32)

    @pl.when(place < count - 1)
    def _():
        block = sums.at[count]
        remote(block, block, send_sems.at[1, place], recv_sems.at[1, place], (place, column)).wait_recv()
        total[...] += sums[count].astype(jnp.float32)

    for step in range(count - 1):
        last = count - 1 - step

        @pl.when(last > place)
        def _():
            block = sums.at[last]
            remote(block, block, send_sems.at[0, last], recv_sems.at[0, last], (place + 1, column)).wait_send()

        @pl.when(step < place)
        def _():
            block = sums.at[step]
            remote(block, block, send_sems.at[1, step], recv_sems.at[1, step], (place - 1, column)).wait_send()


def backward_kernel(
    count, planes, tokens, heads, shard,
    branch_ref, grad_hidden_ref, hidden_ref, gains_ref, router_ref,
    out_rows_hbm, own_cols_hbm, normed_hbm, heads_hbm, query_hbm, pair_hbm,
    proj_hbm, picker_hbm, combined_hbm, lse_ref, turn_cos_ref, turn_sin_ref,
    grad_input_ref, out_total, columns_out, mixed_total, router_total, gain_total, mixed_arrived,
    out_rows, own_cols, normed, heads_low, queries, pair, proj, picker, local_sems,
    branch_full, ag_send, ag_recv,
    grad_heads, grad_proj, grad_pair, gain_parts,
    grad_out, out_pair, out_far, out_sems,
    grad_cols, col_pair, col_far, col_sums, col_sems,
    normed_sums, rs_send, rs_recv, z_sems,
    mixed_rows, mixed_part, mixed_sums, mix_send, mix_recv, mix_local, ms_send, ms_recv,
    router_line, router_sum, router_chip, router_pair, router_sems,
    gain_own, gain_line, gain_chip, gain_pair, gain_sems,
):
    place = lax.axis_index("seq")
    member = lax.axis_index("dp")
    core = lax.rem(member, 2)
    chip = member // 2
    chips = planes // 2
    partner = member + 1 - 2 * core
    length = count * tokens
    query_columns = heads * HEAD_SIZE
    width = query_columns + 2 * HEAD_SIZE
    out_block = query_columns // planes
    scale = HEAD_SIZE ** (-0.5)
    chunks = mixed_part.shape[0]
    wide = MODEL_WIDTH // chunks
    slots = mixed_rows.shape[1]
    low = jnp.bfloat16

    loads = [
        pltpu.make_async_copy(source, target, local_sems.at[index])
        for index, (source, target) in enumerate(
            [
                (out_rows_hbm, out_rows),
                (query_hbm, queries),
                (pair_hbm, pair),
                (heads_hbm, heads_low),
                (proj_hbm, proj),
                (own_cols_hbm, own_cols),
                (normed_hbm, normed),
                (picker_hbm, picker),
            ]
        )
    ]
    for load in loads:
        load.start()
    branch_full[place] = branch_ref[...]

    far_chips = [(k, lax.rem(chip + k, chips)) for k in range(1, chips)]
    far_places = [(k, lax.rem(place + k, count)) for k in range(1, count)]
    others = [(j, lax.rem(member + j, planes)) for j in range(1, planes)]
    greet([(place, other) for _, other in others] + [(other, member) for _, other in far_places])

    line = (count, place, member, branch_full, ag_send, ag_recv)
    line_gather_step(0, *line)

    def mixed_copy(c, j, other):
        part = pl.ds(c * wide, wide)
        return remote(
            combined_hbm.at[other, :, part], mixed_arrived.at[member, :, part],
            mix_send.at[c, j], mix_recv.at[c, j], (place, other),
        )

    for c in range(chunks):
        for j, other in others:
            mixed_copy(c, j, other).start()
    mixed_own = pltpu.make_async_copy(
        combined_hbm.at[member], mixed_arrived.at[member], mix_local.at[0]
    )
    mixed_own.start()
    for load in loads:
        load.wait()

    def head_gradients(block):
        partial_heads = dot_nt(
            branch_full[block], out_rows[...].reshape(query_columns, MODEL_WIDTH)
        ).astype(low)
        for head in range(heads):
            grad_heads[head, pl.ds(pl.multiple_of(block * tokens, tokens), tokens), :] = (
                partial_heads[:, head * HEAD_SIZE : (head + 1) * HEAD_SIZE]
            )

    def gather(step):
        line_gather_step(step, *line)

        @pl.when(place - step >= 0)
        def _():
            head_gradients(place - step)

        @pl.when(place + step < count)
        def _():
            head_gradients(place + step)

    def mixed_line(c):
        return (count, place, member, mixed_part.at[c], mixed_sums.at[c], ms_send.at[c], ms_recv.at[c])

    def mixed_chunk(c):
        for j, other in others:
            mixed_copy(c, j, other).wait_recv()
        if c == 0:
            mixed_own.wait()
        load = pltpu.make_async_copy(
            mixed_arrived.at[:, :, pl.ds(c * wide, wide)], mixed_rows, mix_local.at[1]
        )
        load.start()
        load.wait()
        part = dot_tn(
            picker[...].reshape(planes * slots, length), mixed_rows[...].reshape(planes * slots, wide)
        )
        mixed_part[c] = part.astype(low).reshape(count, tokens, wide)

    waves = list(range(chunks + count - 2))

    def mixed_wave():
        wave = waves.pop(0)
        for c in range(chunks):
            if 0 <= wave - c < count - 1:
                line_sum_step(wave - c, *mixed_line(c))

    head_gradients(place)
    spread = min(chunks, count) - 1
    for step in range(1, count):
        gather(step)
        if step <= spread - 1:
            mixed_chunk(step - 1)
            mixed_wave()

    per_head = HEAD_SIZE // out_block

    def out_gradient(head):
        all_branch = branch_full[...].reshape(length, MODEL_WIDTH)
        part = dot_tn(heads_low[head], all_branch).astype(low)
        if per_head == 1:
            grad_out[head] = part
        else:
            grad_out[head * per_head : (head + 1) * per_head] = part.reshape(
                per_head, out_block, MODEL_WIDTH
            )

    def out_copy(k):
        return remote(
            grad_out.at[2 * k + 1 - core], out_pair.at[k], out_sems.at[0, k], out_sems.at[1, k],
            (place, partner),
        )

    def out_far_copy(k, other):
        return remote(
            out_pair.at[other], out_far.at[k - 1], out_sems.at[2, k], out_sems.at[3, k],
            (place, 2 * other + core),
        )

    if per_head == 1:
        for k in range(chips):
            out_gradient(2 * k + 1 - core)
            out_copy(k).start()
        for k in range(chips):
            out_gradient(2 * k + core)
    else:
        for head in range(heads):
            out_gradient(head)
        for k in range(chips):
            out_copy(k).start()

    done = spread - 1
    while done < chunks - 1:
        mixed_chunk(done)
        mixed_wave()
        done += 1

    lane_part = MODEL_WIDTH // count

    def router_far(k, other):
        return remote(
            router_ref.at[:, pl.ds(pl.multiple_of(other * lane_part, lane_part), lane_part)],
            router_line.at[k - 1], router_sems.at[0, k], router_sems.at[1, k], (other, member),
        )

    def router_near(k, other):
        return remote(
            router_sum.at[0], router_chip.at[k - 1], router_sems.at[2, k], router_sems.at[3, k],
            (place, 2 * other + core),
        )

    def router_last():
        return remote(
            router_sum.at[1], router_pair, router_sems.at[2, 0], router_sems.at[3, 0], (place, partner)
        )

    for k, other in far_places:
        router_far(k, other).start()

    grad_pair[...] = jnp.zeros_like(grad_pair)
    gain_parts[...] = jnp.zeros_like(gain_parts)
    block_rows = min(256, length)
    gain_query = gains_ref[2:3, :HEAD_SIZE]
    gain_key = gains_ref[3:4, :HEAD_SIZE]

    def unprepare(grad, raw, gain):
        turned = grad * turn_cos_ref[...] - pltpu.roll(grad, HEAD_SIZE // 2, 1) * turn_sin_ref[...]
        inverse = lax.rsqrt(jnp.mean(raw * raw, axis=-1, keepdims=True) + EPSILON)
        unit = raw * inverse
        gain_part = jnp.sum(turned * unit, axis=0, keepdims=True)
        turned = turned * gain
        middle = jnp.mean(turned * unit, axis=-1, keepdims=True)
        return inverse * (turned - unit * middle), gain_part

    key_turned = jnp.transpose(pair[0].astype(jnp.float32)).astype(low)

    def one_head(head, carry):
        lse = lse_ref[head]
        grads = []
        for block in range(length // block_rows):
            begin, end = block * block_rows, (block + 1) * block_rows
            query = queries[head, begin:end, :]
            grad = grad_heads[head, begin:end, :]
            scores = dot_nt(pair[0, :end, :], query) * scale
            key_ids = lax.broadcasted_iota(jnp.int32, (end, block_rows), 0)
            query_ids = lax.broadcasted_iota(jnp.int32, (end, block_rows), 1) + begin
            scores = jnp.where(key_ids <= query_ids, scores, FILLER)
            probs = jnp.exp(scores - lse[:, begin:end])
            grad_probs = dot_nt(pair[1, :end, :], grad)
            delta = jnp.sum(probs * grad_probs, axis=0, keepdims=True)
            grad_scores = (probs * (grad_probs - delta)).astype(low)
            grad_pair[0, :end, :] += dot_nn(grad_scores, query) * scale
            grad_pair[1, :end, :] += dot_nn(probs.astype(low), grad)
            grads.append(jnp.transpose(dot_nn(key_turned[:, :end], grad_scores)) * scale)
        grad_query = jnp.concatenate(grads, axis=0)
        grad_raw, gain_part = unprepare(grad_query, proj[head], gain_query)
        gain_parts[0:1, :] += gain_part
        grad_proj[:, pl.ds(pl.multiple_of(head * HEAD_SIZE, HEAD_SIZE), HEAD_SIZE)] = grad_raw.astype(low)
        return carry

    split = heads // 2
    groups = [(0, split), (split, heads + 2)]

    def columns_of(group):
        return pl.ds(groups[group][0] * HEAD_SIZE, (groups[group][1] - groups[group][0]) * HEAD_SIZE)

    def col_copy(group, k):
        part = columns_of(group)
        return remote(
            grad_cols.at[:, 2 * k + 1 - core, :, part], col_pair.at[k, :, :, part],
            col_sems.at[group, 0, k], col_sems.at[group, 1, k], (place, partner),
        )

    def col_far_copy(group, k, other):
        part = columns_of(group)
        return remote(
            col_pair.at[other, :, :, part], col_far.at[k - 1, :, :, part],
            col_sems.at[group, 2, k], col_sems.at[group, 3, k], (place, 2 * other + core),
        )

    def z_copy(group, k, other):
        part = columns_of(group)
        return remote(
            col_sums.at[other, :, part], columns_out.at[place, :, part],
            z_sems.at[group, 0, k], z_sems.at[group, 1, k], (other, member),
        )

    def col_gradient(group):
        first, final = groups[group]
        grads = grad_proj[:, first * HEAD_SIZE : final * HEAD_SIZE]
        block_width = planes * shard
        for block in range(count):
            part = dot_tn(normed[:, block * block_width : (block + 1) * block_width], grads)
            grad_cols[block, :, :, first * HEAD_SIZE : final * HEAD_SIZE] = part.astype(low).reshape(
                planes, shard, (final - first) * HEAD_SIZE
            )
        for k in range(chips):
            col_copy(group, k).start()

    def col_pairs(group):
        first, final = groups[group]
        columns = slice(first * HEAD_SIZE, final * HEAD_SIZE)
        for k in range(chips):
            col_copy(group, k).wait_recv()
            col_pair[k, :, :, columns] = (
                col_pair[k, :, :, columns].astype(jnp.float32)
                + grad_cols[:, 2 * k + core, :, columns].astype(jnp.float32)
            ).astype(low)
        for k, other in far_chips:
            col_far_copy(group, k, other).start()

    def col_totals(group):
        first, final = groups[group]
        columns = slice(first * HEAD_SIZE, final * HEAD_SIZE)
        total = col_pair[chip, :, :, columns].astype(jnp.float32)
        for k, other in far_chips:
            col_far_copy(group, k, other).wait_recv()
            total += col_far[k - 1, :, :, columns].astype(jnp.float32)
        col_sums[:, :, columns] = total.astype(low)
        for k, other in far_places:
            z_copy(group, k, other).start()
        columns_out[place, :, columns] = col_sums[place, :, columns]

    lax.fori_loop(0, split, one_head, 0)
    col_gradient(0)
    for k in range(chips):
        out_copy(k).wait_recv()
        out_pair[k] = (
            out_pair[k].astype(jnp.float32) + grad_out[2 * k + core].astype(jnp.float32)
        ).astype(low)
    for k, other in far_chips:
        out_far_copy(k, other).start()
    mixed_chunk(chunks - 1)
    mixed_wave()
    col_pairs(0)
    lax.fori_loop(split, heads, one_head, 0)
    grad_raw, gain_part = unprepare(grad_pair[0], proj[heads], gain_key)
    gain_parts[1:2, :] += gain_part
    grad_proj[:, query_columns : query_columns + HEAD_SIZE] = grad_raw.astype(low)
    grad_proj[:, query_columns + HEAD_SIZE :] = grad_pair[1].astype(low)
    col_gradient(1)

    line_gather_end(*line)
    normed_part = branch_full
    for block in range(count):
        normed_part[block] = dot_nt(
            grad_proj[block * tokens : (block + 1) * tokens, :],
            own_cols[...].reshape(MODEL_WIDTH, width),
        ).astype(low)
    sums = (count, place, member, normed_part, normed_sums, rs_send, rs_recv)
    line_sum_step(0, *sums)
    col_pairs(1)
    if waves:
        mixed_wave()

    for k, other in far_places:
        router_far(k, other).wait_recv()
    own_lanes = pl.ds(pl.multiple_of(place * lane_part, lane_part), lane_part)
    total = router_ref[:, own_lanes]
    for k, other in far_places:
        total += router_line[k - 1]
    router_sum[0] = total
    for k, other in far_chips:
        router_near(k, other).start()
    for step in range(1, count - 1):
        line_sum_step(step, *sums)
        if waves:
            mixed_wave()
        if step == 1:
            total = out_pair[chip].astype(jnp.float32)
            for k, other in far_chips:
                out_far_copy(k, other).wait_recv()
                total += out_far[k - 1].astype(jnp.float32)
            out_total[...] = total
            col_totals(0)
            total = router_sum[0]
            for k, other in far_chips:
                router_near(k, other).wait_recv()
                total += router_chip[k - 1]
            router_sum[1] = total
            router_last().start()
    while waves:
        mixed_wave()
    for c in range(chunks):
        line_sum_end(*mixed_line(c), mixed_total.at[:, c * wide : (c + 1) * wide])
    col_totals(1)
    router_last().wait_recv()
    router_total[...] = router_sum[1] + router_pair[...]
    line_sum_end(*sums, grad_input_ref)

    hidden = hidden_ref[...].astype(jnp.float32)
    inverse = lax.rsqrt(jnp.mean(hidden * hidden, axis=-1, keepdims=True) + EPSILON)
    unit = hidden * inverse
    grad_normed = grad_input_ref[...]
    gain_row = jnp.sum(grad_normed * unit, axis=0, keepdims=True)
    for k in range(MODEL_WIDTH // HEAD_SIZE):
        gain_own[0, k : k + 1, :] = gain_row[:, k * HEAD_SIZE : (k + 1) * HEAD_SIZE]
    gain_own[0, MODEL_WIDTH // HEAD_SIZE :, :] = gain_parts[...]

    def gain_far(k, other):
        return remote(
            gain_own.at[0], gain_line.at[k - 1], gain_sems.at[0, k], gain_sems.at[1, k], (other, member)
        )

    def gain_near(k, other):
        return remote(
            gain_own.at[1], gain_chip.at[k - 1], gain_sems.at[2, k], gain_sems.at[3, k],
            (place, 2 * other + core),
        )

    def gain_last():
        return remote(
            gain_own.at[2], gain_pair, gain_sems.at[2, 0], gain_sems.at[3, 0], (place, partner)
        )

    for k, other in far_places:
        gain_far(k, other).start()
    turned = grad_normed * gains_ref[0:1, :]
    grad_input_ref[...] = grad_hidden_ref[...] + inverse * (
        turned - unit * jnp.mean(turned * unit, axis=-1, keepdims=True)
    )
    total = gain_own[0]
    for k, other in far_places:
        gain_far(k, other).wait_recv()
        total += gain_line[k - 1]
    gain_own[1] = total
    for k, other in far_chips:
        gain_near(k, other).start()
    for k, other in far_chips:
        gain_near(k, other).wait_recv()
        total += gain_chip[k - 1]
    gain_own[2] = total
    gain_last().start()
    gain_last().wait_recv()
    gain_total[...] = gain_own[2] + gain_pair[...]

    for group in range(2):
        for k, other in far_places:
            z_copy(group, k, other).wait_recv()
            z_copy(group, k, other).wait_send()
        for k in range(chips):
            col_copy(group, k).wait_send()
        for k, other in far_chips:
            col_far_copy(group, k, other).wait_send()
    for k in range(chips):
        out_copy(k).wait_send()
    for k, other in far_chips:
        out_far_copy(k, other).wait_send()
        router_near(k, other).wait_send()
        gain_near(k, other).wait_send()
    for k, other in far_places:
        router_far(k, other).wait_send()
        gain_far(k, other).wait_send()
    router_last().wait_send()
    gain_last().wait_send()
    for c in range(chunks):
        for j, other in others:
            mixed_copy(c, j, other).wait_send()


def attention_backward(
    count, planes, heads, shard, branch, grad_hidden, hidden, gains, router, out_rows, own_cols, normed,
    heads_low, queries, pair, proj, picker, combined, lse, turn_cos, turn_sin,
):
    tokens = branch.shape[0]
    length = count * tokens
    width = (heads + 2) * HEAD_SIZE
    chips = planes // 2
    out_block = heads * HEAD_SIZE // planes
    chunks = 4
    wide = MODEL_WIDTH // chunks
    gain_rows = MODEL_WIDTH // HEAD_SIZE + 8
    router_part = (router.shape[0], MODEL_WIDTH // count)
    low, kind = jnp.bfloat16, jnp.float32
    vmem = pl.BlockSpec(memory_space=pltpu.VMEM)
    anywhere = pl.BlockSpec(memory_space=pl.ANY)
    dma = pltpu.SemaphoreType.DMA
    shape = jax.ShapeDtypeStruct
    most = max(count, chips)
    return pl.pallas_call(
        functools.partial(backward_kernel, count, planes, tokens, heads, shard),
        out_shape=(
            shape((tokens, MODEL_WIDTH), kind),
            shape((out_block, MODEL_WIDTH), kind),
            shape((count, shard, width), low),
            shape((tokens, MODEL_WIDTH), kind),
            shape(router_part, kind),
            shape((gain_rows, HEAD_SIZE), kind),
            shape(combined.shape, low),
        ),
        in_specs=[vmem] * 5 + [anywhere] * 9 + [vmem] * 3,
        out_specs=(vmem,) * 6 + (anywhere,),
        scratch_shapes=[
            pltpu.VMEM(out_rows.shape, low),
            pltpu.VMEM(own_cols.shape, low),
            pltpu.VMEM(normed.shape, low),
            pltpu.VMEM(heads_low.shape, low),
            pltpu.VMEM(queries.shape, low),
            pltpu.VMEM(pair.shape, low),
            pltpu.VMEM(proj.shape, kind),
            pltpu.VMEM(picker.shape, low),
            dma((8,)),
            pltpu.VMEM((count, tokens, MODEL_WIDTH), low),
            dma((2, count)),
            dma((2, count)),
            pltpu.VMEM((heads, length, HEAD_SIZE), low),
            pltpu.VMEM((length, width), low),
            pltpu.VMEM((2, length, HEAD_SIZE), kind),
            pltpu.VMEM((8, HEAD_SIZE), kind),
            pltpu.VMEM((planes, out_block, MODEL_WIDTH), low),
            pltpu.VMEM((chips, out_block, MODEL_WIDTH), low),
            pltpu.VMEM((chips - 1, out_block, MODEL_WIDTH), low),
            dma((4, chips)),
            pltpu.VMEM((count, planes, shard, width), low),
            pltpu.VMEM((chips, count, shard, width), low),
            pltpu.VMEM((chips - 1, count, shard, width), low),
            pltpu.VMEM((count, shard, width), low),
            dma((2, 4, chips)),
            pltpu.VMEM((count + 1, tokens, MODEL_WIDTH), low),
            dma((2, count)),
            dma((2, count)),
            dma((2, 2, count)),
            pltpu.VMEM(combined.shape[:2] + (wide,), low),
            pltpu.VMEM((chunks, count, tokens, wide), low),
            pltpu.VMEM((chunks, count + 1, tokens, wide), low),
            dma((chunks, planes)),
            dma((chunks, planes)),
            dma((2,)),
            dma((chunks, 2, count)),
            dma((chunks, 2, count)),
            pltpu.VMEM((count - 1,) + router_part, kind),
            pltpu.VMEM((2,) + router_part, kind),
            pltpu.VMEM((chips - 1,) + router_part, kind),
            pltpu.VMEM(router_part, kind),
            dma((4, most)),
            pltpu.VMEM((3, gain_rows, HEAD_SIZE), kind),
            pltpu.VMEM((count - 1, gain_rows, HEAD_SIZE), kind),
            pltpu.VMEM((chips - 1, gain_rows, HEAD_SIZE), kind),
            pltpu.VMEM((gain_rows, HEAD_SIZE), kind),
            dma((4, most)),
        ],
        compiler_params=pltpu.CompilerParams(
            collective_id=3, has_side_effects=True, vmem_limit_bytes=VMEM_BYTES
        ),
        name="attention_backward",
    )(
        branch, grad_hidden, hidden, gains, router, out_rows, own_cols, normed, heads_low, queries,
        pair, proj, picker, combined, lse, turn_cos, turn_sin,
    )


def forward_kernel(
    count, planes, tokens, heads, shard, capacity, chunks,
    hidden_ref, routes_ref, gain1_ref, gain2_ref, query_gain_ref, key_gain_ref, router_ref, qkv_ref,
    out_ref, cotangent_ref, turn_cos_ref, turn_sin_ref,
    hidden1_ref, mixed_ref, lse_ref, gains_ref, picker_ref,
    router_out, own_cols_hbm, out_rows_hbm, normed_hbm, heads_hbm, query_hbm, pair_hbm, proj_hbm,
    grad_hbm, masks_hbm,
    column_send, own_cols, c_send, c_recv,
    out_rows, o_send, o_recv,
    hidden_full, h_send, h_recv,
    gains_all, gz_send, gz_recv, gd_send, gd_recv,
    router_all, rz_send, rz_recv, rd_send, rd_recv,
    places_all, p_send, p_recv,
    normed, proj, queries, pair, heads_low,
    grad_full, dy_send, dy_recv,
    grad_sent, d_send, d_recv, mask_sent, m_send, m_recv,
    branch, sums, rs_send, rs_recv, local_sems,
):
    place = lax.axis_index("seq")
    member = lax.axis_index("dp")
    core = lax.rem(member, 2)
    chip = member // 2
    chips = planes // 2
    partner = member + 1 - 2 * core
    length = count * tokens
    query_columns = heads * HEAD_SIZE
    replicas = count // KEY_VALUE_HEADS
    wide = MODEL_WIDTH // chunks
    slots = grad_sent.shape[2]
    rows = planes * slots
    low = jnp.bfloat16
    scale = HEAD_SIZE ** (-0.5)
    far_places = [(k, lax.rem(place + k, count)) for k in range(1, count)]
    far_chips = [(k, lax.rem(chip + k, chips)) for k in range(1, chips)]
    others = [(j, lax.rem(member + j, planes)) for j in range(1, planes)]

    hidden_full[place] = hidden_ref[...]
    index = place * planes + member
    row_lanes = lax.broadcasted_iota(jnp.int32, (1, HEAD_SIZE), 1)
    pieces = []
    for ref in (gain1_ref, gain2_ref, query_gain_ref, key_gain_ref):
        width = ref.shape[1]
        values = ref[...].astype(jnp.float32)
        begin = lax.rem(index, HEAD_SIZE // width) * width
        piece = jnp.zeros((1, HEAD_SIZE), jnp.float32)
        for k in range(width):
            piece += jnp.where(row_lanes == begin + k, values[:, k : k + 1], 0.0)
        pieces.append(piece)
    pieces.append(jnp.zeros((gains_all.shape[2] - 4, HEAD_SIZE), jnp.float32))
    gains_all[place, member] = jnp.concatenate(pieces, axis=0).astype(low)
    router_all[place, member] = jnp.zeros(router_all.shape[2:], low)
    router_all[place, member, :, : router_ref.shape[1]] = router_ref[...]
    for part in range(count):
        head = part // replicas
        keys = QUERY_HEADS * HEAD_SIZE + head * HEAD_SIZE
        values = keys + KEY_VALUE_HEADS * HEAD_SIZE
        column_send[part, :, :query_columns] = qkv_ref[
            :, part * query_columns : (part + 1) * query_columns
        ]
        column_send[part, :, query_columns : query_columns + HEAD_SIZE] = qkv_ref[
            :, keys : keys + HEAD_SIZE
        ]
        column_send[part, :, query_columns + HEAD_SIZE :] = qkv_ref[:, values : values + HEAD_SIZE]
    lanes = lax.broadcasted_iota(jnp.int32, (tokens, places_all.shape[-1]), 1)
    named = jnp.zeros(lanes.shape, jnp.float32)
    for k in range(TOP):
        named += jnp.where(routes_ref[:, k : k + 1] == lanes, 1.0, 0.0)
    row_ids = lax.broadcasted_iota(jnp.int32, (tokens, tokens), 0)
    col_ids = lax.broadcasted_iota(jnp.int32, (tokens, tokens), 1)
    before = jnp.where(row_ids > col_ids, 1.0, 0.0).astype(low)
    earlier = dot_nn(before, named.astype(low))
    places_all[place] = jnp.where(named > 0, earlier, -512.0).astype(low)
    for c in range(chunks):
        grad_full[c, place] = cotangent_ref[:, c * wide : (c + 1) * wide]

    greet([(place, other) for _, other in others] + [(other, member) for _, other in far_places])

    def column_copy(k, other):
        return remote(
            column_send.at[other], own_cols.at[place, member], c_send.at[0, k], c_recv.at[0, k],
            (other, member),
        )

    def gain_line(k, other):
        mine = gains_all.at[place, member]
        return remote(mine, mine, gz_send.at[k], gz_recv.at[k], (other, member))

    def router_line(k, other):
        mine = router_all.at[place, member]
        return remote(mine, mine, rz_send.at[k], rz_recv.at[k], (other, member))

    def places_line(k, other):
        mine = places_all.at[place]
        return remote(mine, mine, p_send.at[k], p_recv.at[k], (other, member))

    def out_copy(k, other):
        return remote(
            out_ref, out_rows.at[member], o_send.at[0, k], o_recv.at[0, k], (place, 2 * other + core)
        )

    def out_pair(k, other):
        source = out_ref if k == 0 else out_rows.at[2 * other + core]
        return remote(
            source, out_rows.at[2 * other + core], o_send.at[1, k], o_recv.at[1, k], (place, partner)
        )

    def block_copy(k, other):
        mine = own_cols.at[:, member]
        return remote(mine, mine, c_send.at[1, k], c_recv.at[1, k], (place, 2 * other + core))

    def block_pair(k, other):
        block = own_cols.at[:, 2 * other + core]
        return remote(block, block, c_send.at[2, k], c_recv.at[2, k], (place, partner))

    for k, other in far_places:
        gain_line(k, other).start()
        column_copy(k, other).start()
    for k, other in far_chips:
        out_copy(k, other).start()
    out_pair(0, chip).start()
    hidden_line = (count, place, member, hidden_full, h_send, h_recv)
    line_gather_step(0, *hidden_line)
    for k, other in far_places:
        places_line(k, other).start()
        router_line(k, other).start()
    own_cols[place, member] = column_send[place]
    out_rows[member] = out_ref[...]

    def gain_plane(j, other):
        mine = gains_all.at[:, member]
        return remote(mine, mine, gd_send.at[j], gd_recv.at[j], (place, other))

    def router_plane(j, other):
        mine = router_all.at[:, member]
        return remote(mine, mine, rd_send.at[j], rd_recv.at[j], (place, other))

    for k, other in far_places:
        gain_line(k, other).wait_recv()
    for j, other in others:
        gain_plane(j, other).start()
    for k, other in far_places:
        column_copy(k, other).wait_recv()
    for k, other in far_chips:
        block_copy(k, other).start()
    block_pair(0, chip).start()
    line_gather_step(1, *hidden_line)

    for k, other in far_places:
        places_line(k, other).wait_recv()
    experts = places_all.shape[-1]
    pick_rows = lax.broadcasted_iota(jnp.int32, (rows, experts), 0)
    pick_experts = lax.broadcasted_iota(jnp.int32, (rows, experts), 1) - place * planes
    slot_ids = lax.broadcasted_iota(jnp.int32, (rows, length), 0)
    token_ids = lax.broadcasted_iota(jnp.int32, (rows, length), 1)
    offsets = jnp.zeros((rows, length), jnp.int32)
    choose = jnp.zeros((rows, experts), jnp.float32)
    for other in range(planes):
        inside = (pick_rows >= other * slots) & (pick_rows < (other + 1) * slots)
        choose += jnp.where(inside & (pick_experts == other), 1.0, 0.0)
        offsets = jnp.where(slot_ids >= other * slots, other * slots, offsets)
    before_block = jnp.zeros((rows, length), jnp.int32)
    for block in range(count):
        before_block = jnp.where(
            token_ids >= block * tokens, block_rank(block, place, count) * capacity, before_block
        )
    wanted = dot_nt(choose.astype(low), places_all[...].reshape(length, experts))
    picker_rows = jnp.where(
        wanted == (slot_ids - offsets - before_block).astype(jnp.float32), 1.0, 0.0
    ).astype(low)
    picker_ref[...] = picker_rows.reshape(planes, slots, length)
    mask_full = jnp.where(places_all[...].reshape(length, experts).astype(jnp.float32) >= 0, 1.0, 0.0)
    mask_sent[...] = (
        dot_nn(picker_rows, mask_full.astype(low)).astype(low).reshape(mask_sent.shape)
    )

    for k, other in far_places:
        router_line(k, other).wait_recv()
    for j, other in others:
        router_plane(j, other).start()

    def mask_copy(j, other):
        return remote(
            mask_sent.at[other], masks_hbm.at[member], m_send.at[j], m_recv.at[j], (place, other)
        )

    for j, other in others:
        mask_copy(j, other).start()
    masks_own = pltpu.make_async_copy(mask_sent.at[member], masks_hbm.at[member], local_sems.at[0])
    masks_own.start()

    for k, other in far_chips:
        out_copy(k, other).wait_recv()
    for k, other in far_chips:
        out_pair(k, lax.rem(chip + chips - k, chips)).start()
    for step in range(2, count):
        line_gather_step(step, *hidden_line)

    def grad_line(c):
        return (count, place, member, grad_full.at[c], dy_send.at[c], dy_recv.at[c])

    def grad_copy(c, j, other):
        return remote(
            grad_sent.at[c, other], grad_hbm.at[c, member], d_send.at[c, j], d_recv.at[c, j], (place, other)
        )

    def grad_own(c):
        return pltpu.make_async_copy(
            grad_sent.at[c, member], grad_hbm.at[c, member], local_sems.at[16 + c]
        )

    def grad_tick(tick):
        for c in range(chunks):
            step = tick - c
            if 0 <= step < count:
                line_gather_step(step, *grad_line(c))
            if step == count - 1:
                picked = dot_nn(
                    picker_ref[...].reshape(rows, length), grad_full[c].reshape(length, wide)
                ).astype(low)
                grad_sent[c] = picked.reshape(planes, slots, wide)
                for j, other in others:
                    grad_copy(c, j, other).start()
                grad_own(c).start()

    ticks = list(range(chunks + count - 1))
    grad_tick(ticks.pop(0))

    for j, other in others:
        gain_plane(j, other).wait_recv()
    per_row = HEAD_SIZE // shard
    small_total = jnp.sum(gains_all[...].astype(jnp.float32), axis=(0, 1))
    gain_rows = []
    for row in range(2):
        parts = []
        for group in range(MODEL_WIDTH // HEAD_SIZE):
            part = jnp.zeros((1, HEAD_SIZE), jnp.float32)
            for index in range(group * per_row, (group + 1) * per_row):
                part += gains_all[index // planes, index % planes, row : row + 1, :].astype(jnp.float32)
            parts.append(part)
        gain_rows.append(jnp.concatenate(parts, axis=1))
    gains_ref[0:1, :] = gain_rows[0]
    gains_ref[1:2, :] = gain_rows[1]
    gain_query = small_total[2:3, :]
    gain_key = small_total[3:4, :]
    gains_ref[2:3, :HEAD_SIZE] = gain_query
    gains_ref[3:4, :HEAD_SIZE] = gain_key

    def normalize(values, gain):
        return (
            values
            * lax.rsqrt(jnp.mean(values * values, axis=-1, keepdims=True) + EPSILON)
            * gain
        )

    for block in range(count):
        values = hidden_full[block].astype(jnp.float32)
        normed[block * tokens : (block + 1) * tokens, :] = normalize(values, gain_rows[0]).astype(low)
    stores = [pltpu.make_async_copy(normed, normed_hbm, local_sems.at[1])]
    stores[-1].start()

    for k, other in far_chips:
        block_copy(k, other).wait_recv()
    for k, other in far_chips:
        block_pair(k, lax.rem(chip + chips - k, chips)).start()
    block_pair(0, chip).wait_recv()
    for k, other in far_chips:
        block_pair(k, lax.rem(chip + chips - k, chips)).wait_recv()
    weights = own_cols[...].reshape(MODEL_WIDTH, query_columns + 2 * HEAD_SIZE)
    stores.append(pltpu.make_async_copy(own_cols, own_cols_hbm, local_sems.at[2]))
    stores[-1].start()

    def prepare(values, gain):
        turned = normalize(values, gain)
        return turned * turn_cos_ref[...] + pltpu.roll(turned, HEAD_SIZE // 2, 1) * turn_sin_ref[...]

    paired = dot_nn(normed[...], weights[:, query_columns:])
    proj[heads] = paired[:, :HEAD_SIZE]
    proj[heads + 1] = paired[:, HEAD_SIZE:]
    pair[0] = prepare(paired[:, :HEAD_SIZE], gain_key).astype(low)
    pair[1] = paired[:, HEAD_SIZE:].astype(low)
    projected = dot_nn(normed[...], weights[:, :query_columns])
    for head in range(heads):
        proj[head] = projected[:, head * HEAD_SIZE : (head + 1) * HEAD_SIZE]
    value_turned = jnp.transpose(paired[:, HEAD_SIZE:]).astype(low)
    stores.append(pltpu.make_async_copy(proj, proj_hbm, local_sems.at[3]))
    stores[-1].start()
    stores.append(pltpu.make_async_copy(pair, pair_hbm, local_sems.at[4]))
    stores[-1].start()
    block_rows = min(256, length)

    def one_head(head, carry):
        queries[head] = prepare(proj[head], gain_query).astype(low)
        for block in range(length // block_rows):
            begin, end = block * block_rows, (block + 1) * block_rows
            scores = dot_nt(pair[0, :end, :], queries[head, begin:end, :]) * scale
            key_ids = lax.broadcasted_iota(jnp.int32, (end, block_rows), 0)
            query_ids = lax.broadcasted_iota(jnp.int32, (end, block_rows), 1) + begin
            scores = jnp.where(key_ids <= query_ids, scores, FILLER)
            top = jnp.max(scores, axis=0, keepdims=True)
            powers = jnp.exp(scores - top)
            total = jnp.sum(powers, axis=0, keepdims=True)
            lse_ref[head, :, begin:end] = top + jnp.log(total)
            probs = (powers * (1.0 / total)).astype(low)
            mixed = dot_nn(value_turned[:, :end], probs)
            heads_low[head, begin:end, :] = jnp.transpose(mixed).astype(low)
        return carry

    halves = 4
    for part in range(halves):
        lax.fori_loop(part * heads // halves, (part + 1) * heads // halves, one_head, 0)
        if ticks:
            grad_tick(ticks.pop(0))
    stores.append(pltpu.make_async_copy(queries, query_hbm, local_sems.at[5]))
    stores[-1].start()
    stores.append(pltpu.make_async_copy(heads_low, heads_hbm, local_sems.at[6]))
    stores[-1].start()

    out_pair(0, chip).wait_recv()
    for k, other in far_chips:
        out_pair(k, lax.rem(chip + chips - k, chips)).wait_recv()
    out_all = out_rows[...].reshape(query_columns, MODEL_WIDTH)
    stores.append(pltpu.make_async_copy(out_rows, out_rows_hbm, local_sems.at[7]))
    stores[-1].start()

    def project(block, carry):
        at = pl.ds(pl.multiple_of(block * tokens, tokens), tokens)
        mixed = jnp.concatenate([heads_low[head, at, :] for head in range(heads)], axis=1)
        branch[block] = dot_nn(mixed, out_all).astype(low)
        return carry

    lax.fori_loop(0, count, project, 0)
    line = (count, place, member, branch, sums, rs_send, rs_recv)
    for step in range(count - 1):
        line_sum_step(step, *line)
        for _ in range(-(-len(ticks) // (count - 1 - step))):
            grad_tick(ticks.pop(0))
    line_sum_end(*line, hidden1_ref)
    hidden1 = hidden_ref[...].astype(jnp.float32) + hidden1_ref[...]
    hidden1_ref[...] = hidden1
    mixed_ref[...] = normalize(hidden1, gain_rows[1]).astype(low)

    for j, other in others:
        router_plane(j, other).wait_recv()
    router_out[...] = router_all[...].reshape(router_out.shape)
    for j, other in others:
        mask_copy(j, other).wait_recv()
        for c in range(chunks):
            grad_copy(c, j, other).wait_recv()
    for k, other in far_places:
        gain_line(k, other).wait_send()
        column_copy(k, other).wait_send()
        places_line(k, other).wait_send()
        router_line(k, other).wait_send()
    for k, other in far_chips:
        out_copy(k, other).wait_send()
        block_copy(k, other).wait_send()
        out_pair(k, other).wait_send()
        block_pair(k, other).wait_send()
    out_pair(0, chip).wait_send()
    block_pair(0, chip).wait_send()
    for j, other in others:
        gain_plane(j, other).wait_send()
        router_plane(j, other).wait_send()
        mask_copy(j, other).wait_send()
        for c in range(chunks):
            grad_copy(c, j, other).wait_send()
    for c in range(chunks):
        grad_own(c).wait()
        line_gather_end(*grad_line(c))
    line_gather_end(*hidden_line)
    masks_own.wait()
    for store in stores:
        store.wait()


def attention_forward(
    count, planes, heads, shard, capacity, slots, chunks,
    hidden, routes, gain_one, gain_two, query_gain, key_gain, router, qkv, out_weight, cotangent,
    turn_cos, turn_sin,
):
    tokens = hidden.shape[0]
    length = count * tokens
    width = (heads + 2) * HEAD_SIZE
    chips = planes // 2
    wide = MODEL_WIDTH // chunks
    experts = -(-router.shape[-1] // 128) * 128
    small_rows = 16
    out_block = out_weight.shape[0]
    low, full = jnp.bfloat16, jnp.float32
    vmem = pl.BlockSpec(memory_space=pltpu.VMEM)
    anywhere = pl.BlockSpec(memory_space=pl.ANY)
    dma = pltpu.SemaphoreType.DMA
    shape = jax.ShapeDtypeStruct
    return pl.pallas_call(
        functools.partial(forward_kernel, count, planes, tokens, heads, shard, capacity, chunks),
        out_shape=(
            shape((tokens, MODEL_WIDTH), full),
            shape((tokens, MODEL_WIDTH), low),
            shape((heads, 1, length), full),
            shape((8, MODEL_WIDTH), full),
            shape((planes, slots, length), low),
            shape((MODEL_WIDTH, experts), low),
            shape((count, planes, shard, width), low),
            shape((planes, out_block, MODEL_WIDTH), low),
            shape((length, MODEL_WIDTH), low),
            shape((heads, length, HEAD_SIZE), low),
            shape((heads, length, HEAD_SIZE), low),
            shape((2, length, HEAD_SIZE), low),
            shape((heads + 2, length, HEAD_SIZE), full),
            shape((chunks, planes, slots, wide), low),
            shape((planes, slots, experts), low),
        ),
        in_specs=[vmem] * 12,
        out_specs=(vmem,) * 6 + (anywhere,) * 9,
        scratch_shapes=[
            pltpu.VMEM((count, shard, width), low),
            pltpu.VMEM((count, planes, shard, width), low),
            dma((3, max(count, chips))),
            dma((3, max(count, chips))),
            pltpu.VMEM((planes, out_block, MODEL_WIDTH), low),
            dma((2, chips)),
            dma((2, chips)),
            pltpu.VMEM((count, tokens, MODEL_WIDTH), low),
            dma((2, count)),
            dma((2, count)),
            pltpu.VMEM((count, planes, small_rows, HEAD_SIZE), low),
            dma((count,)),
            dma((count,)),
            dma((planes,)),
            dma((planes,)),
            pltpu.VMEM((count, planes, shard, experts), low),
            dma((count,)),
            dma((count,)),
            dma((planes,)),
            dma((planes,)),
            pltpu.VMEM((count, tokens, experts), low),
            dma((count,)),
            dma((count,)),
            pltpu.VMEM((length, MODEL_WIDTH), low),
            pltpu.VMEM((heads + 2, length, HEAD_SIZE), full),
            pltpu.VMEM((heads, length, HEAD_SIZE), low),
            pltpu.VMEM((2, length, HEAD_SIZE), low),
            pltpu.VMEM((heads, length, HEAD_SIZE), low),
            pltpu.VMEM((chunks, count, tokens, wide), low),
            dma((chunks, 2, count)),
            dma((chunks, 2, count)),
            pltpu.VMEM((chunks, planes, slots, wide), low),
            dma((chunks, planes)),
            dma((chunks, planes)),
            pltpu.VMEM((planes, slots, experts), low),
            dma((planes,)),
            dma((planes,)),
            pltpu.VMEM((count, tokens, MODEL_WIDTH), low),
            pltpu.VMEM((count + 1, tokens, MODEL_WIDTH), low),
            dma((2, count)),
            dma((2, count)),
            dma((16 + chunks,)),
        ],
        compiler_params=pltpu.CompilerParams(
            collective_id=1, has_side_effects=True, vmem_limit_bytes=VMEM_BYTES
        ),
        name="attention_forward",
    )(
        hidden, routes, gain_one, gain_two, query_gain, key_gain, router, qkv, out_weight, cotangent,
        turn_cos, turn_sin,
    )


def segments(slots):
    step = max(16, slots // 4 // 16 * 16)
    starts = [step * k for k in range(slots // step)]
    return list(zip(starts, starts[1:] + [slots]))


def ranked_block(rank, place, count):
    short = jnp.minimum(place, count - 1 - place)
    near = (rank + 1) // 2
    side = -1 if rank % 2 else 1
    far = rank - short
    far_side = jnp.where(place < count - 1 - place, 1, -1)
    return jnp.where(rank <= 2 * short, place + side * near, place + far_side * far)


def block_rank(block, place, count):
    short = jnp.minimum(place, count - 1 - place)
    away = jnp.abs(block - place)
    near = 2 * away - jnp.where(block < place, 1, 0)
    return jnp.where(away <= short, near, short + away)


def expert_kernel(
    count, planes, tokens, capacity, chunks,
    mixed_ref, hidden1_ref, cotangent_ref, gains_ref, routes_ref, masks_ref,
    picker_hbm, grad_hbm, router_hbm, in_hbm, back_hbm,
    grad_hidden_ref, branch_ref, router_ref, grad_in_hbm, grad_back_hbm, combined_hbm,
    picker, grad_rows, router, weight_in, weight_back, local_sems,
    full, ag_send, ag_recv,
    sent, arrived, x_send, x_recv,
    gate_up, act, grad_gate_up, gate_rows,
    back_arrived, b_send, b_recv,
    gate_sent, gate_arrived, gate_own, gate_sums, gate_total, g_send, g_recv, gs_send, gs_recv,
    sums, rs_send, rs_recv, in_tiles, back_tile, tile_sems,
):
    place = lax.axis_index("seq")
    member = lax.axis_index("dp")
    slots = sent.shape[1]
    rows = planes * slots
    length = count * tokens
    wide = MODEL_WIDTH // chunks
    own_expert = place * planes + member
    experts = count * planes
    lanes = router.shape[-1]
    extra = gate_sent.shape[-1]
    low = jnp.bfloat16
    pieces = segments(slots)
    others = [(j, lax.rem(member + j, planes)) for j in range(1, planes)]

    loads = [
        pltpu.make_async_copy(picker_hbm, picker, local_sems.at[0]),
        pltpu.make_async_copy(in_hbm, weight_in, local_sems.at[1]),
        pltpu.make_async_copy(router_hbm, router, local_sems.at[2]),
        pltpu.make_async_copy(back_hbm, weight_back, local_sems.at[3]),
    ] + [
        pltpu.make_async_copy(
            grad_hbm.at[c], grad_rows.at[:, :, pl.ds(c * wide, wide)], local_sems.at[4 + c]
        )
        for c in range(chunks)
    ]
    for load in loads:
        load.start()
    full[place] = mixed_ref[...]
    greet([(place, other) for _, other in others] + [(lax.rem(place + k, count), member) for k in range(1, count)])

    line = (count, place, member, full, ag_send, ag_recv)

    def row_copy(i, j, other):
        low_row, high_row = pieces[i]
        part = pl.ds(low_row, high_row - low_row)
        return remote(
            sent.at[other, part], arrived.at[member, part], x_send.at[i, j], x_recv.at[i, j], (place, other)
        )

    def back_copy(i, j, other):
        low_row, high_row = pieces[i]
        part = pl.ds(low_row, high_row - low_row)
        return remote(
            sent.at[other, part], back_arrived.at[member, part], b_send.at[i, j], b_recv.at[i, j],
            (place, other),
        )

    def lanes_of(block):
        return pl.ds(pl.multiple_of(block * tokens, tokens), tokens)

    line_gather_step(0, *line)
    loads[0].wait()
    done = 0
    for i, (begin, end) in enumerate(pieces):
        needed = count - 1 if i == len(pieces) - 1 else min((end - 1) // capacity, count - 1)
        while done < needed:
            done += 1
            line_gather_step(done, *line)
        height = planes * (end - begin)
        picked = jnp.zeros((height, MODEL_WIDTH), jnp.float32)
        for rank in range(begin // capacity, min((end - 1) // capacity, count - 1) + 1):
            block = ranked_block(rank, place, count)
            choice = picker[:, begin:end, lanes_of(block)].reshape(height, tokens)
            picked += dot_nn(choice, full[block])
        sent[:, begin:end, :] = picked.astype(low).reshape(planes, end - begin, MODEL_WIDTH)
        for j, other in others:
            row_copy(i, j, other).start()
        arrived[member, begin:end, :] = sent[member, begin:end, :]
    for load in loads[1:]:
        load.wait()

    own_lanes = lax.broadcasted_iota(jnp.int32, (tokens, lanes), 1)
    named = jnp.zeros((tokens, lanes), jnp.float32)
    for k in range(TOP):
        named += jnp.where(routes_ref[:, k : k + 1] == own_lanes, 1.0, 0.0)

    def masked_gates(scores, mask):
        shifted = jnp.where(mask > 0, scores, FILLER)
        powers = jnp.where(mask > 0, jnp.exp(shifted - jnp.max(shifted, axis=-1, keepdims=True)), 0.0)
        total = jnp.sum(powers, axis=-1, keepdims=True)
        return powers / jnp.where(total > 0, total, 1.0)

    own_gates = masked_gates(dot_nn(mixed_ref[...], router[...]), named)

    def work(i):
        begin, end = pieces[i]
        height = planes * (end - begin)
        x = arrived[:, begin:end, :].reshape(height, MODEL_WIDTH)
        gate_up[:height, :] = dot_nn(x, weight_in[...])
        mask = masks_ref[:, begin:end, :].reshape(height, lanes).astype(jnp.float32)
        gates = masked_gates(dot_nn(x, router[...]), mask)
        lane_ids = lax.broadcasted_iota(jnp.int32, (height, lanes), 1)
        gate = jnp.sum(jnp.where(lane_ids == own_expert, gates, 0.0), axis=-1, keepdims=True)
        gate_rows[:, begin:end, :] = jnp.broadcast_to(gate, (height, HEAD_SIZE)).reshape(
            planes, end - begin, HEAD_SIZE
        )
        grads = grad_rows[:, begin:end, :].reshape(height, MODEL_WIDTH).astype(jnp.float32)
        grad_act = dot_nt((grads * gate).astype(low), weight_back[...])
        gate_part = gate_up[:height, :FF]
        up_part = gate_up[:height, FF:]
        chance = jax.nn.sigmoid(gate_part)
        silu = gate_part * chance
        act[:, begin:end, :] = (silu * up_part).astype(low).reshape(planes, end - begin, FF)
        slope = chance + silu * (1.0 - chance)
        grad_gate = (grad_act * up_part * slope).astype(low)
        grad_up = (grad_act * silu).astype(low)
        grad_gate_up[:, begin:end, :FF] = grad_gate.reshape(planes, end - begin, FF)
        grad_gate_up[:, begin:end, FF:] = grad_up.reshape(planes, end - begin, FF)
        for j, other in others:
            row_copy(i, j, other).wait_send()
        back = jnp.concatenate([grad_gate, grad_up], axis=1)
        for c in range(chunks):
            columns = slice(c * wide, (c + 1) * wide)
            sent[:, begin:end, columns] = (
                dot_nt(back, weight_in[columns, :]).astype(low).reshape(planes, end - begin, wide)
            )
        back_arrived[member, begin:end, :] = sent[member, begin:end, :]

    def send_back(i):
        for j, other in others:
            back_copy(i, j, other).start()

    last = len(pieces) - 1
    for i in range(last):
        for j, other in others:
            row_copy(i, j, other).wait_recv()
        work(i)
    for j, other in others:
        row_copy(last, j, other).wait_recv()
    send_back(last - 1)
    work(last)
    send_back(last)
    line_gather_end(*line)

    tile = in_tiles.shape[1]

    def in_copy(slot, index):
        return pltpu.make_async_copy(
            in_tiles.at[slot],
            grad_in_hbm.at[pl.ds(pl.multiple_of(index * tile, tile), tile), pl.ds(slot * FF, FF)],
            tile_sems.at[slot],
        )

    def in_gradient(index, carry):
        x = arrived[:, :, pl.ds(pl.multiple_of(index * tile, tile), tile)].reshape(rows, tile)
        for slot in range(2):

            @pl.when(index > 0)
            def _():
                in_copy(slot, index).wait()

            grads = grad_gate_up[:, :, slot * FF : (slot + 1) * FF].reshape(rows, FF)
            in_tiles[slot] = dot_tn(x, grads)
            in_copy(slot, index).start()
        return carry

    def outputs(c, grad_gate):
        columns = pl.ds(pl.multiple_of(c * wide, wide), wide)
        result = dot_nn(act[...].reshape(rows, FF), weight_back[:, columns])
        result = result.astype(low).astype(jnp.float32)
        grads = grad_rows[:, :, columns].reshape(rows, wide).astype(jnp.float32)
        scale = gate_rows[...].reshape(rows, HEAD_SIZE)[:, 0:1]
        grad_rows[:, :, columns] = (grads * scale).astype(low).reshape(planes, slots, wide)
        arrived[:, :, columns] = (result * scale).astype(low).reshape(planes, slots, wide)
        return grad_gate + jnp.sum(result * grads, axis=-1, keepdims=True)

    def gate_copy(j, other):
        return remote(
            gate_sent.at[other], gate_arrived.at[member], g_send.at[j], g_recv.at[j], (place, other)
        )

    def back_tile_copy(index):
        return pltpu.make_async_copy(
            back_tile,
            grad_back_hbm.at[:, pl.ds(pl.multiple_of(index * tile, tile), tile)],
            tile_sems.at[2],
        )

    def back_gradient(index, carry):
        grads = grad_rows[:, :, pl.ds(pl.multiple_of(index * tile, tile), tile)].reshape(rows, tile)
        result = dot_tn(act[...].reshape(rows, FF), grads)

        @pl.when(index > 0)
        def _():
            back_tile_copy(index).wait()

        back_tile[...] = result
        back_tile_copy(index).start()
        return carry

    tiles = MODEL_WIDTH // tile
    lax.fori_loop(0, tiles, in_gradient, 0)
    grad_gate = lax.fori_loop(0, chunks, outputs, jnp.zeros((rows, 1), jnp.float32))
    combined = pltpu.make_async_copy(arrived, combined_hbm, tile_sems.at[3])
    combined.start()
    high = grad_gate.astype(low).astype(jnp.float32)
    rest = grad_gate - high
    wide_lanes = lax.broadcasted_iota(jnp.int32, (rows, extra), 1)
    columns = jnp.where(
        wide_lanes == own_expert, high, jnp.where(wide_lanes == own_expert + experts, rest, 0.0)
    )
    gate_sent[...] = columns.astype(low).reshape(gate_sent.shape)
    for j, other in others:
        gate_copy(j, other).start()
    gate_arrived[member] = gate_sent[member]
    for i in range(last - 2, -1, -1):
        send_back(i)
    lax.fori_loop(0, tiles, back_gradient, 0)

    for j, other in others:
        gate_copy(j, other).wait_recv()
    gate_own[...] = (
        dot_tn(picker[...].reshape(rows, length), gate_arrived[...].reshape(rows, extra))
        .astype(low)
        .reshape(count, tokens, extra)
    )
    gate_line = (count, place, member, gate_own, gate_sums, gs_send, gs_recv)
    sums_line = (count, place, member, full, sums, rs_send, rs_recv)
    come = set()
    for step in range(count):
        rank = count - 1 - step
        first = rank * capacity // 16 * 16
        final = min(-(-(rank + 1) * capacity // 16) * 16, slots)
        for i in range(last, -1, -1):
            begin, end = pieces[i]
            if i not in come and begin < final and end > first:
                come.add(i)
                for j, other in others:
                    back_copy(i, j, other).wait_recv()
        block = ranked_block(rank, place, count)
        height = planes * (final - first)
        choice = picker[:, first:final, lanes_of(block)].reshape(height, tokens)
        full[block] = dot_tn(
            choice, back_arrived[:, first:final, :].reshape(height, MODEL_WIDTH)
        ).astype(low)
        if step < count - 1:
            line_sum_step(step, *gate_line)
            line_sum_step(step, *sums_line)
    for i in range(len(pieces)):
        if i not in come:
            for j, other in others:
                back_copy(i, j, other).wait_recv()
    line_sum_end(*gate_line, gate_total)
    line_sum_end(*sums_line, grad_hidden_ref)

    if experts % 128 == 0:
        grad_gates = gate_total[:, :experts] + gate_total[:, experts:]
    else:
        grad_gates = gate_total[...] + pltpu.roll(gate_total[...], extra - experts, 1)
    middle = jnp.sum(own_gates * grad_gates, axis=-1, keepdims=True)
    grad_logits = (own_gates * (grad_gates - middle)).astype(low)
    grad_mixed = grad_hidden_ref[...] + dot_nt(grad_logits, router[...])
    router_ref[:experts, :] = dot_tn(grad_logits, mixed_ref[...])[:experts]
    hidden = hidden1_ref[...]
    inverse = lax.rsqrt(jnp.mean(hidden * hidden, axis=-1, keepdims=True) + EPSILON)
    unit = hidden * inverse
    router_ref[experts:, :] = jnp.broadcast_to(
        jnp.sum(grad_mixed * unit, axis=0, keepdims=True), (8, MODEL_WIDTH)
    )
    turned = grad_mixed * gains_ref[1:2, :]
    grad_norm = inverse * (turned - unit * jnp.mean(turned * unit, axis=-1, keepdims=True))
    grad_hidden = cotangent_ref[...].astype(jnp.float32) + grad_norm
    grad_hidden_ref[...] = grad_hidden
    branch_ref[...] = grad_hidden.astype(low)

    for j, other in others:
        for i in range(len(pieces)):
            back_copy(i, j, other).wait_send()
        gate_copy(j, other).wait_send()
    in_copy(0, 0).wait()
    in_copy(1, 0).wait()
    back_tile_copy(0).wait()
    combined.wait()


def expert_layer(
    count, planes, capacity, mixed, hidden1, cotangent, gains, routes, masks, picker, grad_rows,
    router, weight_in, weight_back,
):
    tokens = mixed.shape[0]
    chunks, _, slots, wide = grad_rows.shape
    rows = planes * slots
    extra = -(-2 * count * planes // 128) * 128
    lanes = router.shape[-1]
    height = planes * max(end - begin for begin, end in segments(slots))
    tile = 256 if rows < 1280 else 128
    pieces = len(segments(slots))
    low, kind = jnp.bfloat16, jnp.float32
    vmem = pl.BlockSpec(memory_space=pltpu.VMEM)
    anywhere = pl.BlockSpec(memory_space=pl.ANY)
    dma = pltpu.SemaphoreType.DMA
    shape = jax.ShapeDtypeStruct
    blocks = (planes, slots, MODEL_WIDTH)
    return pl.pallas_call(
        functools.partial(expert_kernel, count, planes, tokens, capacity, chunks),
        out_shape=(
            shape((tokens, MODEL_WIDTH), kind),
            shape((tokens, MODEL_WIDTH), low),
            shape((count * planes + 8, MODEL_WIDTH), kind),
            shape(weight_in.shape, kind),
            shape(weight_back.shape, kind),
            shape(blocks, low),
        ),
        in_specs=[vmem] * 6 + [anywhere] * 5,
        out_specs=(vmem,) * 3 + (anywhere,) * 3,
        scratch_shapes=[
            pltpu.VMEM(picker.shape, low),
            pltpu.VMEM(blocks, low),
            pltpu.VMEM(router.shape, low),
            pltpu.VMEM(weight_in.shape, low),
            pltpu.VMEM(weight_back.shape, low),
            dma((4 + chunks,)),
            pltpu.VMEM((count, tokens, MODEL_WIDTH), low),
            dma((2, count)),
            dma((2, count)),
            pltpu.VMEM(blocks, low),
            pltpu.VMEM(blocks, low),
            dma((pieces, planes)),
            dma((pieces, planes)),
            pltpu.VMEM((height, 2 * FF), kind),
            pltpu.VMEM((planes, slots, FF), low),
            pltpu.VMEM((planes, slots, 2 * FF), low),
            pltpu.VMEM((planes, slots, HEAD_SIZE), kind),
            pltpu.VMEM(blocks, low),
            dma((pieces, planes)),
            dma((pieces, planes)),
            pltpu.VMEM((planes, slots, extra), low),
            pltpu.VMEM((planes, slots, extra), low),
            pltpu.VMEM((count, tokens, extra), low),
            pltpu.VMEM((count + 1, tokens, extra), low),
            pltpu.VMEM((tokens, extra), kind),
            dma((planes,)),
            dma((planes,)),
            dma((2, count)),
            dma((2, count)),
            pltpu.VMEM((count + 1, tokens, MODEL_WIDTH), low),
            dma((2, count)),
            dma((2, count)),
            pltpu.VMEM((2, tile, FF), kind),
            pltpu.VMEM((FF, tile), kind),
            dma((4,)),
        ],
        compiler_params=pltpu.CompilerParams(
            collective_id=2, has_side_effects=True, vmem_limit_bytes=VMEM_BYTES
        ),
        name="expert_layer",
    )(
        mixed, hidden1, cotangent, gains, routes, masks, picker, grad_rows, router, weight_in,
        weight_back,
    )


def turn_tables(length):
    half = HEAD_SIZE // 2
    freqs = np.float32(ROPE_BASE) ** (-(np.arange(half, dtype=np.float32) * np.float32(2 / HEAD_SIZE)))
    angles = np.arange(length, dtype=np.float32)[:, None] * freqs[None, :]
    cosine, sine = np.cos(angles), np.sin(angles)
    return (
        jnp.asarray(np.concatenate([cosine, cosine], axis=1), jnp.float32),
        jnp.asarray(np.concatenate([-sine, sine], axis=1), jnp.float32),
    )


def body(
    hidden_in,
    routes,
    norm1_gain,
    query_gain,
    key_gain,
    qkv_weight,
    out_weight,
    norm2_gain,
    router,
    gate_up_weight,
    down_weight,
    cotangent,
):
    tokens = hidden_in.shape[1]
    sequence_number = lax.axis_size("seq")
    planes = lax.axis_size("dp")
    devices = sequence_number * planes
    group = lax.axis_index("seq")
    member = lax.axis_index("dp")
    index = group * planes + member
    heads = QUERY_HEADS // sequence_number
    query_columns = heads * HEAD_SIZE
    head_replicas = sequence_number // KEY_VALUE_HEADS
    capacity = (tokens * TOP * 9 + 8 * devices - 1) // (8 * devices)
    slots = -(-sequence_number * capacity // 16) * 16
    chunks = 4
    sequence_length = sequence_number * tokens
    shard = norm1_gain.shape[0]
    small_shard = query_gain.shape[0]

    turn_cos, turn_sin = turn_tables(sequence_length)
    (
        hidden1, mixed_low, lse, gains, picker, full_router, own_cols, out_rows, normed_full,
        heads_low, queries, pair, projected, grad_rows, masks,
    ) = attention_forward(
        sequence_number,
        planes,
        heads,
        shard,
        capacity,
        slots,
        chunks,
        hidden_in[0],
        routes[0],
        norm1_gain[None],
        norm2_gain[None],
        query_gain[None],
        key_gain[None],
        router,
        qkv_weight,
        out_weight,
        cotangent[0],
        turn_cos,
        turn_sin,
    )
    (
        grad_hidden1, grad_branch, grad_router, grad_weight_in, grad_weight_back, combined_rows,
    ) = expert_layer(
        sequence_number,
        planes,
        capacity,
        mixed_low,
        hidden1,
        cotangent[0],
        gains,
        routes[0],
        masks,
        picker,
        grad_rows,
        full_router,
        gate_up_weight[0],
        down_weight[0],
    )
    (
        grad_input, shard_out, column_sums, mixed_total, router_total, gain_total, _,
    ) = attention_backward(
        sequence_number,
        planes,
        heads,
        shard,
        grad_branch,
        grad_hidden1,
        hidden_in[0],
        gains,
        grad_router,
        out_rows,
        own_cols,
        normed_full,
        heads_low,
        queries,
        pair,
        projected,
        picker,
        combined_rows,
        lse,
        turn_cos,
        turn_sin,
    )
    output = (hidden1 + mixed_total).astype(jnp.bfloat16)
    column_sums = column_sums.astype(jnp.float32)
    shard_query = jnp.transpose(column_sums[:, :, :query_columns], (1, 0, 2)).reshape(
        shard, QUERY_HEADS * HEAD_SIZE
    )
    shard_paired = jnp.sum(
        column_sums[:, :, query_columns:].reshape(
            KEY_VALUE_HEADS, head_replicas, shard, 2, HEAD_SIZE
        ),
        axis=1,
    )
    shard_paired = jnp.transpose(shard_paired, (1, 2, 0, 3)).reshape(
        shard, 2 * KEY_VALUE_HEADS * HEAD_SIZE
    )
    shard_qkv = jnp.concatenate([shard_query, shard_paired], axis=1)
    index = group * planes + member
    router_own = lax.dynamic_slice_in_dim(router_total, member * shard, shard, 1)
    gain_own = lax.dynamic_slice_in_dim(
        gain_total[: MODEL_WIDTH // HEAD_SIZE].reshape(1, MODEL_WIDTH), index * shard, shard, 1
    )
    head_gains = lax.dynamic_slice_in_dim(
        gain_total[MODEL_WIDTH // HEAD_SIZE :][:2], index * small_shard, small_shard, 1
    )
    return (
        output[None],
        grad_input[None],
        gain_own[0],
        head_gains[0],
        head_gains[1],
        shard_qkv,
        shard_out,
        router_own[devices],
        router_own[:devices].T,
        grad_weight_in[None],
        grad_weight_back[None],
    )


def solution(mesh):
    in_specs = (
        P("dp", "seq", None),
        P("dp", "seq", None),
        P(("seq", "dp")),
        P(("seq", "dp")),
        P(("seq", "dp")),
        P(("seq", "dp"), None),
        P(("seq", "dp"), None),
        P(("seq", "dp")),
        P(("seq", "dp"), None),
        P(("seq", "dp"), None, None),
        P(("seq", "dp"), None, None),
        P("dp", "seq", None),
    )
    out_specs = (
        P("dp", "seq", None),
        P("dp", "seq", None),
        P(("seq", "dp")),
        P(("seq", "dp")),
        P(("seq", "dp")),
        P(("seq", "dp"), None),
        P(("seq", "dp"), None),
        P(("seq", "dp")),
        P(("seq", "dp"), None),
        P(("seq", "dp"), None, None),
        P(("seq", "dp"), None, None),
    )
    return jax.shard_map(body, mesh=mesh, in_specs=in_specs, out_specs=out_specs, check_vma=False)
```

time: 524 us -> 473 us (0.903)
  Pallas kernels: 464 us -> 430 us
  other arithmetic: 15.4 us -> 4.46 us
    pallas_call x2 -> x1, Pallas kernels: 180 us -> 151 us  [expert_layer(): pl.pallas_call(functools.partial(expert_kernel, count, planes, tokens, ca...]
    reduce_sum x6 -> x0, other arithmetic: 6.32 us -> none  [the longest x2 2.61 us: rms_norm(): jnp.mean(values * values, axis=-1, keepdims=True) + EPSILON]
    pallas_call x1, Pallas kernels: 148 us -> 142 us  [attention_backward(): pl.pallas_call(functools.partial(backward_kernel, count, planes, tokens,...]
    unnamed x26 -> x17, local copies, waits for them, and re-layouts: 17.7 us -> 20.2 us
where the time goes in v5:
time: 473 us; the launch traced here: 464 us
  Pallas kernels  430 us (91%)
  local copies, waits for them, and re-layouts  28.3 us (6%)
    pallas_call x1, Pallas kernels, expert_layer(): pl.pallas_call(functools.partial(expert_kernel, count, planes, tokens, ca...  151 us
    pallas_call x1, Pallas kernels, attention_backward(): pl.pallas_call(functools.partial(backward_kernel, count, planes, tokens,...  142 us
    pallas_call x1, Pallas kernels, attention_forward(): pl.pallas_call(functools.partial(forward_kernel, count, planes, tokens, h...  136 us
    unnamed x17, local copies, waits for them, and re-layouts  20.2 us

profile of v5, /device:TPU:0, one launch (start us, length us, event | category | flops | bytes accessed | tf_op | source)
XLA Modules:
  0.0 463.6 jit_solution(2267062167759188041)
XLA Ops:
  0.6 1.4 copy.28
  2.1 1.4 copy.29.router_ref
  3.4 136.4 %attention_forward.1 = (f32[128,2048]{1,0:T(8,128)}, bf16[128,2048]{1,0:T(8,128)(2,1)}, f32[8,1,512]{2,1,0:T(1,128)}, f32[8,2048]{1,0:T(8,128)}, bf16[8,144,512]...) custom-call(bf16[128,2048]{1,0:T(8,128)(2,1)} %bitcast.39, ...), custom_call_target="tpu_custom_call" | custom-call | tf_op jit(solution)/shard_map/attention_forward/pallas_call | solution.py:1094
  139.9 151.3 %expert_layer.1 = (f32[128,2048]{1,0:T(8,128)}, bf16[128,2048]{1,0:T(8,128)(2,1)}, f32[40,2048]{1,0:T(8,128)}, f32[2048,1536]{1,0:T(8,128)}, f32[768,2048]{1,0:T(8,128)}, /*index=5*/bf16[8,144,2048]{2,1,0:T(8,128)(2,1)}) custom-call(bf16[128,2048]{1,0:T(8,128)(2,1)} %get-tuple-element.39.mixed_ref, f32[128,2048]{1,0:T(8,128)} %get-tuple-element.38.hidden1_ref, ...), custom_call_target="tpu_custom_call" | custom-call | tf_op jit(solution)/shard_map/expert_layer/pallas_call | solution.py:1497
  291.2 141.9 %attention_backward.1 = (f32[128,2048]{1,0:T(8,128)}, f32[128,2048]{1,0:T(8,128)}, bf16[4,64,1280]{2,1,0:T(8,128)(2,1)}, f32[128,2048]{1,0:T(8,128)}, f32[40,512...) custom-call(bf16[128,2048]{1,0:T(8,128)(2,1)} %get-tuple-element.45.branch_ref, ...), custom_call_target="tpu_custom_call" | custom-call | tf_op jit(solution)/shard_map/attention_backward/pallas_call | solution.py:629
  433.1 1.2 convert_element_type.7
  434.3 0.0 copy-start.2
  434.4 0.0 copy-start
  434.4 0.1 slice_bitcast_fusion
  434.5 0.1 copy.32
  434.6 1.0 slice.35
  435.6 0.8 reduce_sum.2
  436.4 0.0 copy-start.1
  436.4 1.9 copy.31
  438.3 1.1 reshape.36
  439.4 1.1 pad_maximum_fusion
  440.6 0.0 copy-done.2
  440.6 1.3 fusion.1
  441.8 0.0 copy-done
  441.8 2.1 fusion
  444.0 1.4 dynamic-slice_bitcast_fusion
  445.3 0.1 constant_dynamic-slice_fusion
  445.4 0.5 slice_bitcast_fusion.1
  445.9 2.3 copy.37
  448.2 0.0 copy-done.1
  448.2 0.0 slice-start
  448.2 1.0 copy.38
  449.2 0.0 slice-start.1
  449.2 11.3 %copy.39 = f32[1,2048,1536]{2,1,0:T(8,128)} copy(f32[1,2048,1536]{2,1,0:T(8,128)} %bitcast.30) | data formatting | bytes 25165824
  460.5 0.0 slice-done
  460.5 0.0 slice-done.1
  460.5 2.7 copy.40
  (3 shorter events, 0.0 us)
Async XLA Ops:
  434.3 6.2 %copy-start.2 = (f32[24,128]{1,0:T(8,128)S(1)}, f32[24,128]{1,0:T(8,128)}, u32[]{:S(2)}) copy-start(f32[24,128]{1,0:T(8,128)} %get-tuple-element.59) | copy-start | bytes 36868
  434.4 7.5 %copy-start = (f32[128,2048]{1,0:T(8,128)S(1)}, f32[128,2048]{1,0:T(8,128)}, u32[]{:S(2)}) copy-start(f32[128,2048]{1,0:T(8,128)} %get-tuple-element.38.hidden1_ref) | copy-start | bytes 3145732
  436.4 11.8 %copy-start.1 = (f32[128,2048]{1,0:T(8,128)S(1)}, f32[128,2048]{1,0:T(8,128)}, u32[]{:S(2)}) copy-start(f32[128,2048]{1,0:T(8,128)} %get-tuple-element.86) | copy-start | bytes 3145732
  448.2 12.2 %slice-start = ((s8[6291456]{0:T(1024)(128)(4,1)}), s8[4194304]{0:T(1024)(128)(4,1)S(1)}, s32[]{:S(2)}) async-start(s8[6291456]{0:T(1024)(128)(4,1)} %bitcast.32), calls=%async_computation | async-start | bytes 8388608
  449.2 11.3 %slice-start.1 = ((s8[6291456]{0:T(1024)(128)(4,1)}), s8[2097152]{0:T(1024)(128)(4,1)S(1)}, s32[]{:S(2)}) async-start(s8[6291456]{0:T(1024)(128)(4,1)} %bitcast.32), calls=%async_computation.1 | async-start | bytes 4194304
